TPU v7x, 32 devices: a whole 2x2x4 slice. The times are simulated.
32 devices in a mesh: region: 2 (over core), island: 4 (over y, x), dev: 4 (over z).
Axes of the slice: x: 2, y: 2, z: 4, core: 2. Of those that a mesh axis runs over, the one named last changes fastest.
Arguments:
- activations: bfloat16 [8192, 2560], P(('region', 'island', 'dev')), may hold values from -6 to 6
- cotangent: bfloat16 [8192, 512], P(('region', 'island', 'dev')), may hold values from -6 to 6
- island_weight: float32 [2, 4, 2560, 512], P('region', 'island', 'dev'), may hold values from -6 to 6
- adam_first: float32 [2, 4, 2560, 512], P('region', 'island', 'dev'), may hold values from -6 to 6
- adam_second: float32 [2, 4, 2560, 512], P('region', 'island', 'dev'), may hold values from 0.01 to 1
- region_anchor: float32 [2, 2560, 512], P('region', 'dev'), may hold values from -6 to 6
- region_momentum: float32 [2, 2560, 512], P('region', 'dev'), may hold values from -6 to 6
- global_anchor: float32 [2560, 512], P('dev'), may hold values from -6 to 6
- global_momentum: float32 [2560, 512], P('dev'), may hold values from -6 to 6
Outputs:
- first_new: float32 [2, 4, 2560, 512], P('region', 'island', 'dev')
- second_new: float32 [2, 4, 2560, 512], P('region', 'island', 'dev')
- region_velocity: float32 [2, 2560, 512], P('region', 'dev')
- global_velocity: float32 [2560, 512], P('dev')
- global_new: float32 [2560, 512], P('dev')
- next_keys: bfloat16 [8192, 512], P(('region', 'island', 'dev'))
All inputs are finite; a program needn't handle non-finite values.
Results may differ from a plain program's by a relative error of at most 0.0049.
Values may be sent and summed in bfloat16 or wider, within the bound.
No kernel may reach another device: no remote copies, remote signals or barrier semaphores. Data moves between devices by JAX's collectives and lax.ppermute only.
A program may use at most 64 MiB of HBM per device.

v0:
```python
import math

import jax
import jax.numpy as jnp
from jax import lax
from jax.sharding import PartitionSpec as P

DW = 2560


beta_first = 0.9
beta_second = 0.999
adam_eps = 1e-08
inner_rate = 0.05
weight_decay = 0.1
region_mu = 0.9
region_rate = 0.7
global_mu = 0.9
global_rate = 0.7


def body(
    activations,
    cotangent,
    island_weight,
    adam_first,
    adam_second,
    region_anchor,
    region_momentum,
    global_anchor,
    global_momentum,
):
    island_tokens = activations.shape[0] * lax.axis_size("dev")
    islands = lax.axis_size("island")
    regions = lax.axis_size("region")
    summed = lax.psum_scatter(
        lax.dot_general(
            activations, cotangent, (((0,), (0,)), ((), ())), preferred_element_type=jnp.float32
        ).astype(jnp.bfloat16),
        "dev",
        scatter_dimension=0,
        tiled=True,
    ).astype(jnp.float32)
    gradient = summed * (1.0 / math.sqrt(island_tokens))
    first_new = beta_first * adam_first + (1.0 - beta_first) * gradient
    second_new = beta_second * adam_second + (1.0 - beta_second) * gradient * gradient
    inner = island_weight - inner_rate * (
        first_new / (jnp.sqrt(second_new) + adam_eps) + weight_decay * island_weight
    )
    island_delta = region_anchor[:, None] - inner
    island_total = lax.psum(island_delta, "island")
    region_mean = island_total[:, 0] / islands
    region_velocity = region_mu * region_momentum + region_mean
    region_params = region_anchor - region_rate * (region_mean + region_mu * region_velocity)
    region_gap = global_anchor[None] - region_params
    gap_total = lax.psum(region_gap, "region")
    global_mean = gap_total[0] / regions
    global_velocity = global_mu * global_momentum + global_mean
    global_new = global_anchor - global_rate * (global_mean + global_mu * global_velocity)
    weight_low = global_new.astype(jnp.bfloat16)
    weight_full = lax.all_gather(weight_low, "dev", axis=0, tiled=True)
    projected = jnp.dot(activations, weight_full, preferred_element_type=jnp.float32)
    next_keys = (projected * (1.0 / math.sqrt(DW))).astype(jnp.bfloat16)
    return (first_new, second_new, region_velocity, global_velocity, global_new, next_keys)


def solution(mesh):
    return jax.shard_map(
        body,
        mesh=mesh,
        in_specs=(
            P(("region", "island", "dev"), None),
            P(("region", "island", "dev"), None),
            P("region", "island", "dev", None),
            P("region", "island", "dev", None),
            P("region", "island", "dev", None),
            P("region", "dev", None),
            P("region", "dev", None),
            P("dev", None),
            P("dev", None),
        ),
        out_specs=(
            P("region", "island", "dev", None),
            P("region", "island", "dev", None),
            P("region", "dev", None),
            P("dev", None),
            P("dev", None),
            P(("region", "island", "dev"), None),
        ),
        check_vma=False,
    )
```

profile of v0, /device:TPU:0, one launch (start us, length us, event | category | flops | bytes accessed | tf_op | source)
XLA Modules:
  0.0 222.6 jit_solution(18198151817819253158)
XLA Ops:
  7.2 0.0 copy-start
  7.2 0.0 reduce-scatter.2.cloned.1.call-start
  7.2 1.3 copy-done
  8.5 3.3 %convolution_convert_fusion = bf16[2560,512]{1,0:T(8,128)(2,1)} fusion(bf16[256,2560]{1,0:T(8,128)(2,1)S(1)} %copy-done, bf16[256,512]{1,0:T(8,128)(2,1)} %param.10), kind=kOutput, calls=%fused_computation | convolution fusion | flops 672399360 | bytes 4194304 | tf_op jit(solution)/shard_map/dot_general | solution.py:37
  11.8 0.0 copy-start.1
  11.8 0.0 reduce-scatter.2.cloned.1.call-update
  11.9 0.0 all-reduce.3.cloned.1.call-start
  11.9 54.9 %reduce-scatter.2.cloned.1.call-done = bf16[640,512]{1,0:T(8,128)(2,1)} async-done(((bf16[2560,512]{1,0:T(8,128)(2,1)}), bf16[640,512]{1,0:T(8,128)(2,1)}) %reduce-scatter.2.cloned.1.call-update) | async-done | bytes 655376 | tf_op jit(solution)/shard_map/reduce_scatter | solution.py:36
  66.8 0.0 copy-done.1
  66.8 4.9 %bitcast_subtract_fusion.1 = (f32[1,1,640,512]{3,2,1,0:T(8,128)}, f32[1,1,640,512]{3,2,1,0:T(8,128)}, f32[1,1,640,512]{3,2,1,0:T(8,128)}) fusion(f32[1,640,512]{2,1,0:T(8,128)S(1)} %copy-done.1, f32[1,1,640,512]{3,2,1,0:T(8,128)} %param.11, bf16[640,512]{1,0:T(8,128)(2,1)} %reduce-scatter.2.cloned.1.call-done, f32[1,1,640,512]{3,2,1,0:T(8,128)} %param.13, ...), kind=kLoop, calls=%fused_computation.18 | loop fusion | flops 5242880 | bytes 9830400 | tf_op jit(solution)/shard_map/sub | solution.py:50
  71.7 0.0 all-reduce.3.cloned.1.call-update
  71.7 0.0 all-reduce.5.cloned.1.call-start
  71.8 56.3 %all-reduce.3.cloned.1.call-done = f32[1,1,640,512]{3,2,1,0:T(8,128)} async-done(((f32[1,1,640,512]{3,2,1,0:T(8,128)}), f32[1,1,640,512]{3,2,1,0:T(8,128)}) %all-reduce.3.cloned.1.call-update) | async-done | bytes 1310736 | tf_op jit(solution)/shard_map/psum | solution.py:51
  128.1 4.2 %bitcast_subtract_fusion = (f32[1,640,512]{2,1,0:T(8,128)}, f32[1,640,512]{2,1,0:T(8,128)}) fusion(f32[640,512]{1,0:T(8,128)} %param.16, f32[1,640,512]{2,1,0:T(8,128)S(1)} %copy-done.1, f32[1,1,640,512]{3,2,1,0:T(8,128)} %all-reduce.3.cloned.1.call-done, f32[1,640,512]{2,1,0:T(8,128)} %param.15), kind=kLoop, calls=%fused_computation.13 | loop fusion | flops 2621440 | bytes 7864320 | tf_op jit(solution)/shard_map/sub | solution.py:55
  132.3 0.0 copy-start.2
  132.3 0.0 all-reduce.5.cloned.1.call-update
  132.3 0.0 all-gather.2.cloned.1.call-start
  132.4 20.1 %all-reduce.5.cloned.1.call-done = f32[1,640,512]{2,1,0:T(8,128)} async-done(((f32[1,640,512]{2,1,0:T(8,128)}), f32[1,640,512]{2,1,0:T(8,128)}) %all-reduce.5.cloned.1.call-update) | async-done | bytes 1310736 | tf_op jit(solution)/shard_map/psum | solution.py:56
  152.4 0.0 copy-done.2
  152.4 4.0 %fusion.11 = (bf16[640,512]{1,0:T(8,128)(2,1)}, f32[640,512]{1,0:T(8,128)}, f32[640,512]{1,0:T(8,128)}) fusion(f32[640,512]{1,0:T(8,128)S(1)} %copy-done.2, f32[1,640,512]{2,1,0:T(8,128)} %all-reduce.5.cloned.1.call-done, f32[640,512]{1,0:T(8,128)} %param.17), kind=kLoop, calls=%fused_computation.22 | loop fusion | flops 2621440 | bytes 7208960 | tf_op jit(solution)/shard_map/convert_element_type | solution.py:60
  156.4 0.0 all-gather.2.cloned.1.call-update
  156.4 56.1 %all-gather.2.cloned.1.call-done = bf16[2560,512]{1,0:T(8,128)(2,1)} async-done(((bf16[640,512]{1,0:T(8,128)(2,1)}), bf16[2560,512]{1,0:T(8,128)(2,1)}) %all-gather.2.cloned.1.call-update) | async-done | bytes 2621456 | tf_op jit(solution)/shard_map/all_gather | solution.py:61
  212.6 2.6 %fusion.10 = bf16[256,512]{0,1:T(8,128)(2,1)S(1)} fusion(bf16[2560,512]{1,0:T(8,128)(2,1)} %all-gather.2.cloned.1.call-done, bf16[256,2560]{1,0:T(8,128)(2,1)S(1)} %copy-done), kind=kOutput, calls=%fused_computation.21 | convolution fusion | flops 671350784 | bytes 4194304 | tf_op jit(solution)/shard_map/dot_general | solution.py:62
  215.2 0.8 copy.15
Async XLA Ops:
  7.2 1.3 copy-start
  7.2 59.6 %reduce-scatter.2.cloned.1.call-start = ((), (), s32[]{:S(2)}) async-start(), calls=%async_computation.1 | async-start | bytes 3276800 | tf_op jit(solution)/shard_map/reduce_scatter | solution.py:36
  11.8 55.0 %copy-start.1 = (f32[1,640,512]{2,1,0:T(8,128)S(1)}, f32[1,640,512]{2,1,0:T(8,128)}, u32[]{:S(2)}) copy-start(f32[1,640,512]{2,1,0:T(8,128)} %param.14) | copy-start | bytes 3932164
  11.9 116.2 %all-reduce.3.cloned.1.call-start = ((), (), s32[]{:S(2)}) async-start(), calls=%async_computation.2 | async-start | bytes 2621440 | tf_op jit(solution)/shard_map/psum | solution.py:51
  71.7 80.7 %all-reduce.5.cloned.1.call-start = ((), (), s32[]{:S(2)}) async-start(), calls=%async_computation.3 | async-start | bytes 2621440 | tf_op jit(solution)/shard_map/psum | solution.py:56
  132.3 20.2 %copy-start.2 = (f32[640,512]{1,0:T(8,128)S(1)}, f32[640,512]{1,0:T(8,128)}, u32[]{:S(2)}) copy-start(f32[640,512]{1,0:T(8,128)} %param.16) | copy-start | bytes 3932164
  132.3 80.3 %all-gather.2.cloned.1.call-start = ((), (), s32[]{:S(2)}) async-start(), calls=%async_computation.4 | async-start | bytes 3276800 | tf_op jit(solution)/shard_map/all_gather | solution.py:61
Sparse Core Ops, SparseCore 0:
  12.0 54.8 reduce-scatter.1
  71.8 56.1 all-reduce.2
  132.4 19.9 all-reduce.4
  156.6 55.9 all-gather.1
where the time goes:
time: 223 us
  waiting for transfers between devices  188 us (84%)
  between operations  13.8 us (6%)
  other arithmetic  13.1 us (6%)
  matrix products  5.96 us (3%)
    psum x1, waiting for transfers between devices, body(): island_total = lax.psum(island_delta, 'island')  56.3 us
    all_gather x1, waiting for transfers between devices, body(): weight_full = lax.all_gather(weight_low, 'dev', axis=0, tiled=True)  56.1 us
    reduce_scatter x1, waiting for transfers between devices, body(): lax.psum_scatter(lax.dot_general(activations, cotangent, (((0,), (0,)), (...  54.9 us
    psum x1, waiting for transfers between devices, body(): gap_total = lax.psum(region_gap, 'region')  20.1 us
    sub x1, other arithmetic, body(): island_delta = region_anchor[:, None] - inner  4.86 us
  transfers between devices with their start and end apart: 4, of which 4 were waited for; matrix products, arithmetic and copies ran while one was open for 0% of the time, Pallas kernels for 0%

commit v1 on v0

--- a/solution.py
+++ b/solution.py
@@ -6,6 +6,7 @@
 from jax.sharding import PartitionSpec as P
 
 DW = 2560
+LANES = 128
 
 
 beta_first = 0.9
@@ -19,7 +20,28 @@
 global_rate = 0.7
 
 
-def body(
+def adam(gradient, island_weight, adam_first, adam_second):
+    first_new = beta_first * adam_first + (1.0 - beta_first) * gradient
+    second_new = beta_second * adam_second + (1.0 - beta_second) * gradient * gradient
+    inner = island_weight - inner_rate * (
+        first_new / (jnp.sqrt(second_new) + adam_eps) + weight_decay * island_weight
+    )
+    return first_new, second_new, inner
+
+
+def regional(region_mean, region_anchor, region_momentum):
+    region_velocity = region_mu * region_momentum + region_mean
+    region_params = region_anchor - region_rate * (region_mean + region_mu * region_velocity)
+    return region_velocity, region_params
+
+
+def outer(global_mean, global_anchor, global_momentum):
+    global_velocity = global_mu * global_momentum + global_mean
+    global_new = global_anchor - global_rate * (global_mean + global_mu * global_velocity)
+    return global_velocity, global_new
+
+
+def generic_body(
     activations,
     cotangent,
     island_weight,
@@ -42,31 +64,146 @@
         tiled=True,
     ).astype(jnp.float32)
     gradient = summed * (1.0 / math.sqrt(island_tokens))
-    first_new = beta_first * adam_first + (1.0 - beta_first) * gradient
-    second_new = beta_second * adam_second + (1.0 - beta_second) * gradient * gradient
-    inner = island_weight - inner_rate * (
-        first_new / (jnp.sqrt(second_new) + adam_eps) + weight_decay * island_weight
-    )
+    first_new, second_new, inner = adam(gradient, island_weight, adam_first, adam_second)
     island_delta = region_anchor[:, None] - inner
-    island_total = lax.psum(island_delta, "island")
-    region_mean = island_total[:, 0] / islands
-    region_velocity = region_mu * region_momentum + region_mean
-    region_params = region_anchor - region_rate * (region_mean + region_mu * region_velocity)
+    region_mean = lax.psum(island_delta, "island")[:, 0] / islands
+    region_velocity, region_params = regional(region_mean, region_anchor, region_momentum)
     region_gap = global_anchor[None] - region_params
-    gap_total = lax.psum(region_gap, "region")
-    global_mean = gap_total[0] / regions
-    global_velocity = global_mu * global_momentum + global_mean
-    global_new = global_anchor - global_rate * (global_mean + global_mu * global_velocity)
-    weight_low = global_new.astype(jnp.bfloat16)
-    weight_full = lax.all_gather(weight_low, "dev", axis=0, tiled=True)
+    global_mean = lax.psum(region_gap, "region")[0] / regions
+    global_velocity, global_new = outer(global_mean, global_anchor, global_momentum)
+    weight_full = lax.all_gather(global_new.astype(jnp.bfloat16), "dev", axis=0, tiled=True)
     projected = jnp.dot(activations, weight_full, preferred_element_type=jnp.float32)
-    next_keys = (projected * (1.0 / math.sqrt(DW))).astype(jnp.bfloat16)
+    next_keys = (projected * (1.0 / math.sqrt(activations.shape[1]))).astype(jnp.bfloat16)
     return (first_new, second_new, region_velocity, global_velocity, global_new, next_keys)
 
 
+def flip(array, axis, bits):
+    return lax.ppermute(array, axis, [(i, i ^ bits) for i in range(lax.axis_size(axis))])
+
+
+def chunks_of(rows):
+    units = rows // LANES
+    sizes = [1]
+    while sum(sizes) < units:
+        left = units - sum(sizes)
+        sizes.append(2 if left >= 4 else 1)
+    edges = [0]
+    for size in sizes:
+        edges.append(edges[-1] + size * LANES)
+    return list(zip(edges[:-1], edges[1:]))
+
+
+def paired_body(
+    activations,
+    cotangent,
+    island_weight,
+    adam_first,
+    adam_second,
+    region_anchor,
+    region_momentum,
+    global_anchor,
+    global_momentum,
+):
+    devs = lax.axis_size("dev")
+    islands = lax.axis_size("island")
+    regions = lax.axis_size("region")
+    tokens, features = activations.shape
+    rows = features // devs
+    scale = 1.0 / math.sqrt(tokens * devs)
+    me = lax.axis_index("dev")
+    low, high = me & 1, me >> 1
+    core = lax.axis_index("region")
+    weight, first, second = island_weight[0, 0], adam_first[0, 0], adam_second[0, 0]
+    anchor, momentum = region_anchor[0], region_momentum[0]
+    pieces = chunks_of(rows)
+
+    def columns(low_bit, high_bit, start, stop):
+        at = [activations[:, s * rows + start : s * rows + stop] for s in range(devs)]
+        return jnp.where(
+            high_bit == 0,
+            jnp.where(low_bit == 0, at[0], at[1]),
+            jnp.where(low_bit == 0, at[2], at[3]),
+        )
+
+    def product(left, right):
+        return lax.dot_general(
+            left, right, (((0,), (0,)), ((), ())), preferred_element_type=jnp.float32
+        )
+
+    other_cotangent = flip(cotangent, "dev", 1)
+    arrived = []
+    for start, stop in pieces:
+        message = jnp.concatenate(
+            [columns(1 - low, high, start, stop), columns(1 - low, 1 - high, start, stop)], axis=1
+        )
+        arrived.append(flip(message, "dev", 1))
+
+    gradients, means, global_means, blocks = [], [], [], []
+    for k, (start, stop) in enumerate(pieces):
+        size = stop - start
+        raw = arrived[k]
+        away = product(columns(low, 1 - high, start, stop), cotangent) + product(
+            raw[:, size:], other_cotangent
+        )
+        kept = product(columns(low, high, start, stop), cotangent) + product(
+            raw[:, :size], other_cotangent
+        )
+        summed = kept + flip(away.astype(jnp.bfloat16), "dev", 2).astype(jnp.float32)
+        gradient = summed * scale
+        gradients.append(gradient)
+        _, _, inner = adam(gradient, weight[start:stop], first[start:stop], second[start:stop])
+        total = (anchor[start:stop] - inner).astype(jnp.bfloat16)
+        order = [1, 2] if k % 2 == 0 else [2, 1]
+        for i, bits in enumerate(order):
+            total = total.astype(jnp.float32) + flip(total, "island", bits).astype(jnp.float32)
+            if i < len(order) - 1:
+                total = total.astype(jnp.bfloat16)
+        region_mean = total / islands
+        means.append(region_mean)
+        _, region_params = regional(region_mean, anchor[start:stop], momentum[start:stop])
+        gap = global_anchor[start:stop] - region_params
+        global_mean = (gap + flip(gap, "region", 1)) / regions
+        global_means.append(global_mean)
+        _, fresh = outer(global_mean, global_anchor[start:stop], global_momentum[start:stop])
+        low_weight = fresh.astype(jnp.bfloat16)
+        half = size // 2
+        mine = jnp.where(core == 0, low_weight[:half], low_weight[half:])
+        held = jnp.stack([mine] + [flip(mine, "dev", bits) for bits in range(1, devs)])
+        swapped = flip(held, "region", 1)
+        blocks.append((held, swapped))
+
+    projected = jnp.zeros((tokens, cotangent.shape[1]), jnp.float32)
+    for (start, stop), (held, swapped) in zip(pieces, blocks):
+        half = (stop - start) // 2
+        for bits in range(devs):
+            left = columns(low ^ (bits & 1), high ^ (bits >> 1), start, stop)
+            upper = jnp.where(core == 0, held[bits], swapped[bits])
+            lower = jnp.where(core == 0, swapped[bits], held[bits])
+            projected += jnp.dot(left[:, :half], upper, preferred_element_type=jnp.float32)
+            projected += jnp.dot(left[:, half:], lower, preferred_element_type=jnp.float32)
+    next_keys = (projected * (1.0 / math.sqrt(features))).astype(jnp.bfloat16)
+
+    first_new, second_new, _ = adam(jnp.concatenate(gradients), weight, first, second)
+    region_velocity, _ = regional(jnp.concatenate(means), anchor, momentum)
+    global_velocity, global_new = outer(
+        jnp.concatenate(global_means), global_anchor, global_momentum
+    )
+    return (
+        first_new[None, None],
+        second_new[None, None],
+        region_velocity[None],
+        global_velocity,
+        global_new,
+        next_keys,
+    )
+
+
 def solution(mesh):
+    devs, islands, regions = mesh.shape["dev"], mesh.shape["island"], mesh.shape["region"]
+    aligned = DW % (devs * LANES) == 0
+    paired = devs == 4 and islands == 4 and regions == 2 and aligned
     return jax.shard_map(
-        body,
+        paired_body if paired else generic_body,
         mesh=mesh,
         in_specs=(
             P(("region", "island", "dev"), None),

time: 223 us -> 121 us (0.54)
  waiting for transfers between devices: 188 us -> 42 us
  starting transfers between devices: 0.16 us -> 40 us
  matrix products: 5.96 us -> 23.5 us
  between operations: 13.8 us -> 1.45 us
    psum x2 -> x0, waiting for transfers between devices: 76.4 us -> none  [the longest x1 56.3 us: body(): island_total = lax.psum(island_delta, 'island')]
    all_gather x1 -> x0, waiting for transfers between devices: 56.1 us -> none  [body(): weight_full = lax.all_gather(weight_low, 'dev', axis=0, tiled=True)]
    reduce_scatter x1 -> x0, waiting for transfers between devices: 54.9 us -> none  [body(): lax.psum_scatter(lax.dot_general(activations, cotangent, (((0,), (0,)), (...]
    ppermute x0 -> x37, waiting for transfers between devices: none -> 42 us  [flip(): lax.ppermute(array, axis, [(i, i ^ bits) for i in range(lax.axis_size(axi...]
    ppermute x0 -> x37, starting transfers between devices: none -> 40 us  [flip(): lax.ppermute(array, axis, [(i, i ^ bits) for i in range(lax.axis_size(axi...]
    dot_general x2 -> x48, matrix products: 5.96 us -> 23.5 us  [the longest x16 14.8 us: product(): lax.dot_general(left, right, (((0,), (0,)), ((), ())), preferred_element_...]
    sub x2 -> x3, other arithmetic: 9.09 us -> 2.62 us  [the longest x1 2.01 us: outer(): global_anchor - global_rate * (global_mean + global_mu * global_velocity)]
    select_n x0 -> x15, other arithmetic: none -> 3.68 us  [the longest x11 3.63 us: columns(): jnp.where(high_bit == 0, jnp.where(low_bit == 0, at[0], at[1]), jnp.where...]
  transfers between devices with their start and end apart: 4 -> 37, of which waited for: 4 -> 15; matrix products, arithmetic and copies ran while one was open for 0% -> 26% of each run, Pallas kernels for 0% -> 0%
where the time goes in v1:
time: 121 us
  waiting for transfers between devices  42 us (35%)
  starting transfers between devices  40 us (33%)
  matrix products  23.5 us (19%)
  other arithmetic  13.4 us (11%)
  between operations  1.45 us (1%)
    ppermute x37, waiting for transfers between devices, flip(): lax.ppermute(array, axis, [(i, i ^ bits) for i in range(lax.axis_size(axi...  42 us
    ppermute x37, starting transfers between devices, flip(): lax.ppermute(array, axis, [(i, i ^ bits) for i in range(lax.axis_size(axi...  40 us
    dot_general x16, matrix products, product(): lax.dot_general(left, right, (((0,), (0,)), ((), ())), preferred_element_...  14.8 us
    dot_general x16, matrix products, paired_body(): jnp.dot(left[:, :half], upper, preferred_element_type=jnp.float32)  4.67 us
    dot_general x16, matrix products, paired_body(): jnp.dot(left[:, half:], lower, preferred_element_type=jnp.float32)  4 us
    select_n x11, other arithmetic, columns(): jnp.where(high_bit == 0, jnp.where(low_bit == 0, at[0], at[1]), jnp.where...  3.63 us
    concatenate x4, other arithmetic, paired_body(): jnp.concatenate([columns(1 - low, high, start, stop), columns(1 - low, 1...  2.72 us
  transfers between devices with their start and end apart: 37, of which 15 were waited for; matrix products, arithmetic and copies ran while one was open for 26% of the time, Pallas kernels for 0%

profile of v1, /device:TPU:0, one launch (start us, length us, event | category | flops | bytes accessed | tf_op | source)
XLA Modules:
  0.0 120.9 jit_solution(11650419486133179871)
XLA Ops:
  0.7 1.3 %broadcast_select_fusion.26 = (bf16[256,128]{1,0:T(8,128)(2,1)S(1)}, bf16[256,128]{1,0:T(8,128)(2,1)S(1)}, bf16[256,128]{1,0:T(8,128)(2,1)S(1)}, bf16[256,128]{1,0:T(8,128)(2,1)S(1)}) fusion(pred[]{:T(512)S(6)} %eq.17, bf16[256,2560]{1,0:T(8,128)(2,1)} %param.9, pred[]{:T(512)S(6)} %eq.16, pred[]{:T(512)S(6)} %eq.14), kind=kLoop, calls=%fused_computation.350 | loop fusion | flops 327680 | bytes 1048579 | tf_op jit(solution)/shard_map/jit(_where)/select_n | solution.py:122
  2.7 3.0 %collective-permute-start.7 = (bf16[256,256]{1,0:T(8,128)(2,1)}, bf16[256,256]{1,0:T(8,128)(2,1)}, u32[]{:S(2)}, u32[]{:S(2)}) collective-permute-start(bf16[256,256]{1,0:T(8,128)(2,1)} %pad_maximum_fusion.9), channel_id=1, source_target_pairs={{0,1},{1,0},{2,3},{3,2},{4,5},{5,4},{6,7},{7,6},{8,9},{9,8},{10,11... | collective-permute-start | bytes 393224 | tf_op jit(solution)/shard_map/ppermute | solution.py:81
  6.5 2.0 %collective-permute-start.1 = (bf16[256,512]{1,0:T(8,128)(2,1)S(1)}, bf16[256,512]{1,0:T(8,128)(2,1)S(1)}, u32[]{:S(2)}, u32[]{:S(2)}) collective-permute-start(bf16[256,512]{1,0:T(8,128)(2,1)S(1)} %copy-done), channel_id=1, source_target_pairs={{0,1},{1,0},{2,3},{3,2},{4,5},{5,4},{6,7},{7,6},{8,9},{9,8},{10,11... | collective-permute-start | bytes 786440 | tf_op jit(solution)/shard_map/ppermute | solution.py:81
  9.9 2.0 %collective-permute-start = (bf16[256,256]{1,0:T(8,128)(2,1)}, bf16[256,256]{1,0:T(8,128)(2,1)}, u32[]{:S(2)}, u32[]{:S(2)}) collective-permute-start(bf16[256,256]{1,0:T(8,128)(2,1)} %pad_maximum_fusion.7), channel_id=1, source_target_pairs={{0,1},{1,0},{2,3},{3,2},{4,5},{5,4},{6,7},{7,6},{8,9},{9,8},{10,11... | collective-permute-start | bytes 393224 | tf_op jit(solution)/shard_map/ppermute | solution.py:81
  12.5 0.9 fusion.211
  14.6 0.8 broadcast_select_fusion.9
  15.7 0.9 fusion.251
  16.6 0.9 fusion.248
  17.5 1.0 fusion.249
  18.9 2.6 %collective-permute-done.1 = bf16[256,512]{1,0:T(8,128)(2,1)S(1)} collective-permute-done((bf16[256,512]{1,0:T(8,128)(2,1)S(1)}, bf16[256,512]{1,0:T(8,128)(2,1)S(1)}, u32[]{:S(2)}, u32[]{:S(2)}) %collective-permute-start.1) | collective-permute-done | bytes 262176 | tf_op jit(solution)/shard_map/ppermute | solution.py:81
  21.5 1.3 %fusion.40 = bf16[128,512]{1,0:T(8,128)(2,1)S(1)} fusion(f32[128,512]{1,0:T(8,128)} %fusion.211, bf16[256,512]{1,0:T(8,128)(2,1)S(1)} %collective-permute-done.1, bf16[256,256]{1,0:T(8,128)(2,1)} %collective-permute-done.7), kind=kOutput, calls=%fused_computation.56 | convolution fusion | flops 33685504 | bytes 720896 | tf_op jit(solution)/shard_map/dot_general | solution.py:129
  22.8 2.7 %collective-permute-start.8 = (bf16[128,512]{1,0:T(8,128)(2,1)S(1)}, bf16[128,512]{1,0:T(8,128)(2,1)S(1)}, u32[]{:S(2)}, u32[]{:S(2)}) collective-permute-start(bf16[128,512]{1,0:T(8,128)(2,1)S(1)} %fusion.40), channel_id=1, source_target_pairs={{0,2},{1,3},{2,0},{3,1},{4,6},{5,7},{6,4},{7,5},{8,10},{9,11},{10,... | collective-permute-start | bytes 393224 | tf_op jit(solution)/shard_map/ppermute | solution.py:81
  25.5 2.9 %collective-permute-done = bf16[256,256]{1,0:T(8,128)(2,1)} collective-permute-done((bf16[256,256]{1,0:T(8,128)(2,1)}, bf16[256,256]{1,0:T(8,128)(2,1)}, u32[]{:S(2)}, u32[]{:S(2)}) %collective-permute-start) | collective-permute-done | bytes 131104 | tf_op jit(solution)/shard_map/ppermute | solution.py:81
  28.4 1.0 fusion.38
  29.5 1.5 %collective-permute-start.2 = (bf16[128,512]{1,0:T(8,128)(2,1)S(1)}, bf16[128,512]{1,0:T(8,128)(2,1)S(1)}, u32[]{:S(2)}, u32[]{:S(2)}) collective-permute-start(bf16[128,512]{1,0:T(8,128)(2,1)S(1)} %fusion.38), channel_id=1, source_target_pairs={{0,2},{1,3},{2,0},{3,1},{4,6},{5,7},{6,4},{7,5},{8,10},{9,11},{10,... | collective-permute-start | bytes 393224 | tf_op jit(solution)/shard_map/ppermute | solution.py:81
  31.0 1.0 fusion.39
  32.1 1.5 %collective-permute-start.6 = (bf16[128,512]{1,0:T(8,128)(2,1)S(1)}, bf16[128,512]{1,0:T(8,128)(2,1)S(1)}, u32[]{:S(2)}, u32[]{:S(2)}) collective-permute-start(bf16[128,512]{1,0:T(8,128)(2,1)S(1)} %fusion.39), channel_id=1, source_target_pairs={{0,2},{1,3},{2,0},{3,1},{4,6},{5,7},{6,4},{7,5},{8,10},{9,11},{10,... | collective-permute-start | bytes 393224 | tf_op jit(solution)/shard_map/ppermute | solution.py:81
  33.6 1.0 fusion.35
  34.7 8.2 %collective-permute-done.6 = bf16[128,512]{1,0:T(8,128)(2,1)S(1)} collective-permute-done((bf16[128,512]{1,0:T(8,128)(2,1)S(1)}, bf16[128,512]{1,0:T(8,128)(2,1)S(1)}, u32[]{:S(2)}, u32[]{:S(2)}) %collective-permute-start.6) | collective-permute-done | bytes 131104 | tf_op jit(solution)/shard_map/ppermute | solution.py:81
  42.9 1.0 fusion.36
  44.0 1.8 %fusion.91 = (bf16[128,512]{1,0:T(8,128)(2,1)S(1)}, bf16[128,512]{1,0:T(8,128)(2,1)S(1)}, bf16[128,512]{1,0:T(8,128)(2,1)S(1)}, f32[1,1,128,512]{3,2,1,0:T(8,128...) fusion(f32[1,1,640,512]{3,2,1,0:T(8,128)S(1)} %copy-done.6, ...), kind=kOutput, calls=%fused_computation.145 | convolution fusion | flops 36896768 | bytes 5570560 | tf_op jit(solution)/shard_map/dot_general | solution.py:129
  45.8 1.8 %collective-permute-start.9 = (bf16[128,512]{1,0:T(8,128)(2,1)S(1)}, bf16[128,512]{1,0:T(8,128)(2,1)S(1)}, u32[]{:S(2)}, u32[]{:S(2)}) collective-permute-start(bf16[128,512]{1,0:T(8,128)(2,1)S(1)} %get-tuple-element.28), channel_id=1, source_target_pairs={{0,4},{4,0},{8,12},{12,8},{1,5},{5,1},{9,13},{13,9},{2,6},{6,2},{1... | collective-permute-start | bytes 393224 | tf_op jit(solution)/shard_map/ppermute | solution.py:81
  47.6 1.2 fusion.34
  48.9 1.6 %collective-permute-start.15 = (bf16[128,512]{1,0:T(8,128)(2,1)S(1)}, bf16[128,512]{1,0:T(8,128)(2,1)S(1)}, u32[]{:S(2)}, u32[]{:S(2)}) collective-permute-start(bf16[128,512]{1,0:T(8,128)(2,1)S(1)} %get-tuple-element.29), channel_id=1, source_target_pairs={{0,8},{4,12},{8,0},{12,4},{1,9},{5,13},{9,1},{13,5},{2,10},{6,14},... | collective-permute-start | bytes 393224 | tf_op jit(solution)/shard_map/ppermute | solution.py:81
  51.0 2.2 %collective-permute-start.10 = (bf16[128,512]{1,0:T(8,128)(2,1)S(1)}, bf16[128,512]{1,0:T(8,128)(2,1)S(1)}, u32[]{:S(2)}, u32[]{:S(2)}) collective-permute-start(bf16[128,512]{1,0:T(8,128)(2,1)S(1)} %add_convert_fusion.3), channel_id=1, source_target_pairs={{0,8},{4,12},{8,0},{12,4},{1,9},{5,13},{9,1},{13,5},{2,10},{6,14},... | collective-permute-start | bytes 393224 | tf_op jit(solution)/shard_map/ppermute | solution.py:81
  53.3 1.5 %collective-permute-done.15 = bf16[128,512]{1,0:T(8,128)(2,1)S(1)} collective-permute-done((bf16[128,512]{1,0:T(8,128)(2,1)S(1)}, bf16[128,512]{1,0:T(8,128)(2,1)S(1)}, u32[]{:S(2)}, u32[]{:S(2)}) %collective-permute-start.15) | collective-permute-done | bytes 131104 | tf_op jit(solution)/shard_map/ppermute | solution.py:81
  55.5 1.0 collective-permute-done.13
  57.4 4.4 %collective-permute-done.4 = bf16[256,512]{1,0:T(8,128)(2,1)S(1)} collective-permute-done((bf16[256,512]{1,0:T(8,128)(2,1)S(1)}, bf16[256,512]{1,0:T(8,128)(2,1)S(1)}, u32[]{:S(2)}, u32[]{:S(2)}) %collective-permute-start.4) | collective-permute-done | bytes 262176 | tf_op jit(solution)/shard_map/ppermute | solution.py:81
  61.7 1.7 %fusion.53 = (bf16[256,512]{1,0:T(8,128)(2,1)S(1)}, f32[1,1,256,512]{3,2,1,0:T(8,128)S(1)}) fusion(f32[1,1,640,512]{3,2,1,0:T(8,128)S(1)} %copy-done.6, f32[1,1,640,512]{3,2,1,0:T(8,128)S(1)} %copy-done.7, f32[1,1,640,512]{3,2,1,0:T(8,128)} %param.11, f32[1,640,512]{2,1,0:T(8,128)S(1)} %copy-done.5, bf16[256,512]{1,0:T(8,128)(2,1)S(1)} %collective-permute-done.4, ...), kind=kOutput, calls=%fused_computation.78 | convolution fusion | flops 69599232 | bytes 4063232 | tf_op jit(solution)/shard_map/dot_general | solution.py:129
  63.5 1.6 %collective-permute-start.11 = (bf16[256,512]{1,0:T(8,128)(2,1)S(1)}, bf16[256,512]{1,0:T(8,128)(2,1)S(1)}, u32[]{:S(2)}, u32[]{:S(2)}) collective-permute-start(bf16[256,512]{1,0:T(8,128)(2,1)S(1)} %get-tuple-element.64), channel_id=1, source_target_pairs={{0,8},{4,12},{8,0},{12,4},{1,9},{5,13},{9,1},{13,5},{2,10},{6,14},... | collective-permute-start | bytes 786440 | tf_op jit(solution)/shard_map/ppermute | solution.py:81
  66.1 2.0 %fusion = (f32[1,1,640,512]{3,2,1,0:T(8,128)}, f32[1,1,640,512]{3,2,1,0:T(8,128)}) fusion(f32[1,1,640,512]{3,2,1,0:T(8,128)S(1)} %copy-done.6, f32[1,1,128,512]{3,2,1,0:T(8,128)S(1)} %get-tuple-element.69, f32[1,1,128,512]{3,2,1,0:T(8,128)S(1)} %get-tuple-element.68, f32[1,1,256,512]{3,2,1,0:T(8,128)S(1)} %get-tuple-element.65, ...), kind=kLoop, calls=%fused_computation.1 | loop fusion | flops 3276800 | bytes 6553600 | tf_op jit(solution)/shard_map/add | solution.py:25
  68.1 3.6 %collective-permute-done.11 = bf16[256,512]{1,0:T(8,128)(2,1)S(1)} collective-permute-done((bf16[256,512]{1,0:T(8,128)(2,1)S(1)}, bf16[256,512]{1,0:T(8,128)(2,1)S(1)}, u32[]{:S(2)}, u32[]{:S(2)}) %collective-permute-start.11) | collective-permute-done | bytes 262176 | tf_op jit(solution)/shard_map/ppermute | solution.py:81
  73.1 1.7 %collective-permute-start.31 = (bf16[64,512]{1,0:T(8,128)(2,1)S(1)}, bf16[64,512]{1,0:T(8,128)(2,1)S(1)}, u32[]{:S(2)}, u32[]{:S(2)}) collective-permute-start(bf16[64,512]{1,0:T(8,128)(2,1)S(1)} %slice_select_fusion.2), channel_id=1, source_target_pairs={{0,3},{1,2},{2,1},{3,0},{4,7},{5,6},{6,5},{7,4},{8,11},{9,10},{10,... | collective-permute-start | bytes 196616 | tf_op jit(solution)/shard_map/ppermute | solution.py:81
  74.7 2.8 %collective-permute-start.29 = (bf16[64,512]{1,0:T(8,128)(2,1)S(1)}, bf16[64,512]{1,0:T(8,128)(2,1)S(1)}, u32[]{:S(2)}, u32[]{:S(2)}) collective-permute-start(bf16[64,512]{1,0:T(8,128)(2,1)S(1)} %slice_select_fusion.2), channel_id=1, source_target_pairs={{0,1},{1,0},{2,3},{3,2},{4,5},{5,4},{6,7},{7,6},{8,9},{9,8},{10,11... | collective-permute-start | bytes 196616 | tf_op jit(solution)/shard_map/ppermute | solution.py:81
  77.5 1.7 %collective-permute-start.35 = (bf16[64,512]{1,0:T(8,128)(2,1)S(1)}, bf16[64,512]{1,0:T(8,128)(2,1)S(1)}, u32[]{:S(2)}, u32[]{:S(2)}) collective-permute-start(bf16[64,512]{1,0:T(8,128)(2,1)S(1)} %slice_select_fusion.1), channel_id=1, source_target_pairs={{0,3},{1,2},{2,1},{3,0},{4,7},{5,6},{6,5},{7,4},{8,11},{9,10},{10,... | collective-permute-start | bytes 196616 | tf_op jit(solution)/shard_map/ppermute | solution.py:81
  79.5 3.5 %collective-permute-done.30 = bf16[64,512]{1,0:T(8,128)(2,1)S(1)} collective-permute-done((bf16[64,512]{1,0:T(8,128)(2,1)S(1)}, bf16[64,512]{1,0:T(8,128)(2,1)S(1)}, u32[]{:S(2)}, u32[]{:S(2)}) %collective-permute-start.30) | collective-permute-done | bytes 65568 | tf_op jit(solution)/shard_map/ppermute | solution.py:81
  83.0 2.3 %collective-permute-start.23 = (bf16[64,512]{1,0:T(8,128)(2,1)S(1)}, bf16[64,512]{1,0:T(8,128)(2,1)S(1)}, u32[]{:S(2)}, u32[]{:S(2)}) collective-permute-start(bf16[64,512]{1,0:T(8,128)(2,1)S(1)} %slice_select_fusion.3), channel_id=1, source_target_pairs={{0,3},{1,2},{2,1},{3,0},{4,7},{5,6},{6,5},{7,4},{8,11},{9,10},{10,... | collective-permute-start | bytes 196616 | tf_op jit(solution)/shard_map/ppermute | solution.py:81
  85.3 2.9 %collective-permute-start.22 = (bf16[64,512]{1,0:T(8,128)(2,1)S(1)}, bf16[64,512]{1,0:T(8,128)(2,1)S(1)}, u32[]{:S(2)}, u32[]{:S(2)}) collective-permute-start(bf16[64,512]{1,0:T(8,128)(2,1)S(1)} %slice_select_fusion.3), channel_id=1, source_target_pairs={{0,2},{1,3},{2,0},{3,1},{4,6},{5,7},{6,4},{7,5},{8,10},{9,11},{10,... | collective-permute-start | bytes 196616 | tf_op jit(solution)/shard_map/ppermute | solution.py:81
  88.3 0.8 collective-permute-done.34
  89.7 1.5 %collective-permute-done.22 = bf16[64,512]{1,0:T(8,128)(2,1)S(1)} collective-permute-done((bf16[64,512]{1,0:T(8,128)(2,1)S(1)}, bf16[64,512]{1,0:T(8,128)(2,1)S(1)}, u32[]{:S(2)}, u32[]{:S(2)}) %collective-permute-start.22) | collective-permute-done | bytes 65568 | tf_op jit(solution)/shard_map/ppermute | solution.py:81
  91.2 2.2 %collective-permute-done.21 = bf16[64,512]{1,0:T(8,128)(2,1)S(1)} collective-permute-done((bf16[64,512]{1,0:T(8,128)(2,1)S(1)}, bf16[64,512]{1,0:T(8,128)(2,1)S(1)}, u32[]{:S(2)}, u32[]{:S(2)}) %collective-permute-start.21) | collective-permute-done | bytes 65568 | tf_op jit(solution)/shard_map/ppermute | solution.py:81
  94.2 1.3 %maximum_add_fusion = f32[1,640,512]{2,1,0:T(8,128)} fusion(f32[1,128,512]{2,1,0:T(8,128)S(1)} %get-tuple-element.67, f32[1,128,512]{2,1,0:T(8,128)S(1)} %get-tuple-element.66, f32[1,256,512]{2,1,0:T(8,128)S(1)} %get-tuple-element.63, f32[1,128,512]{2,1,0:T(8,128)S(1)} %get-tuple-element.70, f32[1,640,512]{2,1,0:T(8,128)S(1)} %copy-done.3), kind=kLoop, calls=%fused_computation.3 | loop fusion | flops 1638400 | bytes 3932160 | tf_op jit(solution)/shard_map/add | solution.py:33
  101.4 1.7 %collective-permute-start.27 = (bf16[128,512]{1,0:T(8,128)(2,1)S(1)}, bf16[128,512]{1,0:T(8,128)(2,1)S(1)}, u32[]{:S(2)}, u32[]{:S(2)}) collective-permute-start(bf16[128,512]{1,0:T(8,128)(2,1)S(1)} %slice_select_fusion), channel_id=1, source_target_pairs={{0,3},{1,2},{2,1},{3,0},{4,7},{5,6},{6,5},{7,4},{8,11},{9,10},{10,... | collective-permute-start | bytes 393224 | tf_op jit(solution)/shard_map/ppermute | solution.py:81
  103.0 2.8 %collective-permute-start.25 = (bf16[128,512]{1,0:T(8,128)(2,1)S(1)}, bf16[128,512]{1,0:T(8,128)(2,1)S(1)}, u32[]{:S(2)}, u32[]{:S(2)}) collective-permute-start(bf16[128,512]{1,0:T(8,128)(2,1)S(1)} %slice_select_fusion), channel_id=1, source_target_pairs={{0,1},{1,0},{2,3},{3,2},{4,5},{5,4},{6,7},{7,6},{8,9},{9,8},{10,11... | collective-permute-start | bytes 393224 | tf_op jit(solution)/shard_map/ppermute | solution.py:81
  105.8 3.9 %collective-permute-done.27 = bf16[128,512]{1,0:T(8,128)(2,1)S(1)} collective-permute-done((bf16[128,512]{1,0:T(8,128)(2,1)S(1)}, bf16[128,512]{1,0:T(8,128)(2,1)S(1)}, u32[]{:S(2)}, u32[]{:S(2)}) %collective-permute-start.27) | collective-permute-done | bytes 131104 | tf_op jit(solution)/shard_map/ppermute | solution.py:81
  109.7 5.0 %collective-permute-done.26 = bf16[128,512]{1,0:T(8,128)(2,1)S(1)} collective-permute-done((bf16[128,512]{1,0:T(8,128)(2,1)S(1)}, bf16[128,512]{1,0:T(8,128)(2,1)S(1)}, u32[]{:S(2)}, u32[]{:S(2)}) %collective-permute-start.26) | collective-permute-done | bytes 131104 | tf_op jit(solution)/shard_map/ppermute | solution.py:81
  115.1 2.0 %multiply_subtract_fusion = (f32[640,512]{1,0:T(8,128)}, f32[640,512]{1,0:T(8,128)}) fusion(f32[640,512]{1,0:T(8,128)S(1)} %copy-done.2, f32[128,512]{1,0:T(8,128)S(1)} %get-tuple-element.35, f32[128,512]{1,0:T(8,128)S(1)} %get-tuple-element.37, f32[256,512]{1,0:T(8,128)S(1)} %get-tuple-element.15, f32[128,512]{1,0:T(8,128)S(1)} %get-tuple-element.10, ...), kind=kLoop, calls=%fused_computation.5 | loop fusion | flops 2949120 | bytes 6553600 | tf_op jit(solution)/shard_map/sub | solution.py:40
  119.3 1.6 %fusion.33 = bf16[256,512]{1,0:T(8,128)(2,1)} fusion(f32[256,512]{1,0:T(8,128)S(1)} %fusion.126, f32[256,512]{1,0:T(8,128)S(1)} %fusion.128, f32[256,512]{1,0:T(8,128)S(1)} %fusion.130, f32[256,512]{1,0:T(8,128)S(1)} %fusion.132, f32[256,512]{1,0:T(8,128)S(1)} %fusion.134, f32[256,512]{1,0:T(8,128)S(1)} %fusion.136, f32[256,512]{1,0:T(8,128)S(1)} %fusion.138, ...), kind=kOutput, calls=%fused_computation.43 | convolution fusion | flops 21135360 | bytes 16711681 | tf_op jit(solution)/shard_map/dot_general | solution.py:182
  (148 shorter events, 19.4 us)
Async XLA Ops:
  0.6 5.1 %copy-start.1 = (bf16[256,2560]{1,0:T(8,128)(2,1)S(1)}, bf16[256,2560]{1,0:T(8,128)(2,1)}, u32[]{:S(2)}) copy-start(bf16[256,2560]{1,0:T(8,128)(2,1)} %param.9) | copy-start | bytes 3932164
  0.7 5.8 %copy-start = (bf16[256,512]{1,0:T(8,128)(2,1)S(1)}, bf16[256,512]{1,0:T(8,128)(2,1)}, u32[]{:S(2)}) copy-start(bf16[256,512]{1,0:T(8,128)(2,1)} %param.10) | copy-start | bytes 786436
  2.7 16.2 %collective-permute-start.7 = (bf16[256,256]{1,0:T(8,128)(2,1)}, bf16[256,256]{1,0:T(8,128)(2,1)}, u32[]{:S(2)}, u32[]{:S(2)}) collective-permute-start(bf16[256,256]{1,0:T(8,128)(2,1)} %pad_maximum_fusion.9), channel_id=1, source_target_pairs={{0,1},{1,0},{2,3},{3,2},{4,5},{5,4},{6,7},{7,6},{8,9},{9,8},{10,11... | collective-permute-start | bytes 393224 | tf_op jit(solution)/shard_map/ppermute | solution.py:81
  6.5 41.2 %collective-permute-start.3 = (bf16[256,512]{1,0:T(8,128)(2,1)}, bf16[256,512]{1,0:T(8,128)(2,1)}, u32[]{:S(2)}, u32[]{:S(2)}) collective-permute-start(bf16[256,512]{1,0:T(8,128)(2,1)} %pad_maximum_fusion.3), channel_id=1, source_target_pairs={{0,1},{1,0},{2,3},{3,2},{4,5},{5,4},{6,7},{7,6},{8,9},{9,8},{10,11... | collective-permute-start | bytes 786440 | tf_op jit(solution)/shard_map/ppermute | solution.py:81
  6.5 15.1 %collective-permute-start.1 = (bf16[256,512]{1,0:T(8,128)(2,1)S(1)}, bf16[256,512]{1,0:T(8,128)(2,1)S(1)}, u32[]{:S(2)}, u32[]{:S(2)}) collective-permute-start(bf16[256,512]{1,0:T(8,128)(2,1)S(1)} %copy-done), channel_id=1, source_target_pairs={{0,1},{1,0},{2,3},{3,2},{4,5},{5,4},{6,7},{7,6},{8,9},{9,8},{10,11... | collective-permute-start | bytes 786440 | tf_op jit(solution)/shard_map/ppermute | solution.py:81
  9.2 21.8 %collective-permute-start.5 = (bf16[256,256]{1,0:T(8,128)(2,1)}, bf16[256,256]{1,0:T(8,128)(2,1)}, u32[]{:S(2)}, u32[]{:S(2)}) collective-permute-start(bf16[256,256]{1,0:T(8,128)(2,1)} %pad_maximum_fusion.8), channel_id=1, source_target_pairs={{0,1},{1,0},{2,3},{3,2},{4,5},{5,4},{6,7},{7,6},{8,9},{9,8},{10,11... | collective-permute-start | bytes 393224 | tf_op jit(solution)/shard_map/ppermute | solution.py:81
  9.9 18.5 %collective-permute-start = (bf16[256,256]{1,0:T(8,128)(2,1)}, bf16[256,256]{1,0:T(8,128)(2,1)}, u32[]{:S(2)}, u32[]{:S(2)}) collective-permute-start(bf16[256,256]{1,0:T(8,128)(2,1)} %pad_maximum_fusion.7), channel_id=1, source_target_pairs={{0,1},{1,0},{2,3},{3,2},{4,5},{5,4},{6,7},{7,6},{8,9},{9,8},{10,11... | collective-permute-start | bytes 393224 | tf_op jit(solution)/shard_map/ppermute | solution.py:81
  18.8 14.8 %copy-start.8 = (f32[128,512]{1,0:T(8,128)S(1)}, f32[128,512]{1,0:T(8,128)}, u32[]{:S(2)}) copy-start(f32[128,512]{1,0:T(8,128)} %fusion.251) | copy-start | bytes 786436
  18.8 25.1 %copy-start.17 = (f32[128,512]{1,0:T(8,128)S(1)}, f32[128,512]{1,0:T(8,128)}, u32[]{:S(2)}) copy-start(f32[128,512]{1,0:T(8,128)} %fusion.248) | copy-start | bytes 786436
  21.5 22.4 %copy-start.7 = (f32[1,1,640,512]{3,2,1,0:T(8,128)S(1)}, f32[1,1,640,512]{3,2,1,0:T(8,128)}, u32[]{:S(2)}) copy-start(f32[1,1,640,512]{3,2,1,0:T(8,128)} %param.12) | copy-start | bytes 3932164
  22.8 10.8 %collective-permute-start.8 = (bf16[128,512]{1,0:T(8,128)(2,1)S(1)}, bf16[128,512]{1,0:T(8,128)(2,1)S(1)}, u32[]{:S(2)}, u32[]{:S(2)}) collective-permute-start(bf16[128,512]{1,0:T(8,128)(2,1)S(1)} %fusion.40), channel_id=1, source_target_pairs={{0,2},{1,3},{2,0},{3,1},{4,6},{5,7},{6,4},{7,5},{8,10},{9,11},{10,... | collective-permute-start | bytes 393224 | tf_op jit(solution)/shard_map/ppermute | solution.py:81
  29.5 14.5 %copy-start.5 = (f32[1,640,512]{2,1,0:T(8,128)S(1)}, f32[1,640,512]{2,1,0:T(8,128)}, u32[]{:S(2)}) copy-start(f32[1,640,512]{2,1,0:T(8,128)} %param.14) | copy-start | bytes 3932164
  29.5 14.5 %copy-start.6 = (f32[1,1,640,512]{3,2,1,0:T(8,128)S(1)}, f32[1,1,640,512]{3,2,1,0:T(8,128)}, u32[]{:S(2)}) copy-start(f32[1,1,640,512]{3,2,1,0:T(8,128)} %param.13) | copy-start | bytes 3932164
  29.5 14.4 %collective-permute-start.2 = (bf16[128,512]{1,0:T(8,128)(2,1)S(1)}, bf16[128,512]{1,0:T(8,128)(2,1)S(1)}, u32[]{:S(2)}, u32[]{:S(2)}) collective-permute-start(bf16[128,512]{1,0:T(8,128)(2,1)S(1)} %fusion.38), channel_id=1, source_target_pairs={{0,2},{1,3},{2,0},{3,1},{4,6},{5,7},{6,4},{7,5},{8,10},{9,11},{10,... | collective-permute-start | bytes 393224 | tf_op jit(solution)/shard_map/ppermute | solution.py:81
  32.1 10.8 %collective-permute-start.6 = (bf16[128,512]{1,0:T(8,128)(2,1)S(1)}, bf16[128,512]{1,0:T(8,128)(2,1)S(1)}, u32[]{:S(2)}, u32[]{:S(2)}) collective-permute-start(bf16[128,512]{1,0:T(8,128)(2,1)S(1)} %fusion.39), channel_id=1, source_target_pairs={{0,2},{1,3},{2,0},{3,1},{4,6},{5,7},{6,4},{7,5},{8,10},{9,11},{10,... | collective-permute-start | bytes 393224 | tf_op jit(solution)/shard_map/ppermute | solution.py:81
  45.8 16.0 %copy-start.16 = (f32[256,512]{1,0:T(8,128)S(1)}, f32[256,512]{1,0:T(8,128)}, u32[]{:S(2)}) copy-start(f32[256,512]{1,0:T(8,128)} %fusion.249) | copy-start | bytes 1572868
  45.8 5.2 %collective-permute-start.9 = (bf16[128,512]{1,0:T(8,128)(2,1)S(1)}, bf16[128,512]{1,0:T(8,128)(2,1)S(1)}, u32[]{:S(2)}, u32[]{:S(2)}) collective-permute-start(bf16[128,512]{1,0:T(8,128)(2,1)S(1)} %get-tuple-element.28), channel_id=1, source_target_pairs={{0,4},{4,0},{8,12},{12,8},{1,5},{5,1},{9,13},{13,9},{2,6},{6,2},{1... | collective-permute-start | bytes 393224 | tf_op jit(solution)/shard_map/ppermute | solution.py:81
  48.8 12.9 %collective-permute-start.4 = (bf16[256,512]{1,0:T(8,128)(2,1)S(1)}, bf16[256,512]{1,0:T(8,128)(2,1)S(1)}, u32[]{:S(2)}, u32[]{:S(2)}) collective-permute-start(bf16[256,512]{1,0:T(8,128)(2,1)S(1)} %fusion.34), channel_id=1, source_target_pairs={{0,2},{1,3},{2,0},{3,1},{4,6},{5,7},{6,4},{7,5},{8,10},{9,11},{10,... | collective-permute-start | bytes 786440 | tf_op jit(solution)/shard_map/ppermute | solution.py:81
  48.9 5.9 %collective-permute-start.15 = (bf16[128,512]{1,0:T(8,128)(2,1)S(1)}, bf16[128,512]{1,0:T(8,128)(2,1)S(1)}, u32[]{:S(2)}, u32[]{:S(2)}) collective-permute-start(bf16[128,512]{1,0:T(8,128)(2,1)S(1)} %get-tuple-element.29), channel_id=1, source_target_pairs={{0,8},{4,12},{8,0},{12,4},{1,9},{5,13},{9,1},{13,5},{2,10},{6,14},... | collective-permute-start | bytes 393224 | tf_op jit(solution)/shard_map/ppermute | solution.py:81
  50.5 6.1 %collective-permute-start.13 = (bf16[128,512]{1,0:T(8,128)(2,1)S(1)}, bf16[128,512]{1,0:T(8,128)(2,1)S(1)}, u32[]{:S(2)}, u32[]{:S(2)}) collective-permute-start(bf16[128,512]{1,0:T(8,128)(2,1)S(1)} %get-tuple-element.30), channel_id=1, source_target_pairs={{0,4},{4,0},{8,12},{12,8},{1,5},{5,1},{9,13},{13,9},{2,6},{6,2},{1... | collective-permute-start | bytes 393224 | tf_op jit(solution)/shard_map/ppermute | solution.py:81
  51.0 14.1 %collective-permute-start.10 = (bf16[128,512]{1,0:T(8,128)(2,1)S(1)}, bf16[128,512]{1,0:T(8,128)(2,1)S(1)}, u32[]{:S(2)}, u32[]{:S(2)}) collective-permute-start(bf16[128,512]{1,0:T(8,128)(2,1)S(1)} %add_convert_fusion.3), channel_id=1, source_target_pairs={{0,8},{4,12},{8,0},{12,4},{1,9},{5,13},{9,1},{13,5},{2,10},{6,14},... | collective-permute-start | bytes 393224 | tf_op jit(solution)/shard_map/ppermute | solution.py:81
  54.8 10.3 %collective-permute-start.16 = (bf16[128,512]{1,0:T(8,128)(2,1)S(1)}, bf16[128,512]{1,0:T(8,128)(2,1)S(1)}, u32[]{:S(2)}, u32[]{:S(2)}) collective-permute-start(bf16[128,512]{1,0:T(8,128)(2,1)S(1)} %add_convert_fusion.1), channel_id=1, source_target_pairs={{0,4},{4,0},{8,12},{12,8},{1,5},{5,1},{9,13},{13,9},{2,6},{6,2},{1... | collective-permute-start | bytes 393224 | tf_op jit(solution)/shard_map/ppermute | solution.py:81
  56.6 8.5 %copy-start.2 = (f32[640,512]{1,0:T(8,128)S(1)}, f32[640,512]{1,0:T(8,128)}, u32[]{:S(2)}) copy-start(f32[640,512]{1,0:T(8,128)} %param.16) | copy-start | bytes 3932164
  56.6 8.5 %copy-start.3 = (f32[1,640,512]{2,1,0:T(8,128)S(1)}, f32[1,640,512]{2,1,0:T(8,128)}, u32[]{:S(2)}) copy-start(f32[1,640,512]{2,1,0:T(8,128)} %param.15) | copy-start | bytes 3932164
  56.6 8.5 %collective-permute-start.14 = (bf16[128,512]{1,0:T(8,128)(2,1)S(1)}, bf16[128,512]{1,0:T(8,128)(2,1)S(1)}, u32[]{:S(2)}, u32[]{:S(2)}) collective-permute-start(bf16[128,512]{1,0:T(8,128)(2,1)S(1)} %add_convert_fusion.2), channel_id=1, source_target_pairs={{0,8},{4,12},{8,0},{12,4},{1,9},{5,13},{9,1},{13,5},{2,10},{6,14},... | collective-permute-start | bytes 393224 | tf_op jit(solution)/shard_map/ppermute | solution.py:81
  63.5 8.3 %collective-permute-start.11 = (bf16[256,512]{1,0:T(8,128)(2,1)S(1)}, bf16[256,512]{1,0:T(8,128)(2,1)S(1)}, u32[]{:S(2)}, u32[]{:S(2)}) collective-permute-start(bf16[256,512]{1,0:T(8,128)(2,1)S(1)} %get-tuple-element.64), channel_id=1, source_target_pairs={{0,8},{4,12},{8,0},{12,4},{1,9},{5,13},{9,1},{13,5},{2,10},{6,14},... | collective-permute-start | bytes 786440 | tf_op jit(solution)/shard_map/ppermute | solution.py:81
  65.5 7.1 %collective-permute-start.17 = (f32[128,512]{1,0:T(8,128)S(1)}, f32[128,512]{1,0:T(8,128)S(1)}, u32[]{:S(2)}, u32[]{:S(2)}) collective-permute-start(f32[128,512]{1,0:T(8,128)S(1)} %get-tuple-element.31), channel_id=1, source_target_pairs={{0,16},{16,0},{1,17},{17,1},{2,18},{18,2},{3,19},{19,3},{4,20},{20... | collective-permute-start | bytes 786440 | tf_op jit(solution)/shard_map/ppermute | solution.py:81
  65.6 7.0 %collective-permute-start.20 = (f32[128,512]{1,0:T(8,128)S(1)}, f32[128,512]{1,0:T(8,128)S(1)}, u32[]{:S(2)}, u32[]{:S(2)}) collective-permute-start(f32[128,512]{1,0:T(8,128)S(1)} %get-tuple-element.32), channel_id=1, source_target_pairs={{0,16},{16,0},{1,17},{17,1},{2,18},{18,2},{3,19},{19,3},{4,20},{20... | collective-permute-start | bytes 786440 | tf_op jit(solution)/shard_map/ppermute | solution.py:81
  66.1 6.5 %collective-permute-start.19 = (f32[128,512]{1,0:T(8,128)S(1)}, f32[128,512]{1,0:T(8,128)S(1)}, u32[]{:S(2)}, u32[]{:S(2)}) collective-permute-start(f32[128,512]{1,0:T(8,128)S(1)} %get-tuple-element.33), channel_id=1, source_target_pairs={{0,16},{16,0},{1,17},{17,1},{2,18},{18,2},{3,19},{19,3},{4,20},{20... | collective-permute-start | bytes 786440 | tf_op jit(solution)/shard_map/ppermute | solution.py:81
  66.1 6.4 %copy-start.4 = (f32[640,512]{1,0:T(8,128)S(1)}, f32[640,512]{1,0:T(8,128)}, u32[]{:S(2)}) copy-start(f32[640,512]{1,0:T(8,128)} %param.17) | copy-start | bytes 3932164
  71.9 21.6 %collective-permute-start.12 = (bf16[256,512]{1,0:T(8,128)(2,1)S(1)}, bf16[256,512]{1,0:T(8,128)(2,1)S(1)}, u32[]{:S(2)}, u32[]{:S(2)}) collective-permute-start(bf16[256,512]{1,0:T(8,128)(2,1)S(1)} %add_convert_fusion), channel_id=1, source_target_pairs={{0,4},{4,0},{8,12},{12,8},{1,5},{5,1},{9,13},{13,9},{2,6},{6,2},{1... | collective-permute-start | bytes 786440 | tf_op jit(solution)/shard_map/ppermute | solution.py:81
  73.1 6.4 %collective-permute-start.31 = (bf16[64,512]{1,0:T(8,128)(2,1)S(1)}, bf16[64,512]{1,0:T(8,128)(2,1)S(1)}, u32[]{:S(2)}, u32[]{:S(2)}) collective-permute-start(bf16[64,512]{1,0:T(8,128)(2,1)S(1)} %slice_select_fusion.2), channel_id=1, source_target_pairs={{0,3},{1,2},{2,1},{3,0},{4,7},{5,6},{6,5},{7,4},{8,11},{9,10},{10,... | collective-permute-start | bytes 196616 | tf_op jit(solution)/shard_map/ppermute | solution.py:81
  74.7 8.3 %collective-permute-start.30 = (bf16[64,512]{1,0:T(8,128)(2,1)S(1)}, bf16[64,512]{1,0:T(8,128)(2,1)S(1)}, u32[]{:S(2)}, u32[]{:S(2)}) collective-permute-start(bf16[64,512]{1,0:T(8,128)(2,1)S(1)} %slice_select_fusion.2), channel_id=1, source_target_pairs={{0,2},{1,3},{2,0},{3,1},{4,6},{5,7},{6,4},{7,5},{8,10},{9,11},{10,... | collective-permute-start | bytes 196616 | tf_op jit(solution)/shard_map/ppermute | solution.py:81
  74.7 8.3 %collective-permute-start.29 = (bf16[64,512]{1,0:T(8,128)(2,1)S(1)}, bf16[64,512]{1,0:T(8,128)(2,1)S(1)}, u32[]{:S(2)}, u32[]{:S(2)}) collective-permute-start(bf16[64,512]{1,0:T(8,128)(2,1)S(1)} %slice_select_fusion.2), channel_id=1, source_target_pairs={{0,1},{1,0},{2,3},{3,2},{4,5},{5,4},{6,7},{7,6},{8,9},{9,8},{10,11... | collective-permute-start | bytes 196616 | tf_op jit(solution)/shard_map/ppermute | solution.py:81
  77.5 7.8 %collective-permute-start.35 = (bf16[64,512]{1,0:T(8,128)(2,1)S(1)}, bf16[64,512]{1,0:T(8,128)(2,1)S(1)}, u32[]{:S(2)}, u32[]{:S(2)}) collective-permute-start(bf16[64,512]{1,0:T(8,128)(2,1)S(1)} %slice_select_fusion.1), channel_id=1, source_target_pairs={{0,3},{1,2},{2,1},{3,0},{4,7},{5,6},{6,5},{7,4},{8,11},{9,10},{10,... | collective-permute-start | bytes 196616 | tf_op jit(solution)/shard_map/ppermute | solution.py:81
  79.5 9.6 %collective-permute-start.34 = (bf16[64,512]{1,0:T(8,128)(2,1)S(1)}, bf16[64,512]{1,0:T(8,128)(2,1)S(1)}, u32[]{:S(2)}, u32[]{:S(2)}) collective-permute-start(bf16[64,512]{1,0:T(8,128)(2,1)S(1)} %slice_select_fusion.1), channel_id=1, source_target_pairs={{0,2},{1,3},{2,0},{3,1},{4,6},{5,7},{6,4},{7,5},{8,10},{9,11},{10,... | collective-permute-start | bytes 196616 | tf_op jit(solution)/shard_map/ppermute | solution.py:81
  83.0 6.0 %collective-permute-start.33 = (bf16[64,512]{1,0:T(8,128)(2,1)S(1)}, bf16[64,512]{1,0:T(8,128)(2,1)S(1)}, u32[]{:S(2)}, u32[]{:S(2)}) collective-permute-start(bf16[64,512]{1,0:T(8,128)(2,1)S(1)} %slice_select_fusion.1), channel_id=1, source_target_pairs={{0,1},{1,0},{2,3},{3,2},{4,5},{5,4},{6,7},{7,6},{8,9},{9,8},{10,11... | collective-permute-start | bytes 196616 | tf_op jit(solution)/shard_map/ppermute | solution.py:81
  83.0 6.6 %collective-permute-start.23 = (bf16[64,512]{1,0:T(8,128)(2,1)S(1)}, bf16[64,512]{1,0:T(8,128)(2,1)S(1)}, u32[]{:S(2)}, u32[]{:S(2)}) collective-permute-start(bf16[64,512]{1,0:T(8,128)(2,1)S(1)} %slice_select_fusion.3), channel_id=1, source_target_pairs={{0,3},{1,2},{2,1},{3,0},{4,7},{5,6},{6,5},{7,4},{8,11},{9,10},{10,... | collective-permute-start | bytes 196616 | tf_op jit(solution)/shard_map/ppermute | solution.py:81
  85.3 5.8 %collective-permute-start.22 = (bf16[64,512]{1,0:T(8,128)(2,1)S(1)}, bf16[64,512]{1,0:T(8,128)(2,1)S(1)}, u32[]{:S(2)}, u32[]{:S(2)}) collective-permute-start(bf16[64,512]{1,0:T(8,128)(2,1)S(1)} %slice_select_fusion.3), channel_id=1, source_target_pairs={{0,2},{1,3},{2,0},{3,1},{4,6},{5,7},{6,4},{7,5},{8,10},{9,11},{10,... | collective-permute-start | bytes 196616 | tf_op jit(solution)/shard_map/ppermute | solution.py:81
  89.1 4.3 %collective-permute-start.21 = (bf16[64,512]{1,0:T(8,128)(2,1)S(1)}, bf16[64,512]{1,0:T(8,128)(2,1)S(1)}, u32[]{:S(2)}, u32[]{:S(2)}) collective-permute-start(bf16[64,512]{1,0:T(8,128)(2,1)S(1)} %slice_select_fusion.3), channel_id=1, source_target_pairs={{0,1},{1,0},{2,3},{3,2},{4,5},{5,4},{6,7},{7,6},{8,9},{9,8},{10,11... | collective-permute-start | bytes 196616 | tf_op jit(solution)/shard_map/ppermute | solution.py:81
  89.1 10.2 %collective-permute-start.32 = (bf16[4,64,512]{2,1,0:T(8,128)(2,1)S(1)}, bf16[4,64,512]{2,1,0:T(8,128)(2,1)S(1)}, u32[]{:S(2)}, u32[]{:S(2)}) collective-permute-start(bf16[4,64,512]{2,1,0:T(8,128)(2,1)S(1)} %pad_maximum_fusion.5), channel_id=1, source_target_pairs={{0,16},{16,0},{1,17},{17,1},{2,18},{18,2},{3,19},{19,3},{4,20},{20... | collective-permute-start | bytes 786440 | tf_op jit(solution)/shard_map/ppermute | solution.py:81
  89.6 7.7 %collective-permute-start.36 = (bf16[4,64,512]{2,1,0:T(8,128)(2,1)S(1)}, bf16[4,64,512]{2,1,0:T(8,128)(2,1)S(1)}, u32[]{:S(2)}, u32[]{:S(2)}) collective-permute-start(bf16[4,64,512]{2,1,0:T(8,128)(2,1)S(1)} %pad_maximum_fusion.6), channel_id=1, source_target_pairs={{0,16},{16,0},{1,17},{17,1},{2,18},{18,2},{3,19},{19,3},{4,20},{20... | collective-permute-start | bytes 786440 | tf_op jit(solution)/shard_map/ppermute | solution.py:81
  93.4 2.2 %collective-permute-start.24 = (bf16[4,64,512]{2,1,0:T(8,128)(2,1)S(1)}, bf16[4,64,512]{2,1,0:T(8,128)(2,1)S(1)}, u32[]{:S(2)}, u32[]{:S(2)}) collective-permute-start(bf16[4,64,512]{2,1,0:T(8,128)(2,1)S(1)} %pad_maximum_fusion.4), channel_id=1, source_target_pairs={{0,16},{16,0},{1,17},{17,1},{2,18},{18,2},{3,19},{19,3},{4,20},{20... | collective-permute-start | bytes 786440 | tf_op jit(solution)/shard_map/ppermute | solution.py:81
  93.7 7.4 %collective-permute-start.18 = (f32[256,512]{1,0:T(8,128)S(1)}, f32[256,512]{1,0:T(8,128)S(1)}, u32[]{:S(2)}, u32[]{:S(2)}) collective-permute-start(f32[256,512]{1,0:T(8,128)S(1)} %get-tuple-element.62), channel_id=1, source_target_pairs={{0,16},{16,0},{1,17},{17,1},{2,18},{18,2},{3,19},{19,3},{4,20},{20... | collective-permute-start | bytes 1572872 | tf_op jit(solution)/shard_map/ppermute | solution.py:81
  101.4 8.3 %collective-permute-start.27 = (bf16[128,512]{1,0:T(8,128)(2,1)S(1)}, bf16[128,512]{1,0:T(8,128)(2,1)S(1)}, u32[]{:S(2)}, u32[]{:S(2)}) collective-permute-start(bf16[128,512]{1,0:T(8,128)(2,1)S(1)} %slice_select_fusion), channel_id=1, source_target_pairs={{0,3},{1,2},{2,1},{3,0},{4,7},{5,6},{6,5},{7,4},{8,11},{9,10},{10,... | collective-permute-start | bytes 393224 | tf_op jit(solution)/shard_map/ppermute | solution.py:81
  103.0 11.7 %collective-permute-start.26 = (bf16[128,512]{1,0:T(8,128)(2,1)S(1)}, bf16[128,512]{1,0:T(8,128)(2,1)S(1)}, u32[]{:S(2)}, u32[]{:S(2)}) collective-permute-start(bf16[128,512]{1,0:T(8,128)(2,1)S(1)} %slice_select_fusion), channel_id=1, source_target_pairs={{0,2},{1,3},{2,0},{3,1},{4,6},{5,7},{6,4},{7,5},{8,10},{9,11},{10,... | collective-permute-start | bytes 393224 | tf_op jit(solution)/shard_map/ppermute | solution.py:81
  103.0 11.7 %collective-permute-start.25 = (bf16[128,512]{1,0:T(8,128)(2,1)S(1)}, bf16[128,512]{1,0:T(8,128)(2,1)S(1)}, u32[]{:S(2)}, u32[]{:S(2)}) collective-permute-start(bf16[128,512]{1,0:T(8,128)(2,1)S(1)} %slice_select_fusion), channel_id=1, source_target_pairs={{0,1},{1,0},{2,3},{3,2},{4,5},{5,4},{6,7},{7,6},{8,9},{9,8},{10,11... | collective-permute-start | bytes 393224 | tf_op jit(solution)/shard_map/ppermute | solution.py:81
  114.8 2.3 %collective-permute-start.28 = (bf16[4,128,512]{2,1,0:T(8,128)(2,1)S(1)}, bf16[4,128,512]{2,1,0:T(8,128)(2,1)S(1)}, u32[]{:S(2)}, u32[]{:S(2)}) collective-permute-start(bf16[4,128,512]{2,1,0:T(8,128)(2,1)S(1)} %pad_maximum_fusion.2), channel_id=1, source_target_pairs={{0,16},{16,0},{1,17},{17,1},{2,18},{18,2},{3,19},{19,3},{4,20},{20... | collective-permute-start | bytes 1572872 | tf_op jit(solution)/shard_map/ppermute | solution.py:81
  (7 other events, 8.0 us)

commit v2 on v0

v2 whole, which is shorter than its diff:
```python
import math

import jax
import jax.numpy as jnp
from jax import lax
from jax.experimental import pallas as pl
from jax.experimental.pallas import tpu as pltpu
from jax.sharding import PartitionSpec as P

DW = 2560
LANES = 128
VMEM_BYTES = 16 * 2**20
SIZES = [2, 3]
GROUPS = [[0], [1]]
SHARE = 3
ORDER = ("c0", "c1", "x0", "x1", "b0", "s0", "s1", "a0", "p0", "q0", "a1", "p1", "m1", "k0", "j0", "q1", "v1", "o1", "k1", "j1")


beta_first = 0.9
beta_second = 0.999
adam_eps = 1e-08
inner_rate = 0.05
weight_decay = 0.1
region_mu = 0.9
region_rate = 0.7
global_mu = 0.9
global_rate = 0.7


def moments(gradient, adam_first, adam_second):
    first_new = beta_first * adam_first + (1.0 - beta_first) * gradient
    second_new = beta_second * adam_second + (1.0 - beta_second) * gradient * gradient
    return first_new, second_new


def adam(gradient, island_weight, adam_first, adam_second):
    first_new, second_new = moments(gradient, adam_first, adam_second)
    inner = island_weight - inner_rate * (
        first_new / (jnp.sqrt(second_new) + adam_eps) + weight_decay * island_weight
    )
    return first_new, second_new, inner


def regional(region_mean, region_anchor, region_momentum):
    region_velocity = region_mu * region_momentum + region_mean
    region_params = region_anchor - region_rate * (region_mean + region_mu * region_velocity)
    return region_velocity, region_params


def outer(global_mean, global_anchor, global_momentum):
    global_velocity = global_mu * global_momentum + global_mean
    global_new = global_anchor - global_rate * (global_mean + global_mu * global_velocity)
    return global_velocity, global_new


def generic_body(
    activations,
    cotangent,
    island_weight,
    adam_first,
    adam_second,
    region_anchor,
    region_momentum,
    global_anchor,
    global_momentum,
):
    island_tokens = activations.shape[0] * lax.axis_size("dev")
    islands = lax.axis_size("island")
    regions = lax.axis_size("region")
    summed = lax.psum_scatter(
        lax.dot_general(
            activations, cotangent, (((0,), (0,)), ((), ())), preferred_element_type=jnp.float32
        ).astype(jnp.bfloat16),
        "dev",
        scatter_dimension=0,
        tiled=True,
    ).astype(jnp.float32)
    gradient = summed * (1.0 / math.sqrt(island_tokens))
    first_new, second_new, inner = adam(gradient, island_weight, adam_first, adam_second)
    island_delta = region_anchor[:, None] - inner
    region_mean = lax.psum(island_delta, "island")[:, 0] / islands
    region_velocity, region_params = regional(region_mean, region_anchor, region_momentum)
    region_gap = global_anchor[None] - region_params
    global_mean = lax.psum(region_gap, "region")[0] / regions
    global_velocity, global_new = outer(global_mean, global_anchor, global_momentum)
    weight_full = lax.all_gather(global_new.astype(jnp.bfloat16), "dev", axis=0, tiled=True)
    projected = jnp.dot(activations, weight_full, preferred_element_type=jnp.float32)
    next_keys = (projected * (1.0 / math.sqrt(activations.shape[1]))).astype(jnp.bfloat16)
    return (first_new, second_new, region_velocity, global_velocity, global_new, next_keys)


def flip(array, axis, bits):
    return lax.ppermute(array, axis, [(i, i ^ bits) for i in range(lax.axis_size(axis))])


def chunks_of(rows):
    units = rows // LANES
    sizes = SIZES if sum(SIZES) == units else [1] * units
    edges = [0]
    for size in sizes:
        edges.append(edges[-1] + size * LANES)
    return list(zip(edges[:-1], edges[1:]))


def local_kernel(kernel, out_shapes, place, *operands, order):
    def with_order(place_ref, *refs):
        kernel(place_ref, *refs[len(order) :])

    whole = pl.BlockSpec(memory_space=pltpu.VMEM)
    return pl.pallas_call(
        with_order,
        out_shape=[jax.ShapeDtypeStruct(shape, dtype) for shape, dtype in out_shapes],
        in_specs=[pl.BlockSpec(memory_space=pltpu.SMEM)]
        + [pl.BlockSpec(memory_space=pl.ANY)] * len(order)
        + [whole] * len(operands),
        out_specs=[whole] * len(out_shapes),
        compiler_params=pltpu.CompilerParams(vmem_limit_bytes=VMEM_BYTES),
        cost_estimate=pl.CostEstimate(flops=1, bytes_accessed=1, transcendentals=0),
    )(place, *order, *operands)


def flipped(place, bits):
    return 2 * (place[1] ^ (bits >> 1)) + (place[0] ^ (bits & 1))


def product(left, right):
    return lax.dot_general(
        left, right, (((0,), (0,)), ((), ())), preferred_element_type=jnp.float32
    )


def paired_body(
    activations,
    cotangent,
    island_weight,
    adam_first,
    adam_second,
    region_anchor,
    region_momentum,
    global_anchor,
    global_momentum,
):
    f32, bf16 = jnp.float32, jnp.bfloat16
    devs = lax.axis_size("dev")
    islands = lax.axis_size("island")
    regions = lax.axis_size("region")
    tokens, features = activations.shape
    width = cotangent.shape[1]
    half = width // regions
    rows = features // devs
    scale = 1.0 / math.sqrt(tokens * devs)
    me = lax.axis_index("dev")
    place = jnp.stack([me & 1, me >> 1, lax.axis_index("region")]).astype(jnp.int32)
    weight, first, second = island_weight[0, 0], adam_first[0, 0], adam_second[0, 0]
    anchor, momentum = region_anchor[0], region_momentum[0]
    pieces = chunks_of(rows)
    groups = groups_of(len(pieces))
    spans = [(pieces[members[0]][0], pieces[members[-1]][1]) for members in groups]
    group = [{} for _ in groups]
    bases = []
    token = [place]
    state = [{} for _ in pieces]

    def run(kernel, out_shapes, *operands, late=None):
        order = [token[0]]
        if late is not None:
            order.append(group[late]["held"][0])
        outs = local_kernel(kernel, out_shapes, place, *operands, order=order)
        token[0] = outs[0]
        return outs

    def columns(shard, start, size):
        return pl.ds(pl.multiple_of(shard * rows + start, LANES), size)

    def stage_message(k):
        start, stop = pieces[k]
        size = stop - start
        extra = width if k == 0 else 0

        def kernel(place_ref, *refs):
            a_ref, out_ref = refs[0], refs[-1]
            for i, bits in enumerate((1, 3)):
                at = columns(flipped(place_ref, bits), start, size)
                out_ref[:, i * size : (i + 1) * size] = a_ref[:, at]
            if extra:
                out_ref[:, 2 * size :] = refs[1][...]

        operands = (activations, cotangent) if extra else (activations,)
        (message,) = run(kernel, [((tokens, 2 * size + extra), bf16)], *operands)
        state[k]["raw"] = flip(message, "dev", 1)

    def stage_own(k):
        start, stop = pieces[k]
        size = stop - start

        def kernel(place_ref, a_ref, c_ref, kept_ref, away_ref):
            for bits, ref in ((0, kept_ref), (2, away_ref)):
                at = columns(flipped(place_ref, bits), start, size)
                ref[...] = product(a_ref[:, at], c_ref[...])

        state[k]["own"] = run(kernel, [((size, width), f32)] * 2, activations, cotangent)

    def partner_cotangent(first_ref):
        return first_ref[:, first_ref.shape[1] - width :]

    def stage_sums(k):
        start, stop = pieces[k]
        size = stop - start

        def kernel(place_ref, own_ref, raw_ref, *refs):
            first_ref = refs[0] if k else raw_ref
            out_ref = refs[-1]
            part = product(raw_ref[:, size : 2 * size], partner_cotangent(first_ref))
            out_ref[...] = (own_ref[...] + part).astype(bf16)

        operands = [state[k]["own"][1], state[k]["raw"]] + ([state[0]["raw"]] if k else [])
        (sums,) = run(kernel, [((size, width), bf16)], *operands)
        state[k]["sum"] = flip(sums, "dev", 2)

    def stage_bases(k):
        def kernel(place_ref, w_ref, r_ref, rm_ref, g_ref, gm_ref, delta_ref, gap_ref, new_ref):
            delta_ref[...] = r_ref[...] - (1.0 - inner_rate * weight_decay) * w_ref[...]
            _, params = regional(0.0, r_ref[...], rm_ref[...])
            gap_ref[...] = g_ref[...] - params
            _, new_ref[...] = outer(0.0, g_ref[...], gm_ref[...])

        bases[:] = run(
            kernel,
            [((rows, width), f32)] * 3,
            weight,
            anchor,
            momentum,
            global_anchor,
            global_momentum,
        )
        bases.append(flip(bases[1], "region", 1))

    def stage_adam(g):
        members = groups[g]
        start, stop = spans[g]
        size = stop - start

        def kernel(place_ref, m_ref, v_ref, base_ref, first_ref, *refs):
            delta_ref, gradient_ref = refs[-2:]
            for i, k in enumerate(members):
                low, high = pieces[k]
                count = high - low
                own_ref, raw_ref, sum_ref = refs[3 * i : 3 * i + 3]
                part = product(raw_ref[:, :count], partner_cotangent(first_ref))
                gradient = (own_ref[...] + part + sum_ref[...].astype(f32)) * scale
                span = pl.ds(low, count)
                first_new, second_new = moments(gradient, m_ref[span, :], v_ref[span, :])
                step = inner_rate * (first_new / (jnp.sqrt(second_new) + adam_eps))
                here = pl.ds(low - start, count)
                delta_ref[here, :] = (base_ref[span, :] + step).astype(bf16)
                gradient_ref[here, :] = gradient

        operands = [first, second, bases[0], state[0]["raw"]]
        for k in members:
            operands += [state[k]["own"][0], state[k]["raw"], state[k]["sum"]]
        delta, gradient = run(kernel, [((size, width), bf16), ((size, width), f32)], *operands)
        group[g].update(delta=delta, gradient=gradient, pair=halves(delta, (1, 2)))

    def halves(array, bits):
        middle = array.shape[0] // 2
        return [flip(array[:middle], "island", bits[0]), flip(array[middle:], "island", bits[1])]

    def summed(mine_ref, upper_ref, lower_ref):
        other = jnp.concatenate([upper_ref[...], lower_ref[...]], axis=0)
        return mine_ref[...].astype(f32) + other.astype(f32)

    def stage_pair(k):
        def kernel(place_ref, mine_ref, upper_ref, lower_ref, out_ref):
            out_ref[...] = summed(mine_ref, upper_ref, lower_ref).astype(bf16)

        (pair,) = run(
            kernel, [(group[k]["delta"].shape, bf16)], group[k]["delta"], *group[k]["pair"]
        )
        rest = halves(pair, (2, 1))
        group[k].update(mine=pair, rest=rest, mine2=flip(pair, "region", 1))
        group[k]["rest2"] = [flip(part, "region", 1) for part in rest]

    def stage_means(k):
        start, stop = spans[k]
        size = stop - start
        span = pl.ds(start, size)

        def kernel(place_ref, mine, up, low, mine2, up2, low2, base, base2, new, *outs):
            fresh_ref, share_ref, mean_ref, global_ref = outs
            gain = region_rate * (1.0 + region_mu)
            mean = summed(mine, up, low) / islands
            mean_ref[...] = mean
            gap = base[span, :] + gain * mean
            gap += base2[span, :] + gain * (summed(mine2, up2, low2) / islands)
            mean = gap / regions
            global_ref[...] = mean
            fresh = new[span, :] - global_rate * (1.0 + global_mu) * mean
            fresh_ref[...] = fresh.astype(bf16)
            at = pl.ds(pl.multiple_of(place_ref[2] * half, LANES), half)
            share_ref[...] = fresh_ref[:, at]

        this = group[k]
        fresh, share, mean, global_mean = run(
            kernel,
            [((size, width), bf16), ((size, half), bf16)] + [((size, width), f32)] * 2,
            this["mine"],
            *this["rest"],
            this["mine2"],
            *this["rest2"],
            bases[1],
            bases[3],
            bases[2],
        )
        held = [flip(share, "dev", bits) for bits in range(1, devs)]
        this.update(mean=mean, fresh=fresh, share=share, global_mean=global_mean, held=held)

    def left_columns(place_ref, a_ref, k):
        start, stop = spans[k]
        return [
            a_ref[:, columns(flipped(place_ref, bits), start, stop - start)]
            for bits in range(devs)
        ]

    def cuts_of(k):
        size = spans[k][1] - spans[k][0]
        cut = size * SHARE // 4
        return [(0, size)] if k == len(groups) - 1 else [(0, cut), (cut, size)]

    def stage_near(k):
        size = spans[k][1] - spans[k][0]
        cuts = cuts_of(k)

        def kernel(place_ref, a_ref, share_ref, *refs):
            held, outs, near_ref = refs[: devs - 1], refs[devs - 1 : -1], refs[-1]
            left = left_columns(place_ref, a_ref, k)
            for stack_ref, (low, high) in zip(outs, cuts):
                for i in range(devs - 1):
                    stack_ref[i] = held[i][low:high, :]
            value = jnp.dot(left[0], share_ref[...], preferred_element_type=f32)
            for bits in range(1, devs):
                value += jnp.dot(left[bits], held[bits - 1][...], preferred_element_type=f32)
            near_ref[...] = value

        *stacks, near = run(
            kernel,
            [((devs - 1, high - low, half), bf16) for low, high in cuts]
            + [((tokens, half), f32)],
            activations,
            group[k]["share"],
            *group[k]["held"],
        )
        group[k].update(near=near, swapped=[flip(stack, "region", 1) for stack in stacks])

    def stage_project(k):
        final = k == len(groups) - 1
        cuts = cuts_of(k)

        def kernel(place_ref, a_ref, fresh_ref, near_ref, *refs):
            swapped, out_ref = refs[: len(cuts)], refs[-1]
            left = left_columns(place_ref, a_ref, k)
            core = place_ref[2]
            near_at = pl.ds(pl.multiple_of(core * half, LANES), half)
            far_at = pl.ds(pl.multiple_of((1 - core) * half, LANES), half)
            far = jnp.dot(left[0], fresh_ref[:, far_at], preferred_element_type=f32)
            for bits in range(1, devs):
                right = [part[bits - 1] for part in swapped]
                right = jnp.concatenate(right, axis=0) if len(right) > 1 else right[0]
                far += jnp.dot(left[bits], right, preferred_element_type=f32)
            for value, at in ((near_ref[...], near_at), (far, far_at)):
                if k:
                    value = value + refs[len(cuts)][:, at]
                if final:
                    value = value * (1.0 / math.sqrt(features))
                out_ref[:, at] = value.astype(out_ref.dtype)

        operands = [activations, group[k]["fresh"], group[k]["near"], *group[k]["swapped"]]
        operands += [group[k - 1]["total"]] if k else []
        (total,) = run(kernel, [((tokens, width), bf16 if final else f32)], *operands)
        group[k]["total"] = total

    results = {}

    def stage_moments(k):
        def kernel(place_ref, m_ref, v_ref, *refs):
            for part, span in zip(refs, [pl.ds(low, high - low) for low, high in spans]):
                refs[-2][span, :], refs[-1][span, :] = moments(
                    part[...], m_ref[span, :], v_ref[span, :]
                )

        results["moments"] = run(
            kernel,
            [((rows, width), f32)] * 2,
            first,
            second,
            *[p["gradient"] for p in group],
            late=0,
        )

    def stage_velocity(k):
        def kernel(place_ref, m_ref, *refs):
            for part, span in zip(refs, [pl.ds(low, high - low) for low, high in spans]):
                refs[-1][span, :] = region_mu * m_ref[span, :] + part[...]

        results["velocity"] = run(
            kernel, [((rows, width), f32)], momentum, *[p["mean"] for p in group], late=-1
        )

    def stage_outer(k):
        def kernel(place_ref, g_ref, m_ref, *refs):
            for part, span in zip(refs, [pl.ds(low, high - low) for low, high in spans]):
                velocity, fresh = outer(part[...], g_ref[span, :], m_ref[span, :])
                refs[-2][span, :] = velocity
                refs[-1][span, :] = fresh

        results["outer"] = run(
            kernel,
            [((rows, width), f32)] * 2,
            global_anchor,
            global_momentum,
            *[p["global_mean"] for p in group],
        )

    stages = {
        "c": stage_message,
        "x": stage_own,
        "s": stage_sums,
        "b": stage_bases,
        "a": stage_adam,
        "p": stage_pair,
        "q": stage_means,
        "k": stage_near,
        "j": stage_project,
        "m": stage_moments,
        "v": stage_velocity,
        "o": stage_outer,
    }
    for step in plan_of(len(pieces), len(groups)):
        stages[step[0]](int(step[1:]))

    return (
        results["moments"][0][None, None],
        results["moments"][1][None, None],
        results["velocity"][0][None],
        results["outer"][0],
        results["outer"][1],
        group[-1]["total"],
    )


def groups_of(count):
    return GROUPS if count == len(SIZES) else [[k] for k in range(count)]


def plan_of(count, groups):
    if count == len(SIZES):
        return ORDER
    steps = ["c%d" % k for k in range(count)] + ["x%d" % k for k in range(count)]
    steps += ["s%d" % k for k in range(count)] + ["b0"]
    for letter in "apqkj":
        steps += [letter + "%d" % k for k in range(groups)]
    return steps + ["m0", "v0", "o0"]


def solution(mesh):
    devs, islands, regions = mesh.shape["dev"], mesh.shape["island"], mesh.shape["region"]
    aligned = DW % (devs * LANES) == 0
    paired = devs == 4 and islands == 4 and regions == 2 and aligned
    return jax.shard_map(
        paired_body if paired else generic_body,
        mesh=mesh,
        in_specs=(
            P(("region", "island", "dev"), None),
            P(("region", "island", "dev"), None),
            P("region", "island", "dev", None),
            P("region", "island", "dev", None),
            P("region", "island", "dev", None),
            P("region", "dev", None),
            P("region", "dev", None),
            P("dev", None),
            P("dev", None),
        ),
        out_specs=(
            P("region", "island", "dev", None),
            P("region", "island", "dev", None),
            P("region", "dev", None),
            P("dev", None),
            P("dev", None),
            P(("region", "island", "dev"), None),
        ),
        check_vma=False,
    )
```

time: 223 us -> 107 us (0.48)
  waiting for transfers between devices: 188 us -> 49.2 us
  starting transfers between devices: 0.16 us -> 27 us
  Pallas kernels: 0 us -> 23 us
  other arithmetic: 13.1 us -> 0.08 us
  between operations: 13.8 us -> 0.96 us
  matrix products: 5.96 us -> 0 us
  local copies, waits for them, and re-layouts: 2.12 us -> 6.87 us
    psum x2 -> x0, waiting for transfers between devices: 76.4 us -> none  [the longest x1 56.3 us: body(): island_total = lax.psum(island_delta, 'island')]
    all_gather x1 -> x0, waiting for transfers between devices: 56.1 us -> none  [body(): weight_full = lax.all_gather(weight_low, 'dev', axis=0, tiled=True)]
    reduce_scatter x1 -> x0, waiting for transfers between devices: 54.9 us -> none  [body(): lax.psum_scatter(lax.dot_general(activations, cotangent, (((0,), (0,)), (...]
    ppermute x0 -> x28, waiting for transfers between devices: none -> 49.2 us  [flip(): lax.ppermute(array, axis, [(i, i ^ bits) for i in range(lax.axis_size(axi...]
    ppermute x0 -> x28, starting transfers between devices: none -> 27 us  [flip(): lax.ppermute(array, axis, [(i, i ^ bits) for i in range(lax.axis_size(axi...]
    pallas_call x0 -> x20, Pallas kernels: none -> 23 us  [local_kernel(): pl.pallas_call(with_order, out_shape=[jax.ShapeDtypeStruct(shape, dtype)...]
    sub x2 -> x0, other arithmetic: 9.09 us -> none  [the longest x1 4.86 us: body(): island_delta = region_anchor[:, None] - inner]
    dot_general x2 -> x0, matrix products: 5.96 us -> none  [the longest x1 3.34 us: body(): lax.dot_general(activations, cotangent, (((0,), (0,)), ((), ())), preferr...]
  transfers between devices with their start and end apart: 4 -> 28, of which waited for: 4 -> 15; matrix products, arithmetic and copies ran while one was open for 0% -> 0% of each run, Pallas kernels for 0% -> 16%
where the time goes in v2:
time: 107 us
  waiting for transfers between devices  49.2 us (46%)
  starting transfers between devices  27 us (25%)
  Pallas kernels  23 us (21%)
  local copies, waits for them, and re-layouts  6.87 us (6%)
    ppermute x28, waiting for transfers between devices, flip(): lax.ppermute(array, axis, [(i, i ^ bits) for i in range(lax.axis_size(axi...  49.2 us
    ppermute x28, starting transfers between devices, flip(): lax.ppermute(array, axis, [(i, i ^ bits) for i in range(lax.axis_size(axi...  27 us
    pallas_call x20, Pallas kernels, local_kernel(): pl.pallas_call(with_order, out_shape=[jax.ShapeDtypeStruct(shape, dtype)...  23 us
    unnamed x28, local copies, waits for them, and re-layouts  6.78 us
  transfers between devices with their start and end apart: 28, of which 15 were waited for; matrix products, arithmetic and copies ran while one was open for 0% of the time, Pallas kernels for 16%

profile of v2, /device:TPU:0, one launch (start us, length us, event | category | flops | bytes accessed | tf_op | source)
XLA Modules:
  0.0 107.1 jit_solution(12424845814421023630)
XLA Ops:
  0.7 1.3 %copy-done = bf16[256,2560]{1,0:T(8,128)(2,1)S(1)} copy-done((bf16[256,2560]{1,0:T(8,128)(2,1)S(1)}, bf16[256,2560]{1,0:T(8,128)(2,1)}, u32[]{:S(2)}) %copy-start) | copy-done | bytes 1310744
  2.0 0.9 copy-done.8
  3.6 3.1 %collective-permute-start = (bf16[256,1024]{1,0:T(8,128)(2,1)S(1)}, bf16[256,1024]{1,0:T(8,128)(2,1)S(1)}, u32[]{:S(2)}, u32[]{:S(2)}) collective-permute-start(bf16[256,1024]{1,0:T(8,128)(2,1)S(1)} %shard_map.136.refs_0_), channel_id=1, source_target_pairs={{0,1},{1,0},{2,3},{3,2},{4,5},{5,4},{6,7},{7,6},{8,9},{9,8},{10,11... | collective-permute-start | bytes 1572872 | tf_op jit(solution)/shard_map/ppermute | solution.py:93
  7.3 0.9 shard_map.138
  8.2 0.9 shard_map.139
  9.7 1.2 %shard_map.140 = (f32[640,512]{1,0:T(8,128)S(1)}, f32[640,512]{1,0:T(8,128)S(1)}, f32[640,512]{1,0:T(8,128)S(1)}) custom-call(s32[3]{0:T(128)S(1)} %pad_add_fusion.place_ref.refs_0_, f32[384,512]{1,0:T(8,128)S(1)} %get-tuple-element.35.refs_0_.refs_5_, f32[640,512]{1,0:T(8,128)S(1)} %bitcast.21, f32[640,512]{1,0:T(8,128)S(1)} %bitcast.22, ...), custom_call_target="tpu_custom_call" | custom-call | flops 1 | bytes 1 | tf_op jit(solution)/shard_map/pallas_call | solution.py:110
  11.3 8.1 %collective-permute-done.refs_2_.refs_3_.refs_4_.refs_6_ = bf16[256,1024]{1,0:T(8,128)(2,1)S(1)} collective-permute-done((bf16[256,1024]{1,0:T(8,128)(2,1)S(1)}, bf16[256,1024]{1,0:T(8,128)(2,1)S(1)}, u32[]{:S(2)}, u32[]{:S(2)}) %collective-permute-start) | collective-permute-done | bytes 524320 | tf_op jit(solution)/shard_map/ppermute | solution.py:93
  19.4 0.8 shard_map.141.refs_0_
  20.2 3.1 %collective-permute-start.2 = (bf16[256,512]{1,0:T(8,128)(2,1)S(1)}, bf16[256,512]{1,0:T(8,128)(2,1)S(1)}, u32[]{:S(2)}, u32[]{:S(2)}) collective-permute-start(bf16[256,512]{1,0:T(8,128)(2,1)S(1)} %shard_map.141.refs_0_), channel_id=1, source_target_pairs={{0,2},{1,3},{2,0},{3,1},{4,6},{5,7},{6,4},{7,5},{8,10},{9,11},{10,... | collective-permute-start | bytes 786440 | tf_op jit(solution)/shard_map/ppermute | solution.py:93
  23.4 9.3 %collective-permute-done.1.refs_2_.refs_6_ = bf16[256,768]{1,0:T(8,128)(2,1)S(1)} collective-permute-done((bf16[256,768]{1,0:T(8,128)(2,1)S(1)}, bf16[256,768]{1,0:T(8,128)(2,1)S(1)}, u32[]{:S(2)}, u32[]{:S(2)}) %collective-permute-start.1) | collective-permute-done | bytes 393248 | tf_op jit(solution)/shard_map/ppermute | solution.py:93
  32.6 0.8 shard_map.142.refs_0_
  33.5 1.1 %shard_map.143 = (bf16[256,512]{1,0:T(8,128)(2,1)S(1)}, f32[256,512]{1,0:T(8,128)S(1)}) custom-call(s32[3]{0:T(128)S(1)} %pad_add_fusion.place_ref.refs_0_, bf16[384,512]{1,0:T(8,128)(2,1)S(1)} %shard_map.142.refs_0_, f32[640,512]{1,0:T(8,128)S(1)} %bitcast.11, f32[640,512]{1,0:T(8,128)S(1)} %bitcast.14, f32[640,512]{1,0:T(8,128)S(1)} %get-tuple-element.36.refs_0_.refs_3_, ...), custom_call_target="tpu_custom_call" | custom-call | flops 1 | bytes 1 | tf_op jit(solution)/shard_map/pallas_call | solution.py:110
  34.7 1.8 %collective-permute-start.4 = (bf16[128,512]{1,0:T(8,128)(2,1)S(1)}, bf16[128,512]{1,0:T(8,128)(2,1)S(1)}, u32[]{:S(2)}, u32[]{:S(2)}) collective-permute-start(bf16[128,512]{1,0:T(8,128)(2,1)S(1)} %get-tuple-element.68), channel_id=1, source_target_pairs={{0,8},{4,12},{8,0},{12,4},{1,9},{5,13},{9,1},{13,5},{2,10},{6,14},... | collective-permute-start | bytes 393224 | tf_op jit(solution)/shard_map/ppermute | solution.py:93
  36.4 1.5 %collective-permute-start.3 = (bf16[128,512]{1,0:T(8,128)(2,1)S(1)}, bf16[128,512]{1,0:T(8,128)(2,1)S(1)}, u32[]{:S(2)}, u32[]{:S(2)}) collective-permute-start(bf16[128,512]{1,0:T(8,128)(2,1)S(1)} %get-tuple-element.69), channel_id=1, source_target_pairs={{0,4},{4,0},{8,12},{12,8},{1,5},{5,1},{9,13},{13,9},{2,6},{6,2},{1... | collective-permute-start | bytes 393224 | tf_op jit(solution)/shard_map/ppermute | solution.py:93
  37.9 1.7 %collective-permute-start.11 = (bf16[384,512]{1,0:T(8,128)(2,1)S(1)}, bf16[384,512]{1,0:T(8,128)(2,1)S(1)}, u32[]{:S(2)}, u32[]{:S(2)}) collective-permute-start(bf16[384,512]{1,0:T(8,128)(2,1)S(1)} %shard_map.142.refs_0_), channel_id=1, source_target_pairs={{0,2},{1,3},{2,0},{3,1},{4,6},{5,7},{6,4},{7,5},{8,10},{9,11},{10,... | collective-permute-start | bytes 1179656 | tf_op jit(solution)/shard_map/ppermute | solution.py:93
  39.7 1.7 %collective-permute-done.3.refs_2_ = bf16[128,512]{1,0:T(8,128)(2,1)S(1)} collective-permute-done((bf16[128,512]{1,0:T(8,128)(2,1)S(1)}, bf16[128,512]{1,0:T(8,128)(2,1)S(1)}, u32[]{:S(2)}, u32[]{:S(2)}) %collective-permute-start.3) | collective-permute-done | bytes 131104 | tf_op jit(solution)/shard_map/ppermute | solution.py:93
  41.4 0.6 shard_map.144.refs_0_.refs_1_
  42.0 1.6 %collective-permute-start.6 = (bf16[128,512]{1,0:T(8,128)(2,1)S(1)}, bf16[128,512]{1,0:T(8,128)(2,1)S(1)}, u32[]{:S(2)}, u32[]{:S(2)}) collective-permute-start(bf16[128,512]{1,0:T(8,128)(2,1)S(1)} %get-tuple-element.66), channel_id=1, source_target_pairs={{0,4},{4,0},{8,12},{12,8},{1,5},{5,1},{9,13},{13,9},{2,6},{6,2},{1... | collective-permute-start | bytes 393224 | tf_op jit(solution)/shard_map/ppermute | solution.py:93
  44.1 3.0 %collective-permute-done.6.refs_3_ = bf16[128,512]{1,0:T(8,128)(2,1)S(1)} collective-permute-done((bf16[128,512]{1,0:T(8,128)(2,1)S(1)}, bf16[128,512]{1,0:T(8,128)(2,1)S(1)}, u32[]{:S(2)}, u32[]{:S(2)}) %collective-permute-start.6) | collective-permute-done | bytes 131104 | tf_op jit(solution)/shard_map/ppermute | solution.py:93
  47.1 1.5 %collective-permute-done.5.refs_2_ = bf16[128,512]{1,0:T(8,128)(2,1)S(1)} collective-permute-done((bf16[128,512]{1,0:T(8,128)(2,1)S(1)}, bf16[128,512]{1,0:T(8,128)(2,1)S(1)}, u32[]{:S(2)}, u32[]{:S(2)}) %collective-permute-start.5) | collective-permute-done | bytes 131104 | tf_op jit(solution)/shard_map/ppermute | solution.py:93
  48.6 1.3 %collective-permute-done.8.refs_5_ = bf16[128,512]{1,0:T(8,128)(2,1)S(1)} collective-permute-done((bf16[128,512]{1,0:T(8,128)(2,1)S(1)}, bf16[128,512]{1,0:T(8,128)(2,1)S(1)}, u32[]{:S(2)}, u32[]{:S(2)}) %collective-permute-start.8) | collective-permute-done | bytes 131104 | tf_op jit(solution)/shard_map/ppermute | solution.py:93
  49.9 1.1 %shard_map.145 = (bf16[256,512]{1,0:T(8,128)(2,1)S(1)}, bf16[256,256]{1,0:T(8,128)(2,1)S(1)}, f32[256,512]{1,0:T(8,128)S(1)}, f32[256,512]{1,0:T(8,128)S(1)}) custom-call(s32[3]{0:T(128)S(1)} %pad_add_fusion.place_ref.refs_0_, bf16[256,512]{1,0:T(8,128)(2,1)S(1)} %shard_map.144.refs_0_.refs_1_, bf16[256,512]{1,0:T(8,128)(2,1)S(1)} %shard_map.144.refs_0_.refs_1_, ...), custom_call_target="tpu_custom_call" | custom-call | flops 1 | bytes 1 | tf_op jit(solution)/shard_map/pallas_call | solution.py:110
  51.0 5.6 %collective-permute-done.11.refs_7_ = bf16[384,512]{1,0:T(8,128)(2,1)S(1)} collective-permute-done((bf16[384,512]{1,0:T(8,128)(2,1)S(1)}, bf16[384,512]{1,0:T(8,128)(2,1)S(1)}, u32[]{:S(2)}, u32[]{:S(2)}) %collective-permute-start.11) | collective-permute-done | bytes 393248 | tf_op jit(solution)/shard_map/ppermute | solution.py:93
  56.7 1.3 %shard_map.146 = (bf16[384,512]{1,0:T(8,128)(2,1)S(1)}, f32[384,512]{1,0:T(8,128)S(1)}) custom-call(s32[3]{0:T(128)S(1)} %pad_add_fusion.place_ref.refs_0_, bf16[256,512]{1,0:T(8,128)(2,1)S(1)} %get-tuple-element.42.refs_0_.refs_2_, f32[640,512]{1,0:T(8,128)S(1)} %bitcast.12, f32[640,512]{1,0:T(8,128)S(1)} %bitcast.15, ...), custom_call_target="tpu_custom_call" | custom-call | flops 1 | bytes 1 | tf_op jit(solution)/shard_map/pallas_call | solution.py:110
  58.6 0.7 collective-permute-start.12
  59.3 2.4 %collective-permute-start.16 = (bf16[256,256]{1,0:T(8,128)(2,1)S(1)}, bf16[256,256]{1,0:T(8,128)(2,1)S(1)}, u32[]{:S(2)}, u32[]{:S(2)}) collective-permute-start(bf16[256,256]{1,0:T(8,128)(2,1)S(1)} %get-tuple-element.44.refs_2_), channel_id=1, source_target_pairs={{0,3},{1,2},{2,1},{3,0},{4,7},{5,6},{6,5},{7,4},{8,11},{9,10},{10,... | collective-permute-start | bytes 393224 | tf_op jit(solution)/shard_map/ppermute | solution.py:93
  61.7 2.0 %collective-permute-start.14 = (bf16[256,256]{1,0:T(8,128)(2,1)S(1)}, bf16[256,256]{1,0:T(8,128)(2,1)S(1)}, u32[]{:S(2)}, u32[]{:S(2)}) collective-permute-start(bf16[256,256]{1,0:T(8,128)(2,1)S(1)} %get-tuple-element.44.refs_2_), channel_id=1, source_target_pairs={{0,1},{1,0},{2,3},{3,2},{4,5},{5,4},{6,7},{7,6},{8,9},{9,8},{10,11... | collective-permute-start | bytes 393224 | tf_op jit(solution)/shard_map/ppermute | solution.py:93
  64.3 0.6 shard_map.147.refs_0_.refs_1_
  64.9 0.8 collective-permute-start.20
  65.8 1.5 %collective-permute-start.19 = (bf16[192,512]{1,0:T(8,128)(2,1)S(1)}, bf16[192,512]{1,0:T(8,128)(2,1)S(1)}, u32[]{:S(2)}, u32[]{:S(2)}) collective-permute-start(bf16[192,512]{1,0:T(8,128)(2,1)S(1)} %get-tuple-element.63), channel_id=1, source_target_pairs={{0,8},{4,12},{8,0},{12,4},{1,9},{5,13},{9,1},{13,5},{2,10},{6,14},... | collective-permute-start | bytes 589832 | tf_op jit(solution)/shard_map/ppermute | solution.py:93
  67.3 2.5 %collective-permute-done.14.refs_1_.refs_3_ = bf16[256,256]{1,0:T(8,128)(2,1)S(1)} collective-permute-done((bf16[256,256]{1,0:T(8,128)(2,1)S(1)}, bf16[256,256]{1,0:T(8,128)(2,1)S(1)}, u32[]{:S(2)}, u32[]{:S(2)}) %collective-permute-start.14) | collective-permute-done | bytes 131104 | tf_op jit(solution)/shard_map/ppermute | solution.py:93
  69.7 2.4 %shard_map.148 = (f32[640,512]{1,0:T(8,128)}, f32[640,512]{1,0:T(8,128)}) custom-call(s32[3]{0:T(128)S(1)} %pad_add_fusion.place_ref.refs_0_, bf16[384,512]{1,0:T(8,128)(2,1)S(1)} %shard_map.147.refs_0_.refs_1_, bf16[256,256]{1,0:T(8,128)(2,1)S(1)} %collective-permute-done.14.refs_1_.refs_3_, f32[640,512]{1,0:T(8,128)S(1)} %bitcast.13, ...), custom_call_target="tpu_custom_call" | custom-call | flops 1 | bytes 1 | tf_op jit(solution)/shard_map/pallas_call | solution.py:110
  72.1 1.3 %copy-done.10 = f32[640,512]{1,0:T(8,128)S(1)} copy-done((f32[640,512]{1,0:T(8,128)S(1)}, f32[640,512]{1,0:T(8,128)}, u32[]{:S(2)}) %copy-start.10) | copy-done | bytes 1310744
  73.4 0.9 shard_map.149
  75.5 1.3 %collective-permute-done.18.refs_5_ = bf16[3,64,256]{2,1,0:T(8,128)(2,1)S(1)} collective-permute-done((bf16[3,64,256]{2,1,0:T(8,128)(2,1)S(1)}, bf16[3,64,256]{2,1,0:T(8,128)(2,1)S(1)}, u32[]{:S(2)}, u32[]{:S(2)}) %collective-permute-start.18) | collective-permute-done | bytes 98336 | tf_op jit(solution)/shard_map/ppermute | solution.py:93
  76.8 0.8 shard_map.150.refs_0_.refs_5_
  77.7 1.5 %shard_map.151 = (bf16[384,512]{1,0:T(8,128)(2,1)S(1)}, bf16[384,256]{1,0:T(8,128)(2,1)S(1)}, f32[384,512]{1,0:T(8,128)S(1)}, f32[384,512]{1,0:T(8,128)S(1)}) custom-call(s32[3]{0:T(128)S(1)} %pad_add_fusion.place_ref.refs_0_, f32[256,512]{1,0:T(8,128)S(1)} %shard_map.150.refs_0_.refs_5_, bf16[384,512]{1,0:T(8,128)(2,1)S(1)} %shard_map.147.refs_0_.refs_1_, ...), custom_call_target="tpu_custom_call" | custom-call | flops 1 | bytes 1 | tf_op jit(solution)/shard_map/pallas_call | solution.py:110
  79.2 2.6 %collective-permute-start.24 = (bf16[384,256]{1,0:T(8,128)(2,1)S(1)}, bf16[384,256]{1,0:T(8,128)(2,1)S(1)}, u32[]{:S(2)}, u32[]{:S(2)}) collective-permute-start(bf16[384,256]{1,0:T(8,128)(2,1)S(1)} %get-tuple-element.53.refs_2_), channel_id=1, source_target_pairs={{0,1},{1,0},{2,3},{3,2},{4,5},{5,4},{6,7},{7,6},{8,9},{9,8},{10,11... | collective-permute-start | bytes 589832 | tf_op jit(solution)/shard_map/ppermute | solution.py:93
  82.2 1.1 collective-permute-start.25
  83.3 3.9 %collective-permute-done.24.refs_1_.refs_3_ = bf16[384,256]{1,0:T(8,128)(2,1)S(1)} collective-permute-done((bf16[384,256]{1,0:T(8,128)(2,1)S(1)}, bf16[384,256]{1,0:T(8,128)(2,1)S(1)}, u32[]{:S(2)}, u32[]{:S(2)}) %collective-permute-start.24) | collective-permute-done | bytes 196640 | tf_op jit(solution)/shard_map/ppermute | solution.py:93
  87.2 1.7 %shard_map.152.refs_0_ = f32[640,512]{1,0:T(8,128)} custom-call(s32[3]{0:T(128)S(1)} %pad_add_fusion.place_ref.refs_0_, bf16[384,512]{1,0:T(8,128)(2,1)S(1)} %get-tuple-element.52.refs_0_.refs_2_, bf16[384,256]{1,0:T(8,128)(2,1)S(1)} %collective-permute-done.24.refs_1_.refs_3_, f32[640,512]{1,0:T(8,128)S(1)} %bitcast.19, ...), custom_call_target="tpu_custom_call" | custom-call | flops 1 | bytes 1 | tf_op jit(solution)/shard_map/pallas_call | solution.py:110
  88.9 1.3 %copy-done.4 = f32[640,512]{1,0:T(8,128)S(1)} copy-done((f32[640,512]{1,0:T(8,128)S(1)}, f32[640,512]{1,0:T(8,128)}, u32[]{:S(2)}) %copy-start.4) | copy-done | bytes 1310744
  90.2 2.4 %shard_map.153 = (f32[640,512]{1,0:T(8,128)}, f32[640,512]{1,0:T(8,128)}) custom-call(s32[3]{0:T(128)S(1)} %pad_add_fusion.place_ref.refs_0_, f32[640,512]{1,0:T(8,128)S(1)} %copy-done.4, f32[640,512]{1,0:T(8,128)S(1)} %copy-done.6, f32[640,512]{1,0:T(8,128)S(1)} %copy-done.7, f32[256,512]{1,0:T(8,128)S(1)} %get-tuple-element.56.refs_3_, ...), custom_call_target="tpu_custom_call" | custom-call | flops 1 | bytes 1 | tf_op jit(solution)/shard_map/pallas_call | solution.py:110
  92.6 8.4 %collective-permute-done.25.refs_4_ = bf16[384,256]{1,0:T(8,128)(2,1)S(1)} collective-permute-done((bf16[384,256]{1,0:T(8,128)(2,1)S(1)}, bf16[384,256]{1,0:T(8,128)(2,1)S(1)}, u32[]{:S(2)}, u32[]{:S(2)}) %collective-permute-start.25) | collective-permute-done | bytes 196640 | tf_op jit(solution)/shard_map/ppermute | solution.py:93
  101.0 1.3 %copy-done.11 = f32[640,512]{1,0:T(8,128)S(1)} copy-done((f32[640,512]{1,0:T(8,128)S(1)}, f32[640,512]{1,0:T(8,128)}, u32[]{:S(2)}) %copy-start.11) | copy-done | bytes 1310744
  102.4 1.0 shard_map.154
  103.5 2.0 %collective-permute-done.27.refs_4_ = bf16[3,384,256]{2,1,0:T(8,128)(2,1)S(1)} collective-permute-done((bf16[3,384,256]{2,1,0:T(8,128)(2,1)S(1)}, bf16[3,384,256]{2,1,0:T(8,128)(2,1)S(1)}, u32[]{:S(2)}, u32[]{:S(2)}) %collective-permute-start.27) | collective-permute-done | bytes 589856 | tf_op jit(solution)/shard_map/ppermute | solution.py:93
  105.4 1.7 %shard_map.155 = bf16[256,512]{1,0:T(8,128)(2,1)} custom-call(s32[3]{0:T(128)S(1)} %pad_add_fusion.place_ref.refs_0_, bf16[3,384,256]{2,1,0:T(8,128)(2,1)S(1)} %get-tuple-element.60.refs_0_, bf16[256,2560]{1,0:T(8,128)(2,1)S(1)} %copy-done.1, bf16[384,512]{1,0:T(8,128)(2,1)S(1)} %get-tuple-element.52.refs_0_.refs_2_, ...), custom_call_target="tpu_custom_call" | custom-call | flops 1 | bytes 1 | tf_op jit(solution)/shard_map/pallas_call | solution.py:110
  (61 shorter events, 5.8 us)
Async XLA Ops:
  0.7 1.3 %copy-start = (bf16[256,2560]{1,0:T(8,128)(2,1)S(1)}, bf16[256,2560]{1,0:T(8,128)(2,1)}, u32[]{:S(2)}) copy-start(bf16[256,2560]{1,0:T(8,128)(2,1)} %refs_1_.17) | copy-start | bytes 3932164
  2.0 0.9 copy-start.8
  3.0 6.2 %copy-start.13 = (f32[1,640,512]{2,1,0:T(8,128)S(1)}, f32[1,640,512]{2,1,0:T(8,128)}, u32[]{:S(2)}) copy-start(f32[1,640,512]{2,1,0:T(8,128)} %param.14) | copy-start | bytes 3932164
  3.6 3.7 %copy-start.9 = (bf16[256,512]{1,0:T(8,128)(2,1)S(1)}, bf16[256,512]{1,0:T(8,128)(2,1)}, u32[]{:S(2)}) copy-start(bf16[256,512]{1,0:T(8,128)(2,1)} %refs_2_.6) | copy-start | bytes 786436
  3.6 15.8 %collective-permute-start = (bf16[256,1024]{1,0:T(8,128)(2,1)S(1)}, bf16[256,1024]{1,0:T(8,128)(2,1)S(1)}, u32[]{:S(2)}, u32[]{:S(2)}) collective-permute-start(bf16[256,1024]{1,0:T(8,128)(2,1)S(1)} %shard_map.136.refs_0_), channel_id=1, source_target_pairs={{0,1},{1,0},{2,3},{3,2},{4,5},{5,4},{6,7},{7,6},{8,9},{9,8},{10,11... | collective-permute-start | bytes 1572872 | tf_op jit(solution)/shard_map/ppermute | solution.py:93
  6.7 2.5 %copy-start.12 = (f32[1,1,640,512]{3,2,1,0:T(8,128)S(1)}, f32[1,1,640,512]{3,2,1,0:T(8,128)}, u32[]{:S(2)}) copy-start(f32[1,1,640,512]{3,2,1,0:T(8,128)} %param.11) | copy-start | bytes 3932164
  7.3 1.9 %copy-start.6 = (f32[640,512]{1,0:T(8,128)S(1)}, f32[640,512]{1,0:T(8,128)}, u32[]{:S(2)}) copy-start(f32[640,512]{1,0:T(8,128)} %refs_1_.15) | copy-start | bytes 3932164
  7.3 1.9 %copy-start.7 = (f32[640,512]{1,0:T(8,128)S(1)}, f32[640,512]{1,0:T(8,128)}, u32[]{:S(2)}) copy-start(f32[640,512]{1,0:T(8,128)} %refs_2_.7) | copy-start | bytes 3932164
  8.2 1.5 %copy-start.5 = (f32[1,640,512]{2,1,0:T(8,128)S(1)}, f32[1,640,512]{2,1,0:T(8,128)}, u32[]{:S(2)}) copy-start(f32[1,640,512]{2,1,0:T(8,128)} %param.15) | copy-start | bytes 3932164
  10.9 39.0 %collective-permute-start.10 = (f32[640,512]{1,0:T(8,128)S(1)}, f32[640,512]{1,0:T(8,128)S(1)}, u32[]{:S(2)}, u32[]{:S(2)}) collective-permute-start(f32[640,512]{1,0:T(8,128)S(1)} %get-tuple-element.40.refs_7_), channel_id=1, source_target_pairs={{0,16},{16,0},{1,17},{17,1},{2,18},{18,2},{3,19},{19,3},{4,20},{20... | collective-permute-start | bytes 3932168 | tf_op jit(solution)/shard_map/ppermute | solution.py:93
  11.0 21.6 %collective-permute-start.1 = (bf16[256,768]{1,0:T(8,128)(2,1)S(1)}, bf16[256,768]{1,0:T(8,128)(2,1)S(1)}, u32[]{:S(2)}, u32[]{:S(2)}) collective-permute-start(bf16[256,768]{1,0:T(8,128)(2,1)S(1)} %shard_map.137.refs_0_), channel_id=1, source_target_pairs={{0,1},{1,0},{2,3},{3,2},{4,5},{5,4},{6,7},{7,6},{8,9},{9,8},{10,11... | collective-permute-start | bytes 1179656 | tf_op jit(solution)/shard_map/ppermute | solution.py:93
  19.4 14.1 %copy-start.3 = (f32[1,1,640,512]{3,2,1,0:T(8,128)S(1)}, f32[1,1,640,512]{3,2,1,0:T(8,128)}, u32[]{:S(2)}) copy-start(f32[1,1,640,512]{3,2,1,0:T(8,128)} %param.13) | copy-start | bytes 3932164
  20.2 13.3 %copy-start.2 = (f32[1,1,640,512]{3,2,1,0:T(8,128)S(1)}, f32[1,1,640,512]{3,2,1,0:T(8,128)}, u32[]{:S(2)}) copy-start(f32[1,1,640,512]{3,2,1,0:T(8,128)} %param.12) | copy-start | bytes 3932164
  20.2 13.2 %collective-permute-start.2 = (bf16[256,512]{1,0:T(8,128)(2,1)S(1)}, bf16[256,512]{1,0:T(8,128)(2,1)S(1)}, u32[]{:S(2)}, u32[]{:S(2)}) collective-permute-start(bf16[256,512]{1,0:T(8,128)(2,1)S(1)} %shard_map.141.refs_0_), channel_id=1, source_target_pairs={{0,2},{1,3},{2,0},{3,1},{4,6},{5,7},{6,4},{7,5},{8,10},{9,11},{10,... | collective-permute-start | bytes 786440 | tf_op jit(solution)/shard_map/ppermute | solution.py:93
  34.7 5.0 %collective-permute-start.4 = (bf16[128,512]{1,0:T(8,128)(2,1)S(1)}, bf16[128,512]{1,0:T(8,128)(2,1)S(1)}, u32[]{:S(2)}, u32[]{:S(2)}) collective-permute-start(bf16[128,512]{1,0:T(8,128)(2,1)S(1)} %get-tuple-element.68), channel_id=1, source_target_pairs={{0,8},{4,12},{8,0},{12,4},{1,9},{5,13},{9,1},{13,5},{2,10},{6,14},... | collective-permute-start | bytes 393224 | tf_op jit(solution)/shard_map/ppermute | solution.py:93
  36.4 5.0 %collective-permute-start.3 = (bf16[128,512]{1,0:T(8,128)(2,1)S(1)}, bf16[128,512]{1,0:T(8,128)(2,1)S(1)}, u32[]{:S(2)}, u32[]{:S(2)}) collective-permute-start(bf16[128,512]{1,0:T(8,128)(2,1)S(1)} %get-tuple-element.69), channel_id=1, source_target_pairs={{0,4},{4,0},{8,12},{12,8},{1,5},{5,1},{9,13},{13,9},{2,6},{6,2},{1... | collective-permute-start | bytes 393224 | tf_op jit(solution)/shard_map/ppermute | solution.py:93
  37.9 18.7 %collective-permute-start.11 = (bf16[384,512]{1,0:T(8,128)(2,1)S(1)}, bf16[384,512]{1,0:T(8,128)(2,1)S(1)}, u32[]{:S(2)}, u32[]{:S(2)}) collective-permute-start(bf16[384,512]{1,0:T(8,128)(2,1)S(1)} %shard_map.142.refs_0_), channel_id=1, source_target_pairs={{0,2},{1,3},{2,0},{3,1},{4,6},{5,7},{6,4},{7,5},{8,10},{9,11},{10,... | collective-permute-start | bytes 1179656 | tf_op jit(solution)/shard_map/ppermute | solution.py:93
  42.0 5.0 %collective-permute-start.6 = (bf16[128,512]{1,0:T(8,128)(2,1)S(1)}, bf16[128,512]{1,0:T(8,128)(2,1)S(1)}, u32[]{:S(2)}, u32[]{:S(2)}) collective-permute-start(bf16[128,512]{1,0:T(8,128)(2,1)S(1)} %get-tuple-element.66), channel_id=1, source_target_pairs={{0,4},{4,0},{8,12},{12,8},{1,5},{5,1},{9,13},{13,9},{2,6},{6,2},{1... | collective-permute-start | bytes 393224 | tf_op jit(solution)/shard_map/ppermute | solution.py:93
  43.6 5.0 %collective-permute-start.5 = (bf16[128,512]{1,0:T(8,128)(2,1)S(1)}, bf16[128,512]{1,0:T(8,128)(2,1)S(1)}, u32[]{:S(2)}, u32[]{:S(2)}) collective-permute-start(bf16[128,512]{1,0:T(8,128)(2,1)S(1)} %get-tuple-element.67), channel_id=1, source_target_pairs={{0,8},{4,12},{8,0},{12,4},{1,9},{5,13},{9,1},{13,5},{2,10},{6,14},... | collective-permute-start | bytes 393224 | tf_op jit(solution)/shard_map/ppermute | solution.py:93
  44.1 5.8 %collective-permute-start.7 = (bf16[256,512]{1,0:T(8,128)(2,1)S(1)}, bf16[256,512]{1,0:T(8,128)(2,1)S(1)}, u32[]{:S(2)}, u32[]{:S(2)}) collective-permute-start(bf16[256,512]{1,0:T(8,128)(2,1)S(1)} %shard_map.144.refs_0_.refs_1_), channel_id=1, source_target_pairs={{0,16},{16,0},{1,17},{17,1},{2,18},{18,2},{3,19},{19,3},{4,20},{20... | collective-permute-start | bytes 786440 | tf_op jit(solution)/shard_map/ppermute | solution.py:93
  47.1 1.5 %collective-permute-start.9 = (bf16[128,512]{1,0:T(8,128)(2,1)S(1)}, bf16[128,512]{1,0:T(8,128)(2,1)S(1)}, u32[]{:S(2)}, u32[]{:S(2)}) collective-permute-start(bf16[128,512]{1,0:T(8,128)(2,1)S(1)} %collective-permute-done.6.refs_3_), channel_id=1, source_target_pairs={{0,16},{16,0},{1,17},{17,1},{2,18},{18,2},{3,19},{19,3},{4,20},{20... | collective-permute-start | bytes 393224 | tf_op jit(solution)/shard_map/ppermute | solution.py:93
  48.6 1.3 %collective-permute-start.8 = (bf16[128,512]{1,0:T(8,128)(2,1)S(1)}, bf16[128,512]{1,0:T(8,128)(2,1)S(1)}, u32[]{:S(2)}, u32[]{:S(2)}) collective-permute-start(bf16[128,512]{1,0:T(8,128)(2,1)S(1)} %collective-permute-done.5.refs_2_), channel_id=1, source_target_pairs={{0,16},{16,0},{1,17},{17,1},{2,18},{18,2},{3,19},{19,3},{4,20},{20... | collective-permute-start | bytes 393224 | tf_op jit(solution)/shard_map/ppermute | solution.py:93
  58.0 5.7 %collective-permute-start.13 = (bf16[192,512]{1,0:T(8,128)(2,1)S(1)}, bf16[192,512]{1,0:T(8,128)(2,1)S(1)}, u32[]{:S(2)}, u32[]{:S(2)}) collective-permute-start(bf16[192,512]{1,0:T(8,128)(2,1)S(1)} %get-tuple-element.64), channel_id=1, source_target_pairs={{0,8},{4,12},{8,0},{12,4},{1,9},{5,13},{9,1},{13,5},{2,10},{6,14},... | collective-permute-start | bytes 589832 | tf_op jit(solution)/shard_map/ppermute | solution.py:93
  58.6 5.7 %collective-permute-start.12 = (bf16[192,512]{1,0:T(8,128)(2,1)S(1)}, bf16[192,512]{1,0:T(8,128)(2,1)S(1)}, u32[]{:S(2)}, u32[]{:S(2)}) collective-permute-start(bf16[192,512]{1,0:T(8,128)(2,1)S(1)} %get-tuple-element.65), channel_id=1, source_target_pairs={{0,4},{4,0},{8,12},{12,8},{1,5},{5,1},{9,13},{13,9},{2,6},{6,2},{1... | collective-permute-start | bytes 589832 | tf_op jit(solution)/shard_map/ppermute | solution.py:93
  59.3 12.8 %collective-permute-start.16 = (bf16[256,256]{1,0:T(8,128)(2,1)S(1)}, bf16[256,256]{1,0:T(8,128)(2,1)S(1)}, u32[]{:S(2)}, u32[]{:S(2)}) collective-permute-start(bf16[256,256]{1,0:T(8,128)(2,1)S(1)} %get-tuple-element.44.refs_2_), channel_id=1, source_target_pairs={{0,3},{1,2},{2,1},{3,0},{4,7},{5,6},{6,5},{7,4},{8,11},{9,10},{10,... | collective-permute-start | bytes 393224 | tf_op jit(solution)/shard_map/ppermute | solution.py:93
  61.7 10.4 %collective-permute-start.15 = (bf16[256,256]{1,0:T(8,128)(2,1)S(1)}, bf16[256,256]{1,0:T(8,128)(2,1)S(1)}, u32[]{:S(2)}, u32[]{:S(2)}) collective-permute-start(bf16[256,256]{1,0:T(8,128)(2,1)S(1)} %get-tuple-element.44.refs_2_), channel_id=1, source_target_pairs={{0,2},{1,3},{2,0},{3,1},{4,6},{5,7},{6,4},{7,5},{8,10},{9,11},{10,... | collective-permute-start | bytes 393224 | tf_op jit(solution)/shard_map/ppermute | solution.py:93
  61.7 8.0 %collective-permute-start.14 = (bf16[256,256]{1,0:T(8,128)(2,1)S(1)}, bf16[256,256]{1,0:T(8,128)(2,1)S(1)}, u32[]{:S(2)}, u32[]{:S(2)}) collective-permute-start(bf16[256,256]{1,0:T(8,128)(2,1)S(1)} %get-tuple-element.44.refs_2_), channel_id=1, source_target_pairs={{0,1},{1,0},{2,3},{3,2},{4,5},{5,4},{6,7},{7,6},{8,9},{9,8},{10,11... | collective-permute-start | bytes 393224 | tf_op jit(solution)/shard_map/ppermute | solution.py:93
  64.9 9.9 %collective-permute-start.20 = (bf16[192,512]{1,0:T(8,128)(2,1)S(1)}, bf16[192,512]{1,0:T(8,128)(2,1)S(1)}, u32[]{:S(2)}, u32[]{:S(2)}) collective-permute-start(bf16[192,512]{1,0:T(8,128)(2,1)S(1)} %get-tuple-element.62), channel_id=1, source_target_pairs={{0,4},{4,0},{8,12},{12,8},{1,5},{5,1},{9,13},{13,9},{2,6},{6,2},{1... | collective-permute-start | bytes 589832 | tf_op jit(solution)/shard_map/ppermute | solution.py:93
  65.8 9.2 %collective-permute-start.19 = (bf16[192,512]{1,0:T(8,128)(2,1)S(1)}, bf16[192,512]{1,0:T(8,128)(2,1)S(1)}, u32[]{:S(2)}, u32[]{:S(2)}) collective-permute-start(bf16[192,512]{1,0:T(8,128)(2,1)S(1)} %get-tuple-element.63), channel_id=1, source_target_pairs={{0,8},{4,12},{8,0},{12,4},{1,9},{5,13},{9,1},{13,5},{2,10},{6,14},... | collective-permute-start | bytes 589832 | tf_op jit(solution)/shard_map/ppermute | solution.py:93
  69.7 7.9 %collective-permute-start.21 = (bf16[384,512]{1,0:T(8,128)(2,1)S(1)}, bf16[384,512]{1,0:T(8,128)(2,1)S(1)}, u32[]{:S(2)}, u32[]{:S(2)}) collective-permute-start(bf16[384,512]{1,0:T(8,128)(2,1)S(1)} %shard_map.147.refs_0_.refs_1_), channel_id=1, source_target_pairs={{0,16},{16,0},{1,17},{17,1},{2,18},{18,2},{3,19},{19,3},{4,20},{20... | collective-permute-start | bytes 1179656 | tf_op jit(solution)/shard_map/ppermute | solution.py:93
  69.7 2.4 %copy-start.1 = (bf16[256,2560]{1,0:T(8,128)(2,1)S(1)}, bf16[256,2560]{1,0:T(8,128)(2,1)}, u32[]{:S(2)}) copy-start(bf16[256,2560]{1,0:T(8,128)(2,1)} %refs_1_.17) | copy-start | bytes 3932164
  72.1 1.3 %copy-start.10 = (f32[640,512]{1,0:T(8,128)S(1)}, f32[640,512]{1,0:T(8,128)}, u32[]{:S(2)}) copy-start(f32[640,512]{1,0:T(8,128)} %get-tuple-element.47.refs_0_) | copy-start | bytes 3932164
  74.3 2.5 %collective-permute-start.17 = (bf16[3,192,256]{2,1,0:T(8,128)(2,1)S(1)}, bf16[3,192,256]{2,1,0:T(8,128)(2,1)S(1)}, u32[]{:S(2)}, u32[]{:S(2)}) collective-permute-start(bf16[3,192,256]{2,1,0:T(8,128)(2,1)S(1)} %get-tuple-element.49.refs_0_), channel_id=1, source_target_pairs={{0,16},{16,0},{1,17},{17,1},{2,18},{18,2},{3,19},{19,3},{4,20},{20... | collective-permute-start | bytes 884744 | tf_op jit(solution)/shard_map/ppermute | solution.py:93
  74.9 2.8 %collective-permute-start.23 = (bf16[192,512]{1,0:T(8,128)(2,1)S(1)}, bf16[192,512]{1,0:T(8,128)(2,1)S(1)}, u32[]{:S(2)}, u32[]{:S(2)}) collective-permute-start(bf16[192,512]{1,0:T(8,128)(2,1)S(1)} %collective-permute-done.20.refs_3_), channel_id=1, source_target_pairs={{0,16},{16,0},{1,17},{17,1},{2,18},{18,2},{3,19},{19,3},{4,20},{20... | collective-permute-start | bytes 589832 | tf_op jit(solution)/shard_map/ppermute | solution.py:93
  75.0 2.7 %collective-permute-start.22 = (bf16[192,512]{1,0:T(8,128)(2,1)S(1)}, bf16[192,512]{1,0:T(8,128)(2,1)S(1)}, u32[]{:S(2)}, u32[]{:S(2)}) collective-permute-start(bf16[192,512]{1,0:T(8,128)(2,1)S(1)} %collective-permute-done.19.refs_2_), channel_id=1, source_target_pairs={{0,16},{16,0},{1,17},{17,1},{2,18},{18,2},{3,19},{19,3},{4,20},{20... | collective-permute-start | bytes 589832 | tf_op jit(solution)/shard_map/ppermute | solution.py:93
  75.4 1.4 %collective-permute-start.18 = (bf16[3,64,256]{2,1,0:T(8,128)(2,1)S(1)}, bf16[3,64,256]{2,1,0:T(8,128)(2,1)S(1)}, u32[]{:S(2)}, u32[]{:S(2)}) collective-permute-start(bf16[3,64,256]{2,1,0:T(8,128)(2,1)S(1)} %get-tuple-element.51), channel_id=1, source_target_pairs={{0,16},{16,0},{1,17},{17,1},{2,18},{18,2},{3,19},{19,3},{4,20},{20... | collective-permute-start | bytes 294920 | tf_op jit(solution)/shard_map/ppermute | solution.py:93
  79.2 8.0 %collective-permute-start.24 = (bf16[384,256]{1,0:T(8,128)(2,1)S(1)}, bf16[384,256]{1,0:T(8,128)(2,1)S(1)}, u32[]{:S(2)}, u32[]{:S(2)}) collective-permute-start(bf16[384,256]{1,0:T(8,128)(2,1)S(1)} %get-tuple-element.53.refs_2_), channel_id=1, source_target_pairs={{0,1},{1,0},{2,3},{3,2},{4,5},{5,4},{6,7},{7,6},{8,9},{9,8},{10,11... | collective-permute-start | bytes 589832 | tf_op jit(solution)/shard_map/ppermute | solution.py:93
  81.7 10.9 %collective-permute-start.26 = (bf16[384,256]{1,0:T(8,128)(2,1)S(1)}, bf16[384,256]{1,0:T(8,128)(2,1)S(1)}, u32[]{:S(2)}, u32[]{:S(2)}) collective-permute-start(bf16[384,256]{1,0:T(8,128)(2,1)S(1)} %get-tuple-element.53.refs_2_), channel_id=1, source_target_pairs={{0,3},{1,2},{2,1},{3,0},{4,7},{5,6},{6,5},{7,4},{8,11},{9,10},{10,... | collective-permute-start | bytes 589832 | tf_op jit(solution)/shard_map/ppermute | solution.py:93
  82.2 18.8 %collective-permute-start.25 = (bf16[384,256]{1,0:T(8,128)(2,1)S(1)}, bf16[384,256]{1,0:T(8,128)(2,1)S(1)}, u32[]{:S(2)}, u32[]{:S(2)}) collective-permute-start(bf16[384,256]{1,0:T(8,128)(2,1)S(1)} %get-tuple-element.53.refs_2_), channel_id=1, source_target_pairs={{0,2},{1,3},{2,0},{3,1},{4,6},{5,7},{6,4},{7,5},{8,10},{9,11},{10,... | collective-permute-start | bytes 589832 | tf_op jit(solution)/shard_map/ppermute | solution.py:93
  88.9 1.3 %copy-start.4 = (f32[640,512]{1,0:T(8,128)S(1)}, f32[640,512]{1,0:T(8,128)}, u32[]{:S(2)}) copy-start(f32[640,512]{1,0:T(8,128)} %shard_map.152.refs_0_) | copy-start | bytes 3932164
  101.0 1.3 %copy-start.11 = (f32[640,512]{1,0:T(8,128)S(1)}, f32[640,512]{1,0:T(8,128)}, u32[]{:S(2)}) copy-start(f32[640,512]{1,0:T(8,128)} %get-tuple-element.31.refs_0_) | copy-start | bytes 3932164
  103.4 2.1 %collective-permute-start.27 = (bf16[3,384,256]{2,1,0:T(8,128)(2,1)S(1)}, bf16[3,384,256]{2,1,0:T(8,128)(2,1)S(1)}, u32[]{:S(2)}, u32[]{:S(2)}) collective-permute-start(bf16[3,384,256]{2,1,0:T(8,128)(2,1)S(1)} %get-tuple-element.60.refs_0_), channel_id=1, source_target_pairs={{0,16},{16,0},{1,17},{17,1},{2,18},{18,2},{3,19},{19,3},{4,20},{20... | collective-permute-start | bytes 1769480 | tf_op jit(solution)/shard_map/ppermute | solution.py:93

commit v3 on v2

--- a/solution.py
+++ b/solution.py
@@ -12,8 +12,8 @@
 VMEM_BYTES = 16 * 2**20
 SIZES = [2, 3]
 GROUPS = [[0], [1]]
-SHARE = 3
-ORDER = ("c0", "c1", "x0", "x1", "b0", "s0", "s1", "a0", "p0", "q0", "a1", "p1", "m1", "k0", "j0", "q1", "v1", "o1", "k1", "j1")
+SHARES = (3 / 4, 1.0)
+ORDER = ("c0", "c1", "x0", "x1", "b0", "s0", "s1", "a0", "p0", "q0", "a1", "p1", "k0", "j0", "q1", "v1", "y1", "o1", "m1", "k1", "j1")
 
 
 beta_first = 0.9
@@ -161,10 +161,21 @@
     token = [place]
     state = [{} for _ in pieces]
 
-    def run(kernel, out_shapes, *operands, late=None):
+    def run(kernel, out_shapes, *operands, late=None, mark=False):
         order = [token[0]]
         if late is not None:
             order.append(group[late]["held"][0])
+        if mark:
+
+            def marked(place_ref, *refs):
+                kernel(place_ref, *refs[:-1])
+                refs[-1][...] = jnp.zeros_like(refs[-1])
+
+            small = (8, LANES)
+            *outs, token[0] = local_kernel(
+                marked, [*out_shapes, (small, f32)], place, *operands, order=order
+            )
+            return outs
         outs = local_kernel(kernel, out_shapes, place, *operands, order=order)
         token[0] = outs[0]
         return outs
@@ -311,8 +322,18 @@
             bases[3],
             bases[2],
         )
-        held = [flip(share, "dev", bits) for bits in range(1, devs)]
+        held = [flip(share, "dev", 1), flip(share, "dev", 2)]
+        if k < len(groups) - 1:
+            held.append(flip(share, "dev", 3))
         this.update(mean=mean, fresh=fresh, share=share, global_mean=global_mean, held=held)
+
+    def stage_relay(k):
+        def kernel(place_ref, block_ref, out_ref):
+            out_ref[...] = block_ref[...]
+
+        block = group[k]["held"][1]
+        (block,) = run(kernel, [(block.shape, bf16)], block)
+        group[k]["held"].append(flip(block, "dev", 1))
 
     def left_columns(place_ref, a_ref, k):
         start, stop = spans[k]
@@ -323,52 +344,62 @@
 
     def cuts_of(k):
         size = spans[k][1] - spans[k][0]
-        cut = size * SHARE // 4
-        return [(0, size)] if k == len(groups) - 1 else [(0, cut), (cut, size)]
+        if k == len(groups) - 1:
+            return []
+        shares = SHARES
+        edges = [0] + [round(size * share / 16) * 16 for share in shares]
+        return list(zip(edges[:-1], edges[1:]))
 
     def stage_near(k):
         size = spans[k][1] - spans[k][0]
         cuts = cuts_of(k)
 
         def kernel(place_ref, a_ref, share_ref, *refs):
-            held, outs, near_ref = refs[: devs - 1], refs[devs - 1 : -1], refs[-1]
+            held, near_ref, outs = refs[: devs - 1], refs[devs - 1], refs[devs:]
             left = left_columns(place_ref, a_ref, k)
             for stack_ref, (low, high) in zip(outs, cuts):
                 for i in range(devs - 1):
                     stack_ref[i] = held[i][low:high, :]
+            if not cuts:
+                outs[0][...] = held[-1][...]
             value = jnp.dot(left[0], share_ref[...], preferred_element_type=f32)
             for bits in range(1, devs):
                 value += jnp.dot(left[bits], held[bits - 1][...], preferred_element_type=f32)
             near_ref[...] = value
 
-        *stacks, near = run(
+        near, *stacks = run(
             kernel,
-            [((devs - 1, high - low, half), bf16) for low, high in cuts]
-            + [((tokens, half), f32)],
+            [((tokens, half), f32)]
+            + [((devs - 1, high - low, half), bf16) for low, high in cuts]
+            + ([] if cuts else [((size, half), bf16)]),
             activations,
             group[k]["share"],
             *group[k]["held"],
         )
-        group[k].update(near=near, swapped=[flip(stack, "region", 1) for stack in stacks])
+        blocks = stacks if cuts else group[k]["held"][:-1] + stacks
+        group[k].update(near=near, swapped=[flip(block, "region", 1) for block in blocks])
 
     def stage_project(k):
         final = k == len(groups) - 1
         cuts = cuts_of(k)
+        count = len(cuts) or devs - 1
 
         def kernel(place_ref, a_ref, fresh_ref, near_ref, *refs):
-            swapped, out_ref = refs[: len(cuts)], refs[-1]
+            swapped, out_ref = refs[:count], refs[-1]
             left = left_columns(place_ref, a_ref, k)
             core = place_ref[2]
             near_at = pl.ds(pl.multiple_of(core * half, LANES), half)
             far_at = pl.ds(pl.multiple_of((1 - core) * half, LANES), half)
             far = jnp.dot(left[0], fresh_ref[:, far_at], preferred_element_type=f32)
             for bits in range(1, devs):
-                right = [part[bits - 1] for part in swapped]
-                right = jnp.concatenate(right, axis=0) if len(right) > 1 else right[0]
+                if cuts:
+                    right = jnp.concatenate([part[bits - 1] for part in swapped], axis=0)
+                else:
+                    right = swapped[bits - 1][...]
                 far += jnp.dot(left[bits], right, preferred_element_type=f32)
             for value, at in ((near_ref[...], near_at), (far, far_at)):
                 if k:
-                    value = value + refs[len(cuts)][:, at]
+                    value = value + refs[count][:, at]
                 if final:
                     value = value * (1.0 / math.sqrt(features))
                 out_ref[:, at] = value.astype(out_ref.dtype)
@@ -393,7 +424,7 @@
             first,
             second,
             *[p["gradient"] for p in group],
-            late=0,
+            mark=True,
         )
 
     def stage_velocity(k):
@@ -402,7 +433,7 @@
                 refs[-1][span, :] = region_mu * m_ref[span, :] + part[...]
 
         results["velocity"] = run(
-            kernel, [((rows, width), f32)], momentum, *[p["mean"] for p in group], late=-1
+            kernel, [((rows, width), f32)], momentum, *[p["mean"] for p in group], late=-1, mark=True
         )
 
     def stage_outer(k):
@@ -418,6 +449,7 @@
             global_anchor,
             global_momentum,
             *[p["global_mean"] for p in group],
+            mark=True,
         )
 
     stages = {
@@ -428,6 +460,7 @@
         "a": stage_adam,
         "p": stage_pair,
         "q": stage_means,
+        "y": stage_relay,
         "k": stage_near,
         "j": stage_project,
         "m": stage_moments,
@@ -456,9 +489,12 @@
         return ORDER
     steps = ["c%d" % k for k in range(count)] + ["x%d" % k for k in range(count)]
     steps += ["s%d" % k for k in range(count)] + ["b0"]
-    for letter in "apqkj":
+    for letter in "apq":
         steps += [letter + "%d" % k for k in range(groups)]
-    return steps + ["m0", "v0", "o0"]
+    steps += ["v0", "o0", "m0", "y%d" % (groups - 1)]
+    for letter in "kj":
+        steps += [letter + "%d" % k for k in range(groups)]
+    return steps
 
 
 def solution(mesh):

time: 107 us -> 101 us (0.944)
  local copies, waits for them, and re-layouts: 6.87 us -> 2.93 us
  waiting for transfers between devices: 49.2 us -> 47.4 us
  starting transfers between devices: 27 us -> 25.4 us
    unnamed x28 -> x22, local copies, waits for them, and re-layouts: 6.78 us -> 2.84 us
    ppermute x28 -> x30, waiting for transfers between devices: 49.2 us -> 47.4 us  [flip(): lax.ppermute(array, axis, [(i, i ^ bits) for i in range(lax.axis_size(axi...]
    ppermute x28 -> x30, starting transfers between devices: 27 us -> 25.4 us  [flip(): lax.ppermute(array, axis, [(i, i ^ bits) for i in range(lax.axis_size(axi...]
    pallas_call x20 -> x21, Pallas kernels: 23 us -> 23.6 us  [local_kernel(): pl.pallas_call(with_order, out_shape=[jax.ShapeDtypeStruct(shape, dtype)...]
  transfers between devices with their start and end apart: 28 -> 30, of which waited for: 15 -> 16; matrix products, arithmetic and copies ran while one was open for 0% -> 0% of each run, Pallas kernels for 16% -> 18%
where the time goes in v3:
time: 101 us; the launch traced here: 100 us
  waiting for transfers between devices  47.4 us (47%)
  starting transfers between devices  25.4 us (25%)
  Pallas kernels  23.6 us (23%)
  local copies, waits for them, and re-layouts  2.93 us (3%)
    ppermute x30, waiting for transfers between devices, flip(): lax.ppermute(array, axis, [(i, i ^ bits) for i in range(lax.axis_size(axi...  47.4 us
    ppermute x30, starting transfers between devices, flip(): lax.ppermute(array, axis, [(i, i ^ bits) for i in range(lax.axis_size(axi...  25.4 us
    pallas_call x21, Pallas kernels, local_kernel(): pl.pallas_call(with_order, out_shape=[jax.ShapeDtypeStruct(shape, dtype)...  23.6 us
    unnamed x22, local copies, waits for them, and re-layouts  2.84 us
  transfers between devices with their start and end apart: 30, of which 16 were waited for; matrix products, arithmetic and copies ran while one was open for 0% of the time, Pallas kernels for 18%

profile of v3, /device:TPU:0, one launch (start us, length us, event | category | flops | bytes accessed | tf_op | source)
XLA Modules:
  0.0 100.4 jit_solution(1384715081487562348)
XLA Ops:
  0.7 1.3 %copy-done = bf16[256,2560]{1,0:T(8,128)(2,1)S(1)} copy-done((bf16[256,2560]{1,0:T(8,128)(2,1)S(1)}, bf16[256,2560]{1,0:T(8,128)(2,1)}, u32[]{:S(2)}) %copy-start) | copy-done | bytes 1310744
  2.0 0.9 copy-done.7
  3.0 0.6 shard_map.136.refs_0_
  3.6 3.1 %collective-permute-start = (bf16[256,1024]{1,0:T(8,128)(2,1)S(1)}, bf16[256,1024]{1,0:T(8,128)(2,1)S(1)}, u32[]{:S(2)}, u32[]{:S(2)}) collective-permute-start(bf16[256,1024]{1,0:T(8,128)(2,1)S(1)} %shard_map.136.refs_0_), channel_id=1, source_target_pairs={{0,1},{1,0},{2,3},{3,2},{4,5},{5,4},{6,7},{7,6},{8,9},{9,8},{10,11... | collective-permute-start | bytes 1572872 | tf_op jit(solution)/shard_map/ppermute | solution.py:93
  6.7 0.6 shard_map.137.refs_0_
  7.3 0.9 shard_map.138
  8.2 0.9 shard_map.139
  9.7 1.2 %shard_map.140 = (f32[640,512]{1,0:T(8,128)S(1)}, f32[640,512]{1,0:T(8,128)S(1)}, f32[640,512]{1,0:T(8,128)S(1)}) custom-call(s32[3]{0:T(128)S(1)} %pad_add_fusion.place_ref.refs_0_, f32[384,512]{1,0:T(8,128)S(1)} %get-tuple-element.39.refs_0_.refs_5_, f32[640,512]{1,0:T(8,128)S(1)} %bitcast.19, f32[640,512]{1,0:T(8,128)S(1)} %bitcast.20, ...), custom_call_target="tpu_custom_call" | custom-call | flops 1 | bytes 1 | tf_op jit(solution)/shard_map/pallas_call | solution.py:110
  11.3 8.1 %collective-permute-done.refs_2_.refs_3_.refs_4_.refs_6_ = bf16[256,1024]{1,0:T(8,128)(2,1)S(1)} collective-permute-done((bf16[256,1024]{1,0:T(8,128)(2,1)S(1)}, bf16[256,1024]{1,0:T(8,128)(2,1)S(1)}, u32[]{:S(2)}, u32[]{:S(2)}) %collective-permute-start) | collective-permute-done | bytes 524320 | tf_op jit(solution)/shard_map/ppermute | solution.py:93
  19.4 0.8 shard_map.141.refs_0_
  20.2 3.1 %collective-permute-start.2 = (bf16[256,512]{1,0:T(8,128)(2,1)S(1)}, bf16[256,512]{1,0:T(8,128)(2,1)S(1)}, u32[]{:S(2)}, u32[]{:S(2)}) collective-permute-start(bf16[256,512]{1,0:T(8,128)(2,1)S(1)} %shard_map.141.refs_0_), channel_id=1, source_target_pairs={{0,2},{1,3},{2,0},{3,1},{4,6},{5,7},{6,4},{7,5},{8,10},{9,11},{10,... | collective-permute-start | bytes 786440 | tf_op jit(solution)/shard_map/ppermute | solution.py:93
  23.4 9.3 %collective-permute-done.1.refs_2_.refs_6_ = bf16[256,768]{1,0:T(8,128)(2,1)S(1)} collective-permute-done((bf16[256,768]{1,0:T(8,128)(2,1)S(1)}, bf16[256,768]{1,0:T(8,128)(2,1)S(1)}, u32[]{:S(2)}, u32[]{:S(2)}) %collective-permute-start.1) | collective-permute-done | bytes 393248 | tf_op jit(solution)/shard_map/ppermute | solution.py:93
  32.6 0.8 shard_map.142.refs_0_
  33.5 1.1 %shard_map.143 = (bf16[256,512]{1,0:T(8,128)(2,1)S(1)}, f32[256,512]{1,0:T(8,128)S(1)}) custom-call(s32[3]{0:T(128)S(1)} %pad_add_fusion.place_ref.refs_0_, bf16[384,512]{1,0:T(8,128)(2,1)S(1)} %shard_map.142.refs_0_, f32[640,512]{1,0:T(8,128)S(1)} %bitcast.11, f32[640,512]{1,0:T(8,128)S(1)} %bitcast.14, f32[640,512]{1,0:T(8,128)S(1)} %get-tuple-element.40.refs_0_.refs_3_, ...), custom_call_target="tpu_custom_call" | custom-call | flops 1 | bytes 1 | tf_op jit(solution)/shard_map/pallas_call | solution.py:110
  34.7 1.8 %collective-permute-start.4 = (bf16[128,512]{1,0:T(8,128)(2,1)S(1)}, bf16[128,512]{1,0:T(8,128)(2,1)S(1)}, u32[]{:S(2)}, u32[]{:S(2)}) collective-permute-start(bf16[128,512]{1,0:T(8,128)(2,1)S(1)} %get-tuple-element.76), channel_id=1, source_target_pairs={{0,8},{4,12},{8,0},{12,4},{1,9},{5,13},{9,1},{13,5},{2,10},{6,14},... | collective-permute-start | bytes 393224 | tf_op jit(solution)/shard_map/ppermute | solution.py:93
  36.4 1.5 %collective-permute-start.3 = (bf16[128,512]{1,0:T(8,128)(2,1)S(1)}, bf16[128,512]{1,0:T(8,128)(2,1)S(1)}, u32[]{:S(2)}, u32[]{:S(2)}) collective-permute-start(bf16[128,512]{1,0:T(8,128)(2,1)S(1)} %get-tuple-element.77), channel_id=1, source_target_pairs={{0,4},{4,0},{8,12},{12,8},{1,5},{5,1},{9,13},{13,9},{2,6},{6,2},{1... | collective-permute-start | bytes 393224 | tf_op jit(solution)/shard_map/ppermute | solution.py:93
  37.9 1.7 %collective-permute-start.11 = (bf16[384,512]{1,0:T(8,128)(2,1)S(1)}, bf16[384,512]{1,0:T(8,128)(2,1)S(1)}, u32[]{:S(2)}, u32[]{:S(2)}) collective-permute-start(bf16[384,512]{1,0:T(8,128)(2,1)S(1)} %shard_map.142.refs_0_), channel_id=1, source_target_pairs={{0,2},{1,3},{2,0},{3,1},{4,6},{5,7},{6,4},{7,5},{8,10},{9,11},{10,... | collective-permute-start | bytes 1179656 | tf_op jit(solution)/shard_map/ppermute | solution.py:93
  39.7 1.7 %collective-permute-done.3.refs_2_ = bf16[128,512]{1,0:T(8,128)(2,1)S(1)} collective-permute-done((bf16[128,512]{1,0:T(8,128)(2,1)S(1)}, bf16[128,512]{1,0:T(8,128)(2,1)S(1)}, u32[]{:S(2)}, u32[]{:S(2)}) %collective-permute-start.3) | collective-permute-done | bytes 131104 | tf_op jit(solution)/shard_map/ppermute | solution.py:93
  41.4 0.6 shard_map.144.refs_0_.refs_1_
  42.0 1.6 %collective-permute-start.6 = (bf16[128,512]{1,0:T(8,128)(2,1)S(1)}, bf16[128,512]{1,0:T(8,128)(2,1)S(1)}, u32[]{:S(2)}, u32[]{:S(2)}) collective-permute-start(bf16[128,512]{1,0:T(8,128)(2,1)S(1)} %get-tuple-element.74), channel_id=1, source_target_pairs={{0,4},{4,0},{8,12},{12,8},{1,5},{5,1},{9,13},{13,9},{2,6},{6,2},{1... | collective-permute-start | bytes 393224 | tf_op jit(solution)/shard_map/ppermute | solution.py:93
  44.1 3.0 %collective-permute-done.6.refs_3_ = bf16[128,512]{1,0:T(8,128)(2,1)S(1)} collective-permute-done((bf16[128,512]{1,0:T(8,128)(2,1)S(1)}, bf16[128,512]{1,0:T(8,128)(2,1)S(1)}, u32[]{:S(2)}, u32[]{:S(2)}) %collective-permute-start.6) | collective-permute-done | bytes 131104 | tf_op jit(solution)/shard_map/ppermute | solution.py:93
  47.1 1.5 %collective-permute-done.5.refs_2_ = bf16[128,512]{1,0:T(8,128)(2,1)S(1)} collective-permute-done((bf16[128,512]{1,0:T(8,128)(2,1)S(1)}, bf16[128,512]{1,0:T(8,128)(2,1)S(1)}, u32[]{:S(2)}, u32[]{:S(2)}) %collective-permute-start.5) | collective-permute-done | bytes 131104 | tf_op jit(solution)/shard_map/ppermute | solution.py:93
  48.6 1.3 %collective-permute-done.8.refs_5_ = bf16[128,512]{1,0:T(8,128)(2,1)S(1)} collective-permute-done((bf16[128,512]{1,0:T(8,128)(2,1)S(1)}, bf16[128,512]{1,0:T(8,128)(2,1)S(1)}, u32[]{:S(2)}, u32[]{:S(2)}) %collective-permute-start.8) | collective-permute-done | bytes 131104 | tf_op jit(solution)/shard_map/ppermute | solution.py:93
  49.9 1.1 %shard_map.145 = (bf16[256,512]{1,0:T(8,128)(2,1)S(1)}, bf16[256,256]{1,0:T(8,128)(2,1)S(1)}, f32[256,512]{1,0:T(8,128)S(1)}, f32[256,512]{1,0:T(8,128)S(1)}) custom-call(s32[3]{0:T(128)S(1)} %pad_add_fusion.place_ref.refs_0_, bf16[256,512]{1,0:T(8,128)(2,1)S(1)} %shard_map.144.refs_0_.refs_1_, bf16[256,512]{1,0:T(8,128)(2,1)S(1)} %shard_map.144.refs_0_.refs_1_, ...), custom_call_target="tpu_custom_call" | custom-call | flops 1 | bytes 1 | tf_op jit(solution)/shard_map/pallas_call | solution.py:110
  51.0 5.6 %collective-permute-done.11.refs_7_ = bf16[384,512]{1,0:T(8,128)(2,1)S(1)} collective-permute-done((bf16[384,512]{1,0:T(8,128)(2,1)S(1)}, bf16[384,512]{1,0:T(8,128)(2,1)S(1)}, u32[]{:S(2)}, u32[]{:S(2)}) %collective-permute-start.11) | collective-permute-done | bytes 393248 | tf_op jit(solution)/shard_map/ppermute | solution.py:93
  56.7 1.3 %shard_map.146 = (bf16[384,512]{1,0:T(8,128)(2,1)S(1)}, f32[384,512]{1,0:T(8,128)S(1)}) custom-call(s32[3]{0:T(128)S(1)} %pad_add_fusion.place_ref.refs_0_, bf16[256,512]{1,0:T(8,128)(2,1)S(1)} %get-tuple-element.46.refs_0_.refs_2_, f32[640,512]{1,0:T(8,128)S(1)} %bitcast.12, f32[640,512]{1,0:T(8,128)S(1)} %bitcast.15, ...), custom_call_target="tpu_custom_call" | custom-call | flops 1 | bytes 1 | tf_op jit(solution)/shard_map/pallas_call | solution.py:110
  58.0 0.6 collective-permute-start.13
  58.6 0.7 collective-permute-start.12
  59.3 2.4 %collective-permute-start.16 = (bf16[256,256]{1,0:T(8,128)(2,1)S(1)}, bf16[256,256]{1,0:T(8,128)(2,1)S(1)}, u32[]{:S(2)}, u32[]{:S(2)}) collective-permute-start(bf16[256,256]{1,0:T(8,128)(2,1)S(1)} %get-tuple-element.48.refs_2_), channel_id=1, source_target_pairs={{0,3},{1,2},{2,1},{3,0},{4,7},{5,6},{6,5},{7,4},{8,11},{9,10},{10,... | collective-permute-start | bytes 393224 | tf_op jit(solution)/shard_map/ppermute | solution.py:93
  61.7 2.0 %collective-permute-start.14 = (bf16[256,256]{1,0:T(8,128)(2,1)S(1)}, bf16[256,256]{1,0:T(8,128)(2,1)S(1)}, u32[]{:S(2)}, u32[]{:S(2)}) collective-permute-start(bf16[256,256]{1,0:T(8,128)(2,1)S(1)} %get-tuple-element.48.refs_2_), channel_id=1, source_target_pairs={{0,1},{1,0},{2,3},{3,2},{4,5},{5,4},{6,7},{7,6},{8,9},{9,8},{10,11... | collective-permute-start | bytes 393224 | tf_op jit(solution)/shard_map/ppermute | solution.py:93
  64.3 0.6 shard_map.147.refs_0_.refs_1_
  65.0 0.8 collective-permute-start.20
  65.8 1.5 %collective-permute-start.19 = (bf16[192,512]{1,0:T(8,128)(2,1)S(1)}, bf16[192,512]{1,0:T(8,128)(2,1)S(1)}, u32[]{:S(2)}, u32[]{:S(2)}) collective-permute-start(bf16[192,512]{1,0:T(8,128)(2,1)S(1)} %get-tuple-element.71), channel_id=1, source_target_pairs={{0,8},{4,12},{8,0},{12,4},{1,9},{5,13},{9,1},{13,5},{2,10},{6,14},... | collective-permute-start | bytes 589832 | tf_op jit(solution)/shard_map/ppermute | solution.py:93
  67.3 4.4 %collective-permute-done.15.refs_4_ = bf16[256,256]{1,0:T(8,128)(2,1)S(1)} collective-permute-done((bf16[256,256]{1,0:T(8,128)(2,1)S(1)}, bf16[256,256]{1,0:T(8,128)(2,1)S(1)}, u32[]{:S(2)}, u32[]{:S(2)}) %collective-permute-start.15) | collective-permute-done | bytes 131104 | tf_op jit(solution)/shard_map/ppermute | solution.py:93
  71.7 0.9 shard_map.148
  73.7 1.3 %collective-permute-done.18.refs_5_ = bf16[3,64,256]{2,1,0:T(8,128)(2,1)S(1)} collective-permute-done((bf16[3,64,256]{2,1,0:T(8,128)(2,1)S(1)}, bf16[3,64,256]{2,1,0:T(8,128)(2,1)S(1)}, u32[]{:S(2)}, u32[]{:S(2)}) %collective-permute-start.18) | collective-permute-done | bytes 98336 | tf_op jit(solution)/shard_map/ppermute | solution.py:93
  74.9 0.8 shard_map.149.refs_0_.refs_7_
  75.8 1.5 %shard_map.150 = (bf16[384,512]{1,0:T(8,128)(2,1)S(1)}, bf16[384,256]{1,0:T(8,128)(2,1)S(1)}, f32[384,512]{1,0:T(8,128)S(1)}, f32[384,512]{1,0:T(8,128)S(1)}) custom-call(s32[3]{0:T(128)S(1)} %pad_add_fusion.place_ref.refs_0_, f32[256,512]{1,0:T(8,128)S(1)} %shard_map.149.refs_0_.refs_7_, bf16[384,512]{1,0:T(8,128)(2,1)S(1)} %shard_map.147.refs_0_.refs_1_, ...), custom_call_target="tpu_custom_call" | custom-call | flops 1 | bytes 1 | tf_op jit(solution)/shard_map/pallas_call | solution.py:110
  77.3 0.6 collective-permute-start.24
  77.9 1.5 %collective-permute-start.25 = (bf16[384,256]{1,0:T(8,128)(2,1)S(1)}, bf16[384,256]{1,0:T(8,128)(2,1)S(1)}, u32[]{:S(2)}, u32[]{:S(2)}) collective-permute-start(bf16[384,256]{1,0:T(8,128)(2,1)S(1)} %get-tuple-element.53.refs_2_), channel_id=1, source_target_pairs={{0,2},{1,3},{2,0},{3,1},{4,6},{5,7},{6,4},{7,5},{8,10},{9,11},{10,... | collective-permute-start | bytes 589832 | tf_op jit(solution)/shard_map/ppermute | solution.py:93
  79.4 7.8 %collective-permute-done.24.refs_1_.refs_3_ = bf16[384,256]{1,0:T(8,128)(2,1)S(1)} collective-permute-done((bf16[384,256]{1,0:T(8,128)(2,1)S(1)}, bf16[384,256]{1,0:T(8,128)(2,1)S(1)}, u32[]{:S(2)}, u32[]{:S(2)}) %collective-permute-start.24) | collective-permute-done | bytes 196640 | tf_op jit(solution)/shard_map/ppermute | solution.py:93
  87.2 1.7 %shard_map.151 = (f32[640,512]{1,0:T(8,128)}, f32[8,128]{1,0:T(8,128)S(1)}) custom-call(s32[3]{0:T(128)S(1)} %pad_add_fusion.place_ref.refs_0_, bf16[384,512]{1,0:T(8,128)(2,1)S(1)} %get-tuple-element.52.refs_0_.refs_2_, bf16[384,256]{1,0:T(8,128)(2,1)S(1)} %collective-permute-done.24.refs_1_.refs_3_, f32[640,512]{1,0:T(8,128)S(1)} %bitcast.18, ...), custom_call_target="tpu_custom_call" | custom-call | flops 1 | bytes 1 | tf_op jit(solution)/shard_map/pallas_call | solution.py:110
  88.9 0.8 collective-permute-done.25.refs_1_.refs_4_
  90.4 2.4 %shard_map.153 = (f32[640,512]{1,0:T(8,128)}, f32[640,512]{1,0:T(8,128)}, f32[8,128]{1,0:T(8,128)S(1)}) custom-call(s32[3]{0:T(128)S(1)} %pad_add_fusion.place_ref.refs_0_, bf16[384,256]{1,0:T(8,128)(2,1)S(1)} %shard_map.152.refs_0_, f32[640,512]{1,0:T(8,128)S(1)} %copy-done.5, f32[640,512]{1,0:T(8,128)S(1)} %copy-done.6, ...), custom_call_target="tpu_custom_call" | custom-call | flops 1 | bytes 1 | tf_op jit(solution)/shard_map/pallas_call | solution.py:110
  92.8 2.4 %shard_map.154 = (f32[640,512]{1,0:T(8,128)}, f32[640,512]{1,0:T(8,128)}, f32[8,128]{1,0:T(8,128)S(1)}) custom-call(s32[3]{0:T(128)S(1)} %pad_add_fusion.place_ref.refs_0_, f32[8,128]{1,0:T(8,128)S(1)} %get-tuple-element.59.refs_0_, f32[640,512]{1,0:T(8,128)S(1)} %bitcast.13, f32[640,512]{1,0:T(8,128)S(1)} %bitcast.16, ...), custom_call_target="tpu_custom_call" | custom-call | flops 1 | bytes 1 | tf_op jit(solution)/shard_map/pallas_call | solution.py:110
  96.2 1.0 shard_map.155
  97.3 1.4 %collective-permute-done.29.refs_6_ = bf16[384,256]{1,0:T(8,128)(2,1)S(1)} collective-permute-done((bf16[384,256]{1,0:T(8,128)(2,1)S(1)}, bf16[384,256]{1,0:T(8,128)(2,1)S(1)}, u32[]{:S(2)}, u32[]{:S(2)}) %collective-permute-start.29) | collective-permute-done | bytes 196640 | tf_op jit(solution)/shard_map/ppermute | solution.py:93
  98.7 1.7 %shard_map.156 = bf16[256,512]{1,0:T(8,128)(2,1)} custom-call(s32[3]{0:T(128)S(1)} %pad_add_fusion.place_ref.refs_0_, f32[256,256]{1,0:T(8,128)S(1)} %get-tuple-element.68.refs_0_.refs_3_, bf16[256,2560]{1,0:T(8,128)(2,1)S(1)} %copy-done.1, bf16[384,512]{1,0:T(8,128)(2,1)S(1)} %get-tuple-element.52.refs_0_.refs_2_, ...), custom_call_target="tpu_custom_call" | custom-call | flops 1 | bytes 1 | tf_op jit(solution)/shard_map/pallas_call | solution.py:110
  (60 shorter events, 5.2 us)
Async XLA Ops:
  0.7 1.3 %copy-start = (bf16[256,2560]{1,0:T(8,128)(2,1)S(1)}, bf16[256,2560]{1,0:T(8,128)(2,1)}, u32[]{:S(2)}) copy-start(bf16[256,2560]{1,0:T(8,128)(2,1)} %refs_1_.17) | copy-start | bytes 3932164
  2.0 0.9 copy-start.7
  3.0 6.2 %copy-start.10 = (f32[1,640,512]{2,1,0:T(8,128)S(1)}, f32[1,640,512]{2,1,0:T(8,128)}, u32[]{:S(2)}) copy-start(f32[1,640,512]{2,1,0:T(8,128)} %param.14) | copy-start | bytes 3932164
  3.6 3.7 %copy-start.8 = (bf16[256,512]{1,0:T(8,128)(2,1)S(1)}, bf16[256,512]{1,0:T(8,128)(2,1)}, u32[]{:S(2)}) copy-start(bf16[256,512]{1,0:T(8,128)(2,1)} %refs_2_.6) | copy-start | bytes 786436
  3.6 15.8 %collective-permute-start = (bf16[256,1024]{1,0:T(8,128)(2,1)S(1)}, bf16[256,1024]{1,0:T(8,128)(2,1)S(1)}, u32[]{:S(2)}, u32[]{:S(2)}) collective-permute-start(bf16[256,1024]{1,0:T(8,128)(2,1)S(1)} %shard_map.136.refs_0_), channel_id=1, source_target_pairs={{0,1},{1,0},{2,3},{3,2},{4,5},{5,4},{6,7},{7,6},{8,9},{9,8},{10,11... | collective-permute-start | bytes 1572872 | tf_op jit(solution)/shard_map/ppermute | solution.py:93
  6.7 2.5 %copy-start.9 = (f32[1,1,640,512]{3,2,1,0:T(8,128)S(1)}, f32[1,1,640,512]{3,2,1,0:T(8,128)}, u32[]{:S(2)}) copy-start(f32[1,1,640,512]{3,2,1,0:T(8,128)} %param.11) | copy-start | bytes 3932164
  7.3 1.9 %copy-start.5 = (f32[640,512]{1,0:T(8,128)S(1)}, f32[640,512]{1,0:T(8,128)}, u32[]{:S(2)}) copy-start(f32[640,512]{1,0:T(8,128)} %refs_1_.15) | copy-start | bytes 3932164
  7.3 1.9 %copy-start.6 = (f32[640,512]{1,0:T(8,128)S(1)}, f32[640,512]{1,0:T(8,128)}, u32[]{:S(2)}) copy-start(f32[640,512]{1,0:T(8,128)} %refs_2_.7) | copy-start | bytes 3932164
  8.2 1.5 %copy-start.4 = (f32[1,640,512]{2,1,0:T(8,128)S(1)}, f32[1,640,512]{2,1,0:T(8,128)}, u32[]{:S(2)}) copy-start(f32[1,640,512]{2,1,0:T(8,128)} %param.15) | copy-start | bytes 3932164
  10.9 39.0 %collective-permute-start.10 = (f32[640,512]{1,0:T(8,128)S(1)}, f32[640,512]{1,0:T(8,128)S(1)}, u32[]{:S(2)}, u32[]{:S(2)}) collective-permute-start(f32[640,512]{1,0:T(8,128)S(1)} %get-tuple-element.44.refs_7_), channel_id=1, source_target_pairs={{0,16},{16,0},{1,17},{17,1},{2,18},{18,2},{3,19},{19,3},{4,20},{20... | collective-permute-start | bytes 3932168 | tf_op jit(solution)/shard_map/ppermute | solution.py:93
  11.0 21.6 %collective-permute-start.1 = (bf16[256,768]{1,0:T(8,128)(2,1)S(1)}, bf16[256,768]{1,0:T(8,128)(2,1)S(1)}, u32[]{:S(2)}, u32[]{:S(2)}) collective-permute-start(bf16[256,768]{1,0:T(8,128)(2,1)S(1)} %shard_map.137.refs_0_), channel_id=1, source_target_pairs={{0,1},{1,0},{2,3},{3,2},{4,5},{5,4},{6,7},{7,6},{8,9},{9,8},{10,11... | collective-permute-start | bytes 1179656 | tf_op jit(solution)/shard_map/ppermute | solution.py:93
  19.4 14.1 %copy-start.3 = (f32[1,1,640,512]{3,2,1,0:T(8,128)S(1)}, f32[1,1,640,512]{3,2,1,0:T(8,128)}, u32[]{:S(2)}) copy-start(f32[1,1,640,512]{3,2,1,0:T(8,128)} %param.13) | copy-start | bytes 3932164
  20.2 13.3 %copy-start.2 = (f32[1,1,640,512]{3,2,1,0:T(8,128)S(1)}, f32[1,1,640,512]{3,2,1,0:T(8,128)}, u32[]{:S(2)}) copy-start(f32[1,1,640,512]{3,2,1,0:T(8,128)} %param.12) | copy-start | bytes 3932164
  20.2 13.2 %collective-permute-start.2 = (bf16[256,512]{1,0:T(8,128)(2,1)S(1)}, bf16[256,512]{1,0:T(8,128)(2,1)S(1)}, u32[]{:S(2)}, u32[]{:S(2)}) collective-permute-start(bf16[256,512]{1,0:T(8,128)(2,1)S(1)} %shard_map.141.refs_0_), channel_id=1, source_target_pairs={{0,2},{1,3},{2,0},{3,1},{4,6},{5,7},{6,4},{7,5},{8,10},{9,11},{10,... | collective-permute-start | bytes 786440 | tf_op jit(solution)/shard_map/ppermute | solution.py:93
  34.7 5.0 %collective-permute-start.4 = (bf16[128,512]{1,0:T(8,128)(2,1)S(1)}, bf16[128,512]{1,0:T(8,128)(2,1)S(1)}, u32[]{:S(2)}, u32[]{:S(2)}) collective-permute-start(bf16[128,512]{1,0:T(8,128)(2,1)S(1)} %get-tuple-element.76), channel_id=1, source_target_pairs={{0,8},{4,12},{8,0},{12,4},{1,9},{5,13},{9,1},{13,5},{2,10},{6,14},... | collective-permute-start | bytes 393224 | tf_op jit(solution)/shard_map/ppermute | solution.py:93
  36.4 5.0 %collective-permute-start.3 = (bf16[128,512]{1,0:T(8,128)(2,1)S(1)}, bf16[128,512]{1,0:T(8,128)(2,1)S(1)}, u32[]{:S(2)}, u32[]{:S(2)}) collective-permute-start(bf16[128,512]{1,0:T(8,128)(2,1)S(1)} %get-tuple-element.77), channel_id=1, source_target_pairs={{0,4},{4,0},{8,12},{12,8},{1,5},{5,1},{9,13},{13,9},{2,6},{6,2},{1... | collective-permute-start | bytes 393224 | tf_op jit(solution)/shard_map/ppermute | solution.py:93
  37.9 18.7 %collective-permute-start.11 = (bf16[384,512]{1,0:T(8,128)(2,1)S(1)}, bf16[384,512]{1,0:T(8,128)(2,1)S(1)}, u32[]{:S(2)}, u32[]{:S(2)}) collective-permute-start(bf16[384,512]{1,0:T(8,128)(2,1)S(1)} %shard_map.142.refs_0_), channel_id=1, source_target_pairs={{0,2},{1,3},{2,0},{3,1},{4,6},{5,7},{6,4},{7,5},{8,10},{9,11},{10,... | collective-permute-start | bytes 1179656 | tf_op jit(solution)/shard_map/ppermute | solution.py:93
  42.0 5.0 %collective-permute-start.6 = (bf16[128,512]{1,0:T(8,128)(2,1)S(1)}, bf16[128,512]{1,0:T(8,128)(2,1)S(1)}, u32[]{:S(2)}, u32[]{:S(2)}) collective-permute-start(bf16[128,512]{1,0:T(8,128)(2,1)S(1)} %get-tuple-element.74), channel_id=1, source_target_pairs={{0,4},{4,0},{8,12},{12,8},{1,5},{5,1},{9,13},{13,9},{2,6},{6,2},{1... | collective-permute-start | bytes 393224 | tf_op jit(solution)/shard_map/ppermute | solution.py:93
  43.6 5.0 %collective-permute-start.5 = (bf16[128,512]{1,0:T(8,128)(2,1)S(1)}, bf16[128,512]{1,0:T(8,128)(2,1)S(1)}, u32[]{:S(2)}, u32[]{:S(2)}) collective-permute-start(bf16[128,512]{1,0:T(8,128)(2,1)S(1)} %get-tuple-element.75), channel_id=1, source_target_pairs={{0,8},{4,12},{8,0},{12,4},{1,9},{5,13},{9,1},{13,5},{2,10},{6,14},... | collective-permute-start | bytes 393224 | tf_op jit(solution)/shard_map/ppermute | solution.py:93
  44.1 5.8 %collective-permute-start.7 = (bf16[256,512]{1,0:T(8,128)(2,1)S(1)}, bf16[256,512]{1,0:T(8,128)(2,1)S(1)}, u32[]{:S(2)}, u32[]{:S(2)}) collective-permute-start(bf16[256,512]{1,0:T(8,128)(2,1)S(1)} %shard_map.144.refs_0_.refs_1_), channel_id=1, source_target_pairs={{0,16},{16,0},{1,17},{17,1},{2,18},{18,2},{3,19},{19,3},{4,20},{20... | collective-permute-start | bytes 786440 | tf_op jit(solution)/shard_map/ppermute | solution.py:93
  47.1 1.5 %collective-permute-start.9 = (bf16[128,512]{1,0:T(8,128)(2,1)S(1)}, bf16[128,512]{1,0:T(8,128)(2,1)S(1)}, u32[]{:S(2)}, u32[]{:S(2)}) collective-permute-start(bf16[128,512]{1,0:T(8,128)(2,1)S(1)} %collective-permute-done.6.refs_3_), channel_id=1, source_target_pairs={{0,16},{16,0},{1,17},{17,1},{2,18},{18,2},{3,19},{19,3},{4,20},{20... | collective-permute-start | bytes 393224 | tf_op jit(solution)/shard_map/ppermute | solution.py:93
  48.6 1.3 %collective-permute-start.8 = (bf16[128,512]{1,0:T(8,128)(2,1)S(1)}, bf16[128,512]{1,0:T(8,128)(2,1)S(1)}, u32[]{:S(2)}, u32[]{:S(2)}) collective-permute-start(bf16[128,512]{1,0:T(8,128)(2,1)S(1)} %collective-permute-done.5.refs_2_), channel_id=1, source_target_pairs={{0,16},{16,0},{1,17},{17,1},{2,18},{18,2},{3,19},{19,3},{4,20},{20... | collective-permute-start | bytes 393224 | tf_op jit(solution)/shard_map/ppermute | solution.py:93
  58.0 13.7 %copy-start.1 = (bf16[256,2560]{1,0:T(8,128)(2,1)S(1)}, bf16[256,2560]{1,0:T(8,128)(2,1)}, u32[]{:S(2)}) copy-start(bf16[256,2560]{1,0:T(8,128)(2,1)} %refs_1_.17) | copy-start | bytes 3932164
  58.0 5.7 %collective-permute-start.13 = (bf16[192,512]{1,0:T(8,128)(2,1)S(1)}, bf16[192,512]{1,0:T(8,128)(2,1)S(1)}, u32[]{:S(2)}, u32[]{:S(2)}) collective-permute-start(bf16[192,512]{1,0:T(8,128)(2,1)S(1)} %get-tuple-element.72), channel_id=1, source_target_pairs={{0,8},{4,12},{8,0},{12,4},{1,9},{5,13},{9,1},{13,5},{2,10},{6,14},... | collective-permute-start | bytes 589832 | tf_op jit(solution)/shard_map/ppermute | solution.py:93
  58.6 5.7 %collective-permute-start.12 = (bf16[192,512]{1,0:T(8,128)(2,1)S(1)}, bf16[192,512]{1,0:T(8,128)(2,1)S(1)}, u32[]{:S(2)}, u32[]{:S(2)}) collective-permute-start(bf16[192,512]{1,0:T(8,128)(2,1)S(1)} %get-tuple-element.73), channel_id=1, source_target_pairs={{0,4},{4,0},{8,12},{12,8},{1,5},{5,1},{9,13},{13,9},{2,6},{6,2},{1... | collective-permute-start | bytes 589832 | tf_op jit(solution)/shard_map/ppermute | solution.py:93
  59.3 8.0 %collective-permute-start.16 = (bf16[256,256]{1,0:T(8,128)(2,1)S(1)}, bf16[256,256]{1,0:T(8,128)(2,1)S(1)}, u32[]{:S(2)}, u32[]{:S(2)}) collective-permute-start(bf16[256,256]{1,0:T(8,128)(2,1)S(1)} %get-tuple-element.48.refs_2_), channel_id=1, source_target_pairs={{0,3},{1,2},{2,1},{3,0},{4,7},{5,6},{6,5},{7,4},{8,11},{9,10},{10,... | collective-permute-start | bytes 393224 | tf_op jit(solution)/shard_map/ppermute | solution.py:93
  61.7 10.0 %collective-permute-start.15 = (bf16[256,256]{1,0:T(8,128)(2,1)S(1)}, bf16[256,256]{1,0:T(8,128)(2,1)S(1)}, u32[]{:S(2)}, u32[]{:S(2)}) collective-permute-start(bf16[256,256]{1,0:T(8,128)(2,1)S(1)} %get-tuple-element.48.refs_2_), channel_id=1, source_target_pairs={{0,2},{1,3},{2,0},{3,1},{4,6},{5,7},{6,4},{7,5},{8,10},{9,11},{10,... | collective-permute-start | bytes 393224 | tf_op jit(solution)/shard_map/ppermute | solution.py:93
  61.7 10.0 %collective-permute-start.14 = (bf16[256,256]{1,0:T(8,128)(2,1)S(1)}, bf16[256,256]{1,0:T(8,128)(2,1)S(1)}, u32[]{:S(2)}, u32[]{:S(2)}) collective-permute-start(bf16[256,256]{1,0:T(8,128)(2,1)S(1)} %get-tuple-element.48.refs_2_), channel_id=1, source_target_pairs={{0,1},{1,0},{2,3},{3,2},{4,5},{5,4},{6,7},{7,6},{8,9},{9,8},{10,11... | collective-permute-start | bytes 393224 | tf_op jit(solution)/shard_map/ppermute | solution.py:93
  65.0 7.7 %collective-permute-start.20 = (bf16[192,512]{1,0:T(8,128)(2,1)S(1)}, bf16[192,512]{1,0:T(8,128)(2,1)S(1)}, u32[]{:S(2)}, u32[]{:S(2)}) collective-permute-start(bf16[192,512]{1,0:T(8,128)(2,1)S(1)} %get-tuple-element.70), channel_id=1, source_target_pairs={{0,4},{4,0},{8,12},{12,8},{1,5},{5,1},{9,13},{13,9},{2,6},{6,2},{1... | collective-permute-start | bytes 589832 | tf_op jit(solution)/shard_map/ppermute | solution.py:93
  65.8 7.4 %collective-permute-start.19 = (bf16[192,512]{1,0:T(8,128)(2,1)S(1)}, bf16[192,512]{1,0:T(8,128)(2,1)S(1)}, u32[]{:S(2)}, u32[]{:S(2)}) collective-permute-start(bf16[192,512]{1,0:T(8,128)(2,1)S(1)} %get-tuple-element.71), channel_id=1, source_target_pairs={{0,8},{4,12},{8,0},{12,4},{1,9},{5,13},{9,1},{13,5},{2,10},{6,14},... | collective-permute-start | bytes 589832 | tf_op jit(solution)/shard_map/ppermute | solution.py:93
  67.3 8.5 %collective-permute-start.21 = (bf16[384,512]{1,0:T(8,128)(2,1)S(1)}, bf16[384,512]{1,0:T(8,128)(2,1)S(1)}, u32[]{:S(2)}, u32[]{:S(2)}) collective-permute-start(bf16[384,512]{1,0:T(8,128)(2,1)S(1)} %shard_map.147.refs_0_.refs_1_), channel_id=1, source_target_pairs={{0,16},{16,0},{1,17},{17,1},{2,18},{18,2},{3,19},{19,3},{4,20},{20... | collective-permute-start | bytes 1179656 | tf_op jit(solution)/shard_map/ppermute | solution.py:93
  72.6 2.4 %collective-permute-start.17 = (bf16[3,192,256]{2,1,0:T(8,128)(2,1)S(1)}, bf16[3,192,256]{2,1,0:T(8,128)(2,1)S(1)}, u32[]{:S(2)}, u32[]{:S(2)}) collective-permute-start(bf16[3,192,256]{2,1,0:T(8,128)(2,1)S(1)} %get-tuple-element.50), channel_id=1, source_target_pairs={{0,16},{16,0},{1,17},{17,1},{2,18},{18,2},{3,19},{19,3},{4,20},{20... | collective-permute-start | bytes 884744 | tf_op jit(solution)/shard_map/ppermute | solution.py:93
  72.7 3.1 %collective-permute-start.23 = (bf16[192,512]{1,0:T(8,128)(2,1)S(1)}, bf16[192,512]{1,0:T(8,128)(2,1)S(1)}, u32[]{:S(2)}, u32[]{:S(2)}) collective-permute-start(bf16[192,512]{1,0:T(8,128)(2,1)S(1)} %collective-permute-done.20.refs_3_), channel_id=1, source_target_pairs={{0,16},{16,0},{1,17},{17,1},{2,18},{18,2},{3,19},{19,3},{4,20},{20... | collective-permute-start | bytes 589832 | tf_op jit(solution)/shard_map/ppermute | solution.py:93
  73.2 2.6 %collective-permute-start.22 = (bf16[192,512]{1,0:T(8,128)(2,1)S(1)}, bf16[192,512]{1,0:T(8,128)(2,1)S(1)}, u32[]{:S(2)}, u32[]{:S(2)}) collective-permute-start(bf16[192,512]{1,0:T(8,128)(2,1)S(1)} %collective-permute-done.19.refs_2_), channel_id=1, source_target_pairs={{0,16},{16,0},{1,17},{17,1},{2,18},{18,2},{3,19},{19,3},{4,20},{20... | collective-permute-start | bytes 589832 | tf_op jit(solution)/shard_map/ppermute | solution.py:93
  73.3 1.7 %collective-permute-start.18 = (bf16[3,64,256]{2,1,0:T(8,128)(2,1)S(1)}, bf16[3,64,256]{2,1,0:T(8,128)(2,1)S(1)}, u32[]{:S(2)}, u32[]{:S(2)}) collective-permute-start(bf16[3,64,256]{2,1,0:T(8,128)(2,1)S(1)} %get-tuple-element.51), channel_id=1, source_target_pairs={{0,16},{16,0},{1,17},{17,1},{2,18},{18,2},{3,19},{19,3},{4,20},{20... | collective-permute-start | bytes 294920 | tf_op jit(solution)/shard_map/ppermute | solution.py:93
  77.3 9.8 %collective-permute-start.24 = (bf16[384,256]{1,0:T(8,128)(2,1)S(1)}, bf16[384,256]{1,0:T(8,128)(2,1)S(1)}, u32[]{:S(2)}, u32[]{:S(2)}) collective-permute-start(bf16[384,256]{1,0:T(8,128)(2,1)S(1)} %get-tuple-element.53.refs_2_), channel_id=1, source_target_pairs={{0,1},{1,0},{2,3},{3,2},{4,5},{5,4},{6,7},{7,6},{8,9},{9,8},{10,11... | collective-permute-start | bytes 589832 | tf_op jit(solution)/shard_map/ppermute | solution.py:93
  77.9 11.8 %collective-permute-start.25 = (bf16[384,256]{1,0:T(8,128)(2,1)S(1)}, bf16[384,256]{1,0:T(8,128)(2,1)S(1)}, u32[]{:S(2)}, u32[]{:S(2)}) collective-permute-start(bf16[384,256]{1,0:T(8,128)(2,1)S(1)} %get-tuple-element.53.refs_2_), channel_id=1, source_target_pairs={{0,2},{1,3},{2,0},{3,1},{4,6},{5,7},{6,4},{7,5},{8,10},{9,11},{10,... | collective-permute-start | bytes 589832 | tf_op jit(solution)/shard_map/ppermute | solution.py:93
  90.3 5.9 %collective-permute-start.26 = (bf16[384,256]{1,0:T(8,128)(2,1)S(1)}, bf16[384,256]{1,0:T(8,128)(2,1)S(1)}, u32[]{:S(2)}, u32[]{:S(2)}) collective-permute-start(bf16[384,256]{1,0:T(8,128)(2,1)S(1)} %shard_map.152.refs_0_), channel_id=1, source_target_pairs={{0,1},{1,0},{2,3},{3,2},{4,5},{5,4},{6,7},{7,6},{8,9},{9,8},{10,11... | collective-permute-start | bytes 589832 | tf_op jit(solution)/shard_map/ppermute | solution.py:93
  95.1 2.1 %collective-permute-start.28 = (bf16[384,256]{1,0:T(8,128)(2,1)S(1)}, bf16[384,256]{1,0:T(8,128)(2,1)S(1)}, u32[]{:S(2)}, u32[]{:S(2)}) collective-permute-start(bf16[384,256]{1,0:T(8,128)(2,1)S(1)} %collective-permute-done.25.refs_1_.refs_4_), channel_id=1, source_target_pairs={{0,16},{16,0},{1,17},{17,1},{2,18},{18,2},{3,19},{19,3},{4,20},{20... | collective-permute-start | bytes 589832 | tf_op jit(solution)/shard_map/ppermute | solution.py:93
  95.1 2.1 %collective-permute-start.27 = (bf16[384,256]{1,0:T(8,128)(2,1)S(1)}, bf16[384,256]{1,0:T(8,128)(2,1)S(1)}, u32[]{:S(2)}, u32[]{:S(2)}) collective-permute-start(bf16[384,256]{1,0:T(8,128)(2,1)S(1)} %collective-permute-done.24.refs_1_.refs_3_), channel_id=1, source_target_pairs={{0,16},{16,0},{1,17},{17,1},{2,18},{18,2},{3,19},{19,3},{4,20},{20... | collective-permute-start | bytes 589832 | tf_op jit(solution)/shard_map/ppermute | solution.py:93
  97.2 1.5 %collective-permute-start.29 = (bf16[384,256]{1,0:T(8,128)(2,1)S(1)}, bf16[384,256]{1,0:T(8,128)(2,1)S(1)}, u32[]{:S(2)}, u32[]{:S(2)}) collective-permute-start(bf16[384,256]{1,0:T(8,128)(2,1)S(1)} %get-tuple-element.69), channel_id=1, source_target_pairs={{0,16},{16,0},{1,17},{17,1},{2,18},{18,2},{3,19},{19,3},{4,20},{20... | collective-permute-start | bytes 589832 | tf_op jit(solution)/shard_map/ppermute | solution.py:93

commit v4 on v3

--- a/solution.py
+++ b/solution.py
@@ -13,7 +13,7 @@
 SIZES = [2, 3]
 GROUPS = [[0], [1]]
 SHARES = (3 / 4, 1.0)
-ORDER = ("c0", "c1", "x0", "x1", "b0", "s0", "s1", "a0", "p0", "q0", "a1", "p1", "k0", "j0", "q1", "v1", "y1", "o1", "m1", "k1", "j1")
+ORDER = ("c0", "c1", "x0", "x1", "b0", "s0", "s1", "a0", "p0", "q0", "a1", "p1", "k0", "q1", "j0", "v1", "o1", "y1", "m1", "k1", "j1")
 
 
 beta_first = 0.9
@@ -161,10 +161,8 @@
     token = [place]
     state = [{} for _ in pieces]
 
-    def run(kernel, out_shapes, *operands, late=None, mark=False):
-        order = [token[0]]
-        if late is not None:
-            order.append(group[late]["held"][0])
+    def run(kernel, out_shapes, *operands, mark=False, after=()):
+        order = [token[0], *after]
         if mark:
 
             def marked(place_ref, *refs):
@@ -321,6 +319,7 @@
             bases[1],
             bases[3],
             bases[2],
+            after=[group[k - 1]["swapped"][0]] if k and "swapped" in group[k - 1] else [],
         )
         held = [flip(share, "dev", 1), flip(share, "dev", 2)]
         if k < len(groups) - 1:
@@ -433,7 +432,7 @@
                 refs[-1][span, :] = region_mu * m_ref[span, :] + part[...]
 
         results["velocity"] = run(
-            kernel, [((rows, width), f32)], momentum, *[p["mean"] for p in group], late=-1, mark=True
+            kernel, [((rows, width), f32)], momentum, *[p["mean"] for p in group], mark=True
         )
 
     def stage_outer(k):

time: 101 us -> 100 us (0.990)
  transfers between devices with their start and end apart: 30 -> 30, of which waited for: 16 -> 17; matrix products, arithmetic and copies ran while one was open for 0% -> 0% of each run, Pallas kernels for 18% -> 18%
where the time goes in v4:
time: 100 us
  waiting for transfers between devices  47.5 us (48%)
  starting transfers between devices  25 us (25%)
  Pallas kernels  23.6 us (24%)
  local copies, waits for them, and re-layouts  2.93 us (3%)
    ppermute x30, waiting for transfers between devices, flip(): lax.ppermute(array, axis, [(i, i ^ bits) for i in range(lax.axis_size(axi...  47.5 us
    ppermute x30, starting transfers between devices, flip(): lax.ppermute(array, axis, [(i, i ^ bits) for i in range(lax.axis_size(axi...  25 us
    pallas_call x21, Pallas kernels, local_kernel(): pl.pallas_call(with_order, out_shape=[jax.ShapeDtypeStruct(shape, dtype)...  23.6 us
    unnamed x22, local copies, waits for them, and re-layouts  2.84 us
  transfers between devices with their start and end apart: 30, of which 17 were waited for; matrix products, arithmetic and copies ran while one was open for 0% of the time, Pallas kernels for 18%

profile of v4, /device:TPU:0, one launch (start us, length us, event | category | flops | bytes accessed | tf_op | source)
XLA Modules:
  0.0 100.0 jit_solution(17394242190716009215)
XLA Ops:
  0.7 1.3 %copy-done = bf16[256,2560]{1,0:T(8,128)(2,1)S(1)} copy-done((bf16[256,2560]{1,0:T(8,128)(2,1)S(1)}, bf16[256,2560]{1,0:T(8,128)(2,1)}, u32[]{:S(2)}) %copy-start) | copy-done | bytes 1310744
  2.0 0.9 copy-done.7
  3.0 0.6 shard_map.136.refs_0_
  3.6 3.1 %collective-permute-start = (bf16[256,1024]{1,0:T(8,128)(2,1)S(1)}, bf16[256,1024]{1,0:T(8,128)(2,1)S(1)}, u32[]{:S(2)}, u32[]{:S(2)}) collective-permute-start(bf16[256,1024]{1,0:T(8,128)(2,1)S(1)} %shard_map.136.refs_0_), channel_id=1, source_target_pairs={{0,1},{1,0},{2,3},{3,2},{4,5},{5,4},{6,7},{7,6},{8,9},{9,8},{10,11... | collective-permute-start | bytes 1572872 | tf_op jit(solution)/shard_map/ppermute | solution.py:93
  6.7 0.6 shard_map.137.refs_0_
  7.3 0.9 shard_map.138
  8.2 0.9 shard_map.139
  9.7 1.2 %shard_map.140 = (f32[640,512]{1,0:T(8,128)S(1)}, f32[640,512]{1,0:T(8,128)S(1)}, f32[640,512]{1,0:T(8,128)S(1)}) custom-call(s32[3]{0:T(128)S(1)} %pad_add_fusion.place_ref.refs_0_, f32[384,512]{1,0:T(8,128)S(1)} %get-tuple-element.39.refs_0_.refs_5_, f32[640,512]{1,0:T(8,128)S(1)} %bitcast.19, f32[640,512]{1,0:T(8,128)S(1)} %bitcast.20, ...), custom_call_target="tpu_custom_call" | custom-call | flops 1 | bytes 1 | tf_op jit(solution)/shard_map/pallas_call | solution.py:110
  11.3 8.1 %collective-permute-done.refs_2_.refs_3_.refs_4_.refs_6_ = bf16[256,1024]{1,0:T(8,128)(2,1)S(1)} collective-permute-done((bf16[256,1024]{1,0:T(8,128)(2,1)S(1)}, bf16[256,1024]{1,0:T(8,128)(2,1)S(1)}, u32[]{:S(2)}, u32[]{:S(2)}) %collective-permute-start) | collective-permute-done | bytes 524320 | tf_op jit(solution)/shard_map/ppermute | solution.py:93
  19.4 0.8 shard_map.141.refs_0_
  20.2 3.1 %collective-permute-start.2 = (bf16[256,512]{1,0:T(8,128)(2,1)S(1)}, bf16[256,512]{1,0:T(8,128)(2,1)S(1)}, u32[]{:S(2)}, u32[]{:S(2)}) collective-permute-start(bf16[256,512]{1,0:T(8,128)(2,1)S(1)} %shard_map.141.refs_0_), channel_id=1, source_target_pairs={{0,2},{1,3},{2,0},{3,1},{4,6},{5,7},{6,4},{7,5},{8,10},{9,11},{10,... | collective-permute-start | bytes 786440 | tf_op jit(solution)/shard_map/ppermute | solution.py:93
  23.4 9.3 %collective-permute-done.1.refs_2_.refs_6_ = bf16[256,768]{1,0:T(8,128)(2,1)S(1)} collective-permute-done((bf16[256,768]{1,0:T(8,128)(2,1)S(1)}, bf16[256,768]{1,0:T(8,128)(2,1)S(1)}, u32[]{:S(2)}, u32[]{:S(2)}) %collective-permute-start.1) | collective-permute-done | bytes 393248 | tf_op jit(solution)/shard_map/ppermute | solution.py:93
  32.6 0.8 shard_map.142.refs_0_
  33.5 1.1 %shard_map.143 = (bf16[256,512]{1,0:T(8,128)(2,1)S(1)}, f32[256,512]{1,0:T(8,128)S(1)}) custom-call(s32[3]{0:T(128)S(1)} %pad_add_fusion.place_ref.refs_0_, bf16[384,512]{1,0:T(8,128)(2,1)S(1)} %shard_map.142.refs_0_, f32[640,512]{1,0:T(8,128)S(1)} %bitcast.11, f32[640,512]{1,0:T(8,128)S(1)} %bitcast.14, f32[640,512]{1,0:T(8,128)S(1)} %get-tuple-element.40.refs_0_.refs_3_, ...), custom_call_target="tpu_custom_call" | custom-call | flops 1 | bytes 1 | tf_op jit(solution)/shard_map/pallas_call | solution.py:110
  34.7 1.8 %collective-permute-start.4 = (bf16[128,512]{1,0:T(8,128)(2,1)S(1)}, bf16[128,512]{1,0:T(8,128)(2,1)S(1)}, u32[]{:S(2)}, u32[]{:S(2)}) collective-permute-start(bf16[128,512]{1,0:T(8,128)(2,1)S(1)} %get-tuple-element.76), channel_id=1, source_target_pairs={{0,8},{4,12},{8,0},{12,4},{1,9},{5,13},{9,1},{13,5},{2,10},{6,14},... | collective-permute-start | bytes 393224 | tf_op jit(solution)/shard_map/ppermute | solution.py:93
  36.4 1.5 %collective-permute-start.3 = (bf16[128,512]{1,0:T(8,128)(2,1)S(1)}, bf16[128,512]{1,0:T(8,128)(2,1)S(1)}, u32[]{:S(2)}, u32[]{:S(2)}) collective-permute-start(bf16[128,512]{1,0:T(8,128)(2,1)S(1)} %get-tuple-element.77), channel_id=1, source_target_pairs={{0,4},{4,0},{8,12},{12,8},{1,5},{5,1},{9,13},{13,9},{2,6},{6,2},{1... | collective-permute-start | bytes 393224 | tf_op jit(solution)/shard_map/ppermute | solution.py:93
  37.9 1.7 %collective-permute-start.11 = (bf16[384,512]{1,0:T(8,128)(2,1)S(1)}, bf16[384,512]{1,0:T(8,128)(2,1)S(1)}, u32[]{:S(2)}, u32[]{:S(2)}) collective-permute-start(bf16[384,512]{1,0:T(8,128)(2,1)S(1)} %shard_map.142.refs_0_), channel_id=1, source_target_pairs={{0,2},{1,3},{2,0},{3,1},{4,6},{5,7},{6,4},{7,5},{8,10},{9,11},{10,... | collective-permute-start | bytes 1179656 | tf_op jit(solution)/shard_map/ppermute | solution.py:93
  39.7 1.7 %collective-permute-done.3.refs_2_ = bf16[128,512]{1,0:T(8,128)(2,1)S(1)} collective-permute-done((bf16[128,512]{1,0:T(8,128)(2,1)S(1)}, bf16[128,512]{1,0:T(8,128)(2,1)S(1)}, u32[]{:S(2)}, u32[]{:S(2)}) %collective-permute-start.3) | collective-permute-done | bytes 131104 | tf_op jit(solution)/shard_map/ppermute | solution.py:93
  41.4 0.6 shard_map.144.refs_0_.refs_1_
  42.0 1.6 %collective-permute-start.6 = (bf16[128,512]{1,0:T(8,128)(2,1)S(1)}, bf16[128,512]{1,0:T(8,128)(2,1)S(1)}, u32[]{:S(2)}, u32[]{:S(2)}) collective-permute-start(bf16[128,512]{1,0:T(8,128)(2,1)S(1)} %get-tuple-element.74), channel_id=1, source_target_pairs={{0,4},{4,0},{8,12},{12,8},{1,5},{5,1},{9,13},{13,9},{2,6},{6,2},{1... | collective-permute-start | bytes 393224 | tf_op jit(solution)/shard_map/ppermute | solution.py:93
  44.1 3.0 %collective-permute-done.6.refs_3_ = bf16[128,512]{1,0:T(8,128)(2,1)S(1)} collective-permute-done((bf16[128,512]{1,0:T(8,128)(2,1)S(1)}, bf16[128,512]{1,0:T(8,128)(2,1)S(1)}, u32[]{:S(2)}, u32[]{:S(2)}) %collective-permute-start.6) | collective-permute-done | bytes 131104 | tf_op jit(solution)/shard_map/ppermute | solution.py:93
  47.1 1.5 %collective-permute-done.5.refs_2_ = bf16[128,512]{1,0:T(8,128)(2,1)S(1)} collective-permute-done((bf16[128,512]{1,0:T(8,128)(2,1)S(1)}, bf16[128,512]{1,0:T(8,128)(2,1)S(1)}, u32[]{:S(2)}, u32[]{:S(2)}) %collective-permute-start.5) | collective-permute-done | bytes 131104 | tf_op jit(solution)/shard_map/ppermute | solution.py:93
  48.6 1.3 %collective-permute-done.8.refs_5_ = bf16[128,512]{1,0:T(8,128)(2,1)S(1)} collective-permute-done((bf16[128,512]{1,0:T(8,128)(2,1)S(1)}, bf16[128,512]{1,0:T(8,128)(2,1)S(1)}, u32[]{:S(2)}, u32[]{:S(2)}) %collective-permute-start.8) | collective-permute-done | bytes 131104 | tf_op jit(solution)/shard_map/ppermute | solution.py:93
  49.9 1.1 %shard_map.145 = (bf16[256,512]{1,0:T(8,128)(2,1)S(1)}, bf16[256,256]{1,0:T(8,128)(2,1)S(1)}, f32[256,512]{1,0:T(8,128)S(1)}, f32[256,512]{1,0:T(8,128)S(1)}) custom-call(s32[3]{0:T(128)S(1)} %pad_add_fusion.place_ref.refs_0_, bf16[256,512]{1,0:T(8,128)(2,1)S(1)} %shard_map.144.refs_0_.refs_1_, bf16[256,512]{1,0:T(8,128)(2,1)S(1)} %shard_map.144.refs_0_.refs_1_, ...), custom_call_target="tpu_custom_call" | custom-call | flops 1 | bytes 1 | tf_op jit(solution)/shard_map/pallas_call | solution.py:110
  51.0 5.6 %collective-permute-done.11.refs_7_ = bf16[384,512]{1,0:T(8,128)(2,1)S(1)} collective-permute-done((bf16[384,512]{1,0:T(8,128)(2,1)S(1)}, bf16[384,512]{1,0:T(8,128)(2,1)S(1)}, u32[]{:S(2)}, u32[]{:S(2)}) %collective-permute-start.11) | collective-permute-done | bytes 393248 | tf_op jit(solution)/shard_map/ppermute | solution.py:93
  56.7 1.3 %shard_map.146 = (bf16[384,512]{1,0:T(8,128)(2,1)S(1)}, f32[384,512]{1,0:T(8,128)S(1)}) custom-call(s32[3]{0:T(128)S(1)} %pad_add_fusion.place_ref.refs_0_, bf16[256,512]{1,0:T(8,128)(2,1)S(1)} %get-tuple-element.46.refs_0_.refs_2_, f32[640,512]{1,0:T(8,128)S(1)} %bitcast.12, f32[640,512]{1,0:T(8,128)S(1)} %bitcast.15, ...), custom_call_target="tpu_custom_call" | custom-call | flops 1 | bytes 1 | tf_op jit(solution)/shard_map/pallas_call | solution.py:110
  58.0 0.6 collective-permute-start.13
  58.6 0.7 collective-permute-start.12
  59.3 2.4 %collective-permute-start.16 = (bf16[256,256]{1,0:T(8,128)(2,1)S(1)}, bf16[256,256]{1,0:T(8,128)(2,1)S(1)}, u32[]{:S(2)}, u32[]{:S(2)}) collective-permute-start(bf16[256,256]{1,0:T(8,128)(2,1)S(1)} %get-tuple-element.48.refs_2_), channel_id=1, source_target_pairs={{0,3},{1,2},{2,1},{3,0},{4,7},{5,6},{6,5},{7,4},{8,11},{9,10},{10,... | collective-permute-start | bytes 393224 | tf_op jit(solution)/shard_map/ppermute | solution.py:93
  61.7 2.0 %collective-permute-start.14 = (bf16[256,256]{1,0:T(8,128)(2,1)S(1)}, bf16[256,256]{1,0:T(8,128)(2,1)S(1)}, u32[]{:S(2)}, u32[]{:S(2)}) collective-permute-start(bf16[256,256]{1,0:T(8,128)(2,1)S(1)} %get-tuple-element.48.refs_2_), channel_id=1, source_target_pairs={{0,1},{1,0},{2,3},{3,2},{4,5},{5,4},{6,7},{7,6},{8,9},{9,8},{10,11... | collective-permute-start | bytes 393224 | tf_op jit(solution)/shard_map/ppermute | solution.py:93
  64.3 0.6 shard_map.147.refs_0_.refs_2_
  65.0 0.8 collective-permute-start.19
  65.8 1.5 %collective-permute-start.18 = (bf16[192,512]{1,0:T(8,128)(2,1)S(1)}, bf16[192,512]{1,0:T(8,128)(2,1)S(1)}, u32[]{:S(2)}, u32[]{:S(2)}) collective-permute-start(bf16[192,512]{1,0:T(8,128)(2,1)S(1)} %get-tuple-element.71), channel_id=1, source_target_pairs={{0,8},{4,12},{8,0},{12,4},{1,9},{5,13},{9,1},{13,5},{2,10},{6,14},... | collective-permute-start | bytes 589832 | tf_op jit(solution)/shard_map/ppermute | solution.py:93
  67.3 4.4 %collective-permute-done.15.refs_4_ = bf16[256,256]{1,0:T(8,128)(2,1)S(1)} collective-permute-done((bf16[256,256]{1,0:T(8,128)(2,1)S(1)}, bf16[256,256]{1,0:T(8,128)(2,1)S(1)}, u32[]{:S(2)}, u32[]{:S(2)}) %collective-permute-start.15) | collective-permute-done | bytes 131104 | tf_op jit(solution)/shard_map/ppermute | solution.py:93
  71.7 0.9 shard_map.148
  73.3 1.0 collective-permute-done.17.refs_1_.refs_4_
  74.8 1.5 %shard_map.149 = (bf16[384,512]{1,0:T(8,128)(2,1)S(1)}, bf16[384,256]{1,0:T(8,128)(2,1)S(1)}, f32[384,512]{1,0:T(8,128)S(1)}, f32[384,512]{1,0:T(8,128)S(1)}) custom-call(s32[3]{0:T(128)S(1)} %pad_add_fusion.place_ref.refs_0_, f32[256,256]{1,0:T(8,128)S(1)} %get-tuple-element.49.refs_0_.refs_3_, ...), custom_call_target="tpu_custom_call" | custom-call | flops 1 | bytes 1 | tf_op jit(solution)/shard_map/pallas_call | solution.py:110
  76.6 1.8 %collective-permute-start.25 = (bf16[384,256]{1,0:T(8,128)(2,1)S(1)}, bf16[384,256]{1,0:T(8,128)(2,1)S(1)}, u32[]{:S(2)}, u32[]{:S(2)}) collective-permute-start(bf16[384,256]{1,0:T(8,128)(2,1)S(1)} %get-tuple-element.59.refs_2_), channel_id=1, source_target_pairs={{0,1},{1,0},{2,3},{3,2},{4,5},{5,4},{6,7},{7,6},{8,9},{9,8},{10,11... | collective-permute-start | bytes 589832 | tf_op jit(solution)/shard_map/ppermute | solution.py:93
  78.3 0.8 shard_map.150.refs_0_.refs_7_
  79.2 1.7 %shard_map.151 = (f32[640,512]{1,0:T(8,128)}, f32[8,128]{1,0:T(8,128)S(1)}) custom-call(s32[3]{0:T(128)S(1)} %pad_add_fusion.place_ref.refs_0_, f32[256,512]{1,0:T(8,128)S(1)} %shard_map.150.refs_0_.refs_7_, f32[640,512]{1,0:T(8,128)S(1)} %bitcast.18, f32[256,512]{1,0:T(8,128)S(1)} %get-tuple-element.53.refs_2_, f32[384,512]{1,0:T(8,128)S(1)} %get-tuple-element.54.refs_3_), custom_call_target="tpu_custom_call" | custom-call | flops 1 | bytes 1 | tf_op jit(solution)/shard_map/pallas_call | solution.py:110
  80.9 2.4 %shard_map.152 = (f32[640,512]{1,0:T(8,128)}, f32[640,512]{1,0:T(8,128)}, f32[8,128]{1,0:T(8,128)S(1)}) custom-call(s32[3]{0:T(128)S(1)} %pad_add_fusion.place_ref.refs_0_, f32[8,128]{1,0:T(8,128)S(1)} %get-tuple-element.55.refs_0_, f32[640,512]{1,0:T(8,128)S(1)} %copy-done.4, f32[640,512]{1,0:T(8,128)S(1)} %copy-done.5, ...), custom_call_target="tpu_custom_call" | custom-call | flops 1 | bytes 1 | tf_op jit(solution)/shard_map/pallas_call | solution.py:110
  83.3 5.0 %collective-permute-done.24.refs_1_.refs_4_ = bf16[384,256]{1,0:T(8,128)(2,1)S(1)} collective-permute-done((bf16[384,256]{1,0:T(8,128)(2,1)S(1)}, bf16[384,256]{1,0:T(8,128)(2,1)S(1)}, u32[]{:S(2)}, u32[]{:S(2)}) %collective-permute-start.24) | collective-permute-done | bytes 196640 | tf_op jit(solution)/shard_map/ppermute | solution.py:93
  88.3 0.6 shard_map.153.refs_0_
  89.0 2.4 %shard_map.154 = (f32[640,512]{1,0:T(8,128)}, f32[640,512]{1,0:T(8,128)}, f32[8,128]{1,0:T(8,128)S(1)}) custom-call(s32[3]{0:T(128)S(1)} %pad_add_fusion.place_ref.refs_0_, bf16[384,256]{1,0:T(8,128)(2,1)S(1)} %shard_map.153.refs_0_, f32[640,512]{1,0:T(8,128)S(1)} %bitcast.13, f32[640,512]{1,0:T(8,128)S(1)} %bitcast.16, ...), custom_call_target="tpu_custom_call" | custom-call | flops 1 | bytes 1 | tf_op jit(solution)/shard_map/pallas_call | solution.py:110
  91.9 3.9 %collective-permute-done.26.refs_5_ = bf16[384,256]{1,0:T(8,128)(2,1)S(1)} collective-permute-done((bf16[384,256]{1,0:T(8,128)(2,1)S(1)}, bf16[384,256]{1,0:T(8,128)(2,1)S(1)}, u32[]{:S(2)}, u32[]{:S(2)}) %collective-permute-start.26) | collective-permute-done | bytes 196640 | tf_op jit(solution)/shard_map/ppermute | solution.py:93
  95.8 1.0 shard_map.155
  96.9 1.4 %collective-permute-done.29.refs_6_ = bf16[384,256]{1,0:T(8,128)(2,1)S(1)} collective-permute-done((bf16[384,256]{1,0:T(8,128)(2,1)S(1)}, bf16[384,256]{1,0:T(8,128)(2,1)S(1)}, u32[]{:S(2)}, u32[]{:S(2)}) %collective-permute-start.29) | collective-permute-done | bytes 196640 | tf_op jit(solution)/shard_map/ppermute | solution.py:93
  98.3 1.7 %shard_map.156 = bf16[256,512]{1,0:T(8,128)(2,1)} custom-call(s32[3]{0:T(128)S(1)} %pad_add_fusion.place_ref.refs_0_, f32[256,256]{1,0:T(8,128)S(1)} %get-tuple-element.68.refs_0_.refs_3_, bf16[256,2560]{1,0:T(8,128)(2,1)S(1)} %copy-done.1, bf16[384,512]{1,0:T(8,128)(2,1)S(1)} %get-tuple-element.51.refs_0_.refs_2_, ...), custom_call_target="tpu_custom_call" | custom-call | flops 1 | bytes 1 | tf_op jit(solution)/shard_map/pallas_call | solution.py:110
  (60 shorter events, 4.5 us)
Async XLA Ops:
  0.7 1.3 %copy-start = (bf16[256,2560]{1,0:T(8,128)(2,1)S(1)}, bf16[256,2560]{1,0:T(8,128)(2,1)}, u32[]{:S(2)}) copy-start(bf16[256,2560]{1,0:T(8,128)(2,1)} %refs_1_.17) | copy-start | bytes 3932164
  2.0 0.9 copy-start.7
  3.0 6.2 %copy-start.10 = (f32[1,640,512]{2,1,0:T(8,128)S(1)}, f32[1,640,512]{2,1,0:T(8,128)}, u32[]{:S(2)}) copy-start(f32[1,640,512]{2,1,0:T(8,128)} %param.14) | copy-start | bytes 3932164
  3.6 3.7 %copy-start.8 = (bf16[256,512]{1,0:T(8,128)(2,1)S(1)}, bf16[256,512]{1,0:T(8,128)(2,1)}, u32[]{:S(2)}) copy-start(bf16[256,512]{1,0:T(8,128)(2,1)} %refs_2_.6) | copy-start | bytes 786436
  3.6 15.8 %collective-permute-start = (bf16[256,1024]{1,0:T(8,128)(2,1)S(1)}, bf16[256,1024]{1,0:T(8,128)(2,1)S(1)}, u32[]{:S(2)}, u32[]{:S(2)}) collective-permute-start(bf16[256,1024]{1,0:T(8,128)(2,1)S(1)} %shard_map.136.refs_0_), channel_id=1, source_target_pairs={{0,1},{1,0},{2,3},{3,2},{4,5},{5,4},{6,7},{7,6},{8,9},{9,8},{10,11... | collective-permute-start | bytes 1572872 | tf_op jit(solution)/shard_map/ppermute | solution.py:93
  6.7 2.5 %copy-start.9 = (f32[1,1,640,512]{3,2,1,0:T(8,128)S(1)}, f32[1,1,640,512]{3,2,1,0:T(8,128)}, u32[]{:S(2)}) copy-start(f32[1,1,640,512]{3,2,1,0:T(8,128)} %param.11) | copy-start | bytes 3932164
  7.3 1.9 %copy-start.5 = (f32[640,512]{1,0:T(8,128)S(1)}, f32[640,512]{1,0:T(8,128)}, u32[]{:S(2)}) copy-start(f32[640,512]{1,0:T(8,128)} %refs_2_.7) | copy-start | bytes 3932164
  7.3 1.9 %copy-start.6 = (f32[1,640,512]{2,1,0:T(8,128)S(1)}, f32[1,640,512]{2,1,0:T(8,128)}, u32[]{:S(2)}) copy-start(f32[1,640,512]{2,1,0:T(8,128)} %param.15) | copy-start | bytes 3932164
  8.2 1.5 %copy-start.4 = (f32[640,512]{1,0:T(8,128)S(1)}, f32[640,512]{1,0:T(8,128)}, u32[]{:S(2)}) copy-start(f32[640,512]{1,0:T(8,128)} %refs_1_.15) | copy-start | bytes 3932164
  10.9 39.0 %collective-permute-start.10 = (f32[640,512]{1,0:T(8,128)S(1)}, f32[640,512]{1,0:T(8,128)S(1)}, u32[]{:S(2)}, u32[]{:S(2)}) collective-permute-start(f32[640,512]{1,0:T(8,128)S(1)} %get-tuple-element.44.refs_7_.refs_8_), channel_id=1, source_target_pairs={{0,16},{16,0},{1,17},{17,1},{2,18},{18,2},{3,19},{19,3},{4,20},{20... | collective-permute-start | bytes 3932168 | tf_op jit(solution)/shard_map/ppermute | solution.py:93
  11.0 21.6 %collective-permute-start.1 = (bf16[256,768]{1,0:T(8,128)(2,1)S(1)}, bf16[256,768]{1,0:T(8,128)(2,1)S(1)}, u32[]{:S(2)}, u32[]{:S(2)}) collective-permute-start(bf16[256,768]{1,0:T(8,128)(2,1)S(1)} %shard_map.137.refs_0_), channel_id=1, source_target_pairs={{0,1},{1,0},{2,3},{3,2},{4,5},{5,4},{6,7},{7,6},{8,9},{9,8},{10,11... | collective-permute-start | bytes 1179656 | tf_op jit(solution)/shard_map/ppermute | solution.py:93
  19.4 14.1 %copy-start.3 = (f32[1,1,640,512]{3,2,1,0:T(8,128)S(1)}, f32[1,1,640,512]{3,2,1,0:T(8,128)}, u32[]{:S(2)}) copy-start(f32[1,1,640,512]{3,2,1,0:T(8,128)} %param.13) | copy-start | bytes 3932164
  20.2 13.3 %copy-start.2 = (f32[1,1,640,512]{3,2,1,0:T(8,128)S(1)}, f32[1,1,640,512]{3,2,1,0:T(8,128)}, u32[]{:S(2)}) copy-start(f32[1,1,640,512]{3,2,1,0:T(8,128)} %param.12) | copy-start | bytes 3932164
  20.2 13.2 %collective-permute-start.2 = (bf16[256,512]{1,0:T(8,128)(2,1)S(1)}, bf16[256,512]{1,0:T(8,128)(2,1)S(1)}, u32[]{:S(2)}, u32[]{:S(2)}) collective-permute-start(bf16[256,512]{1,0:T(8,128)(2,1)S(1)} %shard_map.141.refs_0_), channel_id=1, source_target_pairs={{0,2},{1,3},{2,0},{3,1},{4,6},{5,7},{6,4},{7,5},{8,10},{9,11},{10,... | collective-permute-start | bytes 786440 | tf_op jit(solution)/shard_map/ppermute | solution.py:93
  34.7 5.0 %collective-permute-start.4 = (bf16[128,512]{1,0:T(8,128)(2,1)S(1)}, bf16[128,512]{1,0:T(8,128)(2,1)S(1)}, u32[]{:S(2)}, u32[]{:S(2)}) collective-permute-start(bf16[128,512]{1,0:T(8,128)(2,1)S(1)} %get-tuple-element.76), channel_id=1, source_target_pairs={{0,8},{4,12},{8,0},{12,4},{1,9},{5,13},{9,1},{13,5},{2,10},{6,14},... | collective-permute-start | bytes 393224 | tf_op jit(solution)/shard_map/ppermute | solution.py:93
  36.4 5.0 %collective-permute-start.3 = (bf16[128,512]{1,0:T(8,128)(2,1)S(1)}, bf16[128,512]{1,0:T(8,128)(2,1)S(1)}, u32[]{:S(2)}, u32[]{:S(2)}) collective-permute-start(bf16[128,512]{1,0:T(8,128)(2,1)S(1)} %get-tuple-element.77), channel_id=1, source_target_pairs={{0,4},{4,0},{8,12},{12,8},{1,5},{5,1},{9,13},{13,9},{2,6},{6,2},{1... | collective-permute-start | bytes 393224 | tf_op jit(solution)/shard_map/ppermute | solution.py:93
  37.9 18.7 %collective-permute-start.11 = (bf16[384,512]{1,0:T(8,128)(2,1)S(1)}, bf16[384,512]{1,0:T(8,128)(2,1)S(1)}, u32[]{:S(2)}, u32[]{:S(2)}) collective-permute-start(bf16[384,512]{1,0:T(8,128)(2,1)S(1)} %shard_map.142.refs_0_), channel_id=1, source_target_pairs={{0,2},{1,3},{2,0},{3,1},{4,6},{5,7},{6,4},{7,5},{8,10},{9,11},{10,... | collective-permute-start | bytes 1179656 | tf_op jit(solution)/shard_map/ppermute | solution.py:93
  42.0 5.0 %collective-permute-start.6 = (bf16[128,512]{1,0:T(8,128)(2,1)S(1)}, bf16[128,512]{1,0:T(8,128)(2,1)S(1)}, u32[]{:S(2)}, u32[]{:S(2)}) collective-permute-start(bf16[128,512]{1,0:T(8,128)(2,1)S(1)} %get-tuple-element.74), channel_id=1, source_target_pairs={{0,4},{4,0},{8,12},{12,8},{1,5},{5,1},{9,13},{13,9},{2,6},{6,2},{1... | collective-permute-start | bytes 393224 | tf_op jit(solution)/shard_map/ppermute | solution.py:93
  43.6 5.0 %collective-permute-start.5 = (bf16[128,512]{1,0:T(8,128)(2,1)S(1)}, bf16[128,512]{1,0:T(8,128)(2,1)S(1)}, u32[]{:S(2)}, u32[]{:S(2)}) collective-permute-start(bf16[128,512]{1,0:T(8,128)(2,1)S(1)} %get-tuple-element.75), channel_id=1, source_target_pairs={{0,8},{4,12},{8,0},{12,4},{1,9},{5,13},{9,1},{13,5},{2,10},{6,14},... | collective-permute-start | bytes 393224 | tf_op jit(solution)/shard_map/ppermute | solution.py:93
  44.1 5.8 %collective-permute-start.7 = (bf16[256,512]{1,0:T(8,128)(2,1)S(1)}, bf16[256,512]{1,0:T(8,128)(2,1)S(1)}, u32[]{:S(2)}, u32[]{:S(2)}) collective-permute-start(bf16[256,512]{1,0:T(8,128)(2,1)S(1)} %shard_map.144.refs_0_.refs_1_), channel_id=1, source_target_pairs={{0,16},{16,0},{1,17},{17,1},{2,18},{18,2},{3,19},{19,3},{4,20},{20... | collective-permute-start | bytes 786440 | tf_op jit(solution)/shard_map/ppermute | solution.py:93
  47.1 1.5 %collective-permute-start.9 = (bf16[128,512]{1,0:T(8,128)(2,1)S(1)}, bf16[128,512]{1,0:T(8,128)(2,1)S(1)}, u32[]{:S(2)}, u32[]{:S(2)}) collective-permute-start(bf16[128,512]{1,0:T(8,128)(2,1)S(1)} %collective-permute-done.6.refs_3_), channel_id=1, source_target_pairs={{0,16},{16,0},{1,17},{17,1},{2,18},{18,2},{3,19},{19,3},{4,20},{20... | collective-permute-start | bytes 393224 | tf_op jit(solution)/shard_map/ppermute | solution.py:93
  48.6 1.3 %collective-permute-start.8 = (bf16[128,512]{1,0:T(8,128)(2,1)S(1)}, bf16[128,512]{1,0:T(8,128)(2,1)S(1)}, u32[]{:S(2)}, u32[]{:S(2)}) collective-permute-start(bf16[128,512]{1,0:T(8,128)(2,1)S(1)} %collective-permute-done.5.refs_2_), channel_id=1, source_target_pairs={{0,16},{16,0},{1,17},{17,1},{2,18},{18,2},{3,19},{19,3},{4,20},{20... | collective-permute-start | bytes 393224 | tf_op jit(solution)/shard_map/ppermute | solution.py:93
  58.0 13.7 %copy-start.1 = (bf16[256,2560]{1,0:T(8,128)(2,1)S(1)}, bf16[256,2560]{1,0:T(8,128)(2,1)}, u32[]{:S(2)}) copy-start(bf16[256,2560]{1,0:T(8,128)(2,1)} %refs_1_.17) | copy-start | bytes 3932164
  58.0 5.7 %collective-permute-start.13 = (bf16[192,512]{1,0:T(8,128)(2,1)S(1)}, bf16[192,512]{1,0:T(8,128)(2,1)S(1)}, u32[]{:S(2)}, u32[]{:S(2)}) collective-permute-start(bf16[192,512]{1,0:T(8,128)(2,1)S(1)} %get-tuple-element.72), channel_id=1, source_target_pairs={{0,8},{4,12},{8,0},{12,4},{1,9},{5,13},{9,1},{13,5},{2,10},{6,14},... | collective-permute-start | bytes 589832 | tf_op jit(solution)/shard_map/ppermute | solution.py:93
  58.6 5.7 %collective-permute-start.12 = (bf16[192,512]{1,0:T(8,128)(2,1)S(1)}, bf16[192,512]{1,0:T(8,128)(2,1)S(1)}, u32[]{:S(2)}, u32[]{:S(2)}) collective-permute-start(bf16[192,512]{1,0:T(8,128)(2,1)S(1)} %get-tuple-element.73), channel_id=1, source_target_pairs={{0,4},{4,0},{8,12},{12,8},{1,5},{5,1},{9,13},{13,9},{2,6},{6,2},{1... | collective-permute-start | bytes 589832 | tf_op jit(solution)/shard_map/ppermute | solution.py:93
  59.3 8.0 %collective-permute-start.16 = (bf16[256,256]{1,0:T(8,128)(2,1)S(1)}, bf16[256,256]{1,0:T(8,128)(2,1)S(1)}, u32[]{:S(2)}, u32[]{:S(2)}) collective-permute-start(bf16[256,256]{1,0:T(8,128)(2,1)S(1)} %get-tuple-element.48.refs_2_), channel_id=1, source_target_pairs={{0,3},{1,2},{2,1},{3,0},{4,7},{5,6},{6,5},{7,4},{8,11},{9,10},{10,... | collective-permute-start | bytes 393224 | tf_op jit(solution)/shard_map/ppermute | solution.py:93
  61.7 10.0 %collective-permute-start.15 = (bf16[256,256]{1,0:T(8,128)(2,1)S(1)}, bf16[256,256]{1,0:T(8,128)(2,1)S(1)}, u32[]{:S(2)}, u32[]{:S(2)}) collective-permute-start(bf16[256,256]{1,0:T(8,128)(2,1)S(1)} %get-tuple-element.48.refs_2_), channel_id=1, source_target_pairs={{0,2},{1,3},{2,0},{3,1},{4,6},{5,7},{6,4},{7,5},{8,10},{9,11},{10,... | collective-permute-start | bytes 393224 | tf_op jit(solution)/shard_map/ppermute | solution.py:93
  61.7 10.0 %collective-permute-start.14 = (bf16[256,256]{1,0:T(8,128)(2,1)S(1)}, bf16[256,256]{1,0:T(8,128)(2,1)S(1)}, u32[]{:S(2)}, u32[]{:S(2)}) collective-permute-start(bf16[256,256]{1,0:T(8,128)(2,1)S(1)} %get-tuple-element.48.refs_2_), channel_id=1, source_target_pairs={{0,1},{1,0},{2,3},{3,2},{4,5},{5,4},{6,7},{7,6},{8,9},{9,8},{10,11... | collective-permute-start | bytes 393224 | tf_op jit(solution)/shard_map/ppermute | solution.py:93
  65.0 7.7 %collective-permute-start.19 = (bf16[192,512]{1,0:T(8,128)(2,1)S(1)}, bf16[192,512]{1,0:T(8,128)(2,1)S(1)}, u32[]{:S(2)}, u32[]{:S(2)}) collective-permute-start(bf16[192,512]{1,0:T(8,128)(2,1)S(1)} %get-tuple-element.70), channel_id=1, source_target_pairs={{0,4},{4,0},{8,12},{12,8},{1,5},{5,1},{9,13},{13,9},{2,6},{6,2},{1... | collective-permute-start | bytes 589832 | tf_op jit(solution)/shard_map/ppermute | solution.py:93
  65.8 7.4 %collective-permute-start.18 = (bf16[192,512]{1,0:T(8,128)(2,1)S(1)}, bf16[192,512]{1,0:T(8,128)(2,1)S(1)}, u32[]{:S(2)}, u32[]{:S(2)}) collective-permute-start(bf16[192,512]{1,0:T(8,128)(2,1)S(1)} %get-tuple-element.71), channel_id=1, source_target_pairs={{0,8},{4,12},{8,0},{12,4},{1,9},{5,13},{9,1},{13,5},{2,10},{6,14},... | collective-permute-start | bytes 589832 | tf_op jit(solution)/shard_map/ppermute | solution.py:93
  67.3 7.5 %collective-permute-start.20 = (bf16[384,512]{1,0:T(8,128)(2,1)S(1)}, bf16[384,512]{1,0:T(8,128)(2,1)S(1)}, u32[]{:S(2)}, u32[]{:S(2)}) collective-permute-start(bf16[384,512]{1,0:T(8,128)(2,1)S(1)} %shard_map.147.refs_0_.refs_2_), channel_id=1, source_target_pairs={{0,16},{16,0},{1,17},{17,1},{2,18},{18,2},{3,19},{19,3},{4,20},{20... | collective-permute-start | bytes 1179656 | tf_op jit(solution)/shard_map/ppermute | solution.py:93
  72.6 1.6 %collective-permute-start.17 = (bf16[3,192,256]{2,1,0:T(8,128)(2,1)S(1)}, bf16[3,192,256]{2,1,0:T(8,128)(2,1)S(1)}, u32[]{:S(2)}, u32[]{:S(2)}) collective-permute-start(bf16[3,192,256]{2,1,0:T(8,128)(2,1)S(1)} %get-tuple-element.50), channel_id=1, source_target_pairs={{0,16},{16,0},{1,17},{17,1},{2,18},{18,2},{3,19},{19,3},{4,20},{20... | collective-permute-start | bytes 884744 | tf_op jit(solution)/shard_map/ppermute | solution.py:93
  72.7 1.8 %collective-permute-start.22 = (bf16[192,512]{1,0:T(8,128)(2,1)S(1)}, bf16[192,512]{1,0:T(8,128)(2,1)S(1)}, u32[]{:S(2)}, u32[]{:S(2)}) collective-permute-start(bf16[192,512]{1,0:T(8,128)(2,1)S(1)} %collective-permute-done.19.refs_4_), channel_id=1, source_target_pairs={{0,16},{16,0},{1,17},{17,1},{2,18},{18,2},{3,19},{19,3},{4,20},{20... | collective-permute-start | bytes 589832 | tf_op jit(solution)/shard_map/ppermute | solution.py:93
  73.2 1.6 %collective-permute-start.21 = (bf16[192,512]{1,0:T(8,128)(2,1)S(1)}, bf16[192,512]{1,0:T(8,128)(2,1)S(1)}, u32[]{:S(2)}, u32[]{:S(2)}) collective-permute-start(bf16[192,512]{1,0:T(8,128)(2,1)S(1)} %collective-permute-done.18.refs_3_), channel_id=1, source_target_pairs={{0,16},{16,0},{1,17},{17,1},{2,18},{18,2},{3,19},{19,3},{4,20},{20... | collective-permute-start | bytes 589832 | tf_op jit(solution)/shard_map/ppermute | solution.py:93
  76.3 12.1 %collective-permute-start.24 = (bf16[384,256]{1,0:T(8,128)(2,1)S(1)}, bf16[384,256]{1,0:T(8,128)(2,1)S(1)}, u32[]{:S(2)}, u32[]{:S(2)}) collective-permute-start(bf16[384,256]{1,0:T(8,128)(2,1)S(1)} %get-tuple-element.59.refs_2_), channel_id=1, source_target_pairs={{0,2},{1,3},{2,0},{3,1},{4,6},{5,7},{6,4},{7,5},{8,10},{9,11},{10,... | collective-permute-start | bytes 589832 | tf_op jit(solution)/shard_map/ppermute | solution.py:93
  76.4 2.0 %collective-permute-start.23 = (bf16[3,64,256]{2,1,0:T(8,128)(2,1)S(1)}, bf16[3,64,256]{2,1,0:T(8,128)(2,1)S(1)}, u32[]{:S(2)}, u32[]{:S(2)}) collective-permute-start(bf16[3,64,256]{2,1,0:T(8,128)(2,1)S(1)} %get-tuple-element.52), channel_id=1, source_target_pairs={{0,16},{16,0},{1,17},{17,1},{2,18},{18,2},{3,19},{19,3},{4,20},{20... | collective-permute-start | bytes 294920 | tf_op jit(solution)/shard_map/ppermute | solution.py:93
  76.6 14.8 %collective-permute-start.25 = (bf16[384,256]{1,0:T(8,128)(2,1)S(1)}, bf16[384,256]{1,0:T(8,128)(2,1)S(1)}, u32[]{:S(2)}, u32[]{:S(2)}) collective-permute-start(bf16[384,256]{1,0:T(8,128)(2,1)S(1)} %get-tuple-element.59.refs_2_), channel_id=1, source_target_pairs={{0,1},{1,0},{2,3},{3,2},{4,5},{5,4},{6,7},{7,6},{8,9},{9,8},{10,11... | collective-permute-start | bytes 589832 | tf_op jit(solution)/shard_map/ppermute | solution.py:93
  88.9 6.9 %collective-permute-start.26 = (bf16[384,256]{1,0:T(8,128)(2,1)S(1)}, bf16[384,256]{1,0:T(8,128)(2,1)S(1)}, u32[]{:S(2)}, u32[]{:S(2)}) collective-permute-start(bf16[384,256]{1,0:T(8,128)(2,1)S(1)} %shard_map.153.refs_0_), channel_id=1, source_target_pairs={{0,1},{1,0},{2,3},{3,2},{4,5},{5,4},{6,7},{7,6},{8,9},{9,8},{10,11... | collective-permute-start | bytes 589832 | tf_op jit(solution)/shard_map/ppermute | solution.py:93
  91.4 5.5 %collective-permute-start.28 = (bf16[384,256]{1,0:T(8,128)(2,1)S(1)}, bf16[384,256]{1,0:T(8,128)(2,1)S(1)}, u32[]{:S(2)}, u32[]{:S(2)}) collective-permute-start(bf16[384,256]{1,0:T(8,128)(2,1)S(1)} %collective-permute-done.24.refs_1_.refs_4_), channel_id=1, source_target_pairs={{0,16},{16,0},{1,17},{17,1},{2,18},{18,2},{3,19},{19,3},{4,20},{20... | collective-permute-start | bytes 589832 | tf_op jit(solution)/shard_map/ppermute | solution.py:93
  91.4 5.5 %collective-permute-start.27 = (bf16[384,256]{1,0:T(8,128)(2,1)S(1)}, bf16[384,256]{1,0:T(8,128)(2,1)S(1)}, u32[]{:S(2)}, u32[]{:S(2)}) collective-permute-start(bf16[384,256]{1,0:T(8,128)(2,1)S(1)} %collective-permute-done.25.refs_3_), channel_id=1, source_target_pairs={{0,16},{16,0},{1,17},{17,1},{2,18},{18,2},{3,19},{19,3},{4,20},{20... | collective-permute-start | bytes 589832 | tf_op jit(solution)/shard_map/ppermute | solution.py:93
  96.8 1.5 %collective-permute-start.29 = (bf16[384,256]{1,0:T(8,128)(2,1)S(1)}, bf16[384,256]{1,0:T(8,128)(2,1)S(1)}, u32[]{:S(2)}, u32[]{:S(2)}) collective-permute-start(bf16[384,256]{1,0:T(8,128)(2,1)S(1)} %get-tuple-element.69), channel_id=1, source_target_pairs={{0,16},{16,0},{1,17},{17,1},{2,18},{18,2},{3,19},{19,3},{4,20},{20... | collective-permute-start | bytes 589832 | tf_op jit(solution)/shard_map/ppermute | solution.py:93

commit v5 on v4

--- a/solution.py
+++ b/solution.py
@@ -184,18 +184,23 @@
     def stage_message(k):
         start, stop = pieces[k]
         size = stop - start
-        extra = width if k == 0 else 0
-
-        def kernel(place_ref, *refs):
-            a_ref, out_ref = refs[0], refs[-1]
+
+        def kernel(place_ref, a_ref, out_ref):
             for i, bits in enumerate((1, 3)):
                 at = columns(flipped(place_ref, bits), start, size)
                 out_ref[:, i * size : (i + 1) * size] = a_ref[:, at]
-            if extra:
-                out_ref[:, 2 * size :] = refs[1][...]
-
-        operands = (activations, cotangent) if extra else (activations,)
-        (message,) = run(kernel, [((tokens, 2 * size + extra), bf16)], *operands)
+
+        if k:
+            (message,) = run(kernel, [((tokens, 2 * size), bf16)], activations)
+        else:
+            at = [activations[:, i * rows + start : i * rows + stop] for i in range(devs)]
+            lower, upper = [
+                jnp.where(place[0] == 0, at[2 * i + 1], at[2 * i]) for i in range(devs // 2)
+            ]
+            kept = jnp.where(place[1] == 0, lower, upper)
+            sent = jnp.where(place[1] == 0, upper, lower)
+            message = jnp.concatenate([kept, sent, cotangent], axis=1)
+            token[0] = message
         state[k]["raw"] = flip(message, "dev", 1)
 
     def stage_own(k):

time: 100 us -> 99.5 us (level)
  other arithmetic: 0.08 us -> 2.31 us
  waiting for transfers between devices: 47.5 us -> 46.1 us
    ppermute x30, waiting for transfers between devices: 47.5 us -> 46.1 us  [flip(): lax.ppermute(array, axis, [(i, i ^ bits) for i in range(lax.axis_size(axi...]
    select_n x0 -> x1, other arithmetic: none -> 1.23 us  [stage_message(): kept = jnp.where(place[1] == 0, lower, upper)]
    unnamed x22 -> x18, local copies, waits for them, and re-layouts: 2.84 us -> 1.88 us
    pallas_call x21 -> x20, Pallas kernels: 23.6 us -> 23 us  [local_kernel(): pl.pallas_call(with_order, out_shape=[jax.ShapeDtypeStruct(shape, dtype)...]
  transfers between devices with their start and end apart: 30 -> 30, of which waited for: 17 -> 17; matrix products, arithmetic and copies ran while one was open for 0% -> 0% of each run, Pallas kernels for 18% -> 19%
where the time goes in v5:
time: 99.5 us; the launch traced here: 99.3 us
  waiting for transfers between devices  46.1 us (46%)
  starting transfers between devices  24.9 us (25%)
  Pallas kernels  23 us (23%)
  other arithmetic  2.31 us (2%)
  local copies, waits for them, and re-layouts  1.98 us (2%)
    ppermute x30, waiting for transfers between devices, flip(): lax.ppermute(array, axis, [(i, i ^ bits) for i in range(lax.axis_size(axi...  46.1 us
    ppermute x30, starting transfers between devices, flip(): lax.ppermute(array, axis, [(i, i ^ bits) for i in range(lax.axis_size(axi...  24.9 us
    pallas_call x20, Pallas kernels, local_kernel(): pl.pallas_call(with_order, out_shape=[jax.ShapeDtypeStruct(shape, dtype)...  23 us
  transfers between devices with their start and end apart: 30, of which 17 were waited for; matrix products, arithmetic and copies ran while one was open for 0% of the time, Pallas kernels for 19%

profile of v5, /device:TPU:0, one launch (start us, length us, event | category | flops | bytes accessed | tf_op | source)
XLA Modules:
  0.0 99.3 jit_solution(820713792179594373)
XLA Ops:
  0.7 1.2 %broadcast_select_fusion.1 = (bf16[256,256]{1,0:T(8,128)(2,1)S(1)}, bf16[256,256]{1,0:T(8,128)(2,1)S(1)}) fusion(pred[]{:T(512)S(6)} %eq.8, bf16[256,2560]{1,0:T(8,128)(2,1)} %refs_1_.15, pred[]{:T(512)S(6)} %eq.9), kind=kLoop, calls=%fused_computation.4 | loop fusion | flops 262144 | bytes 786434 | tf_op jit(solution)/shard_map/jit(_where)/select_n | solution.py:200
  1.9 1.0 %pad_maximum_fusion.refs_0_ = bf16[256,1024]{1,0:T(8,128)(2,1)S(1)} fusion(bf16[256,512]{1,0:T(8,128)(2,1)} %refs_2_.4, bf16[256,256]{1,0:T(8,128)(2,1)S(1)} %get-tuple-element.71, bf16[256,256]{1,0:T(8,128)(2,1)S(1)} %get-tuple-element.70), kind=kLoop, calls=%fused_computation | loop fusion | flops 1572864 | bytes 1048576 | tf_op jit(solution)/shard_map/concatenate | solution.py:202
  2.9 3.1 %collective-permute-start = (bf16[256,1024]{1,0:T(8,128)(2,1)S(1)}, bf16[256,1024]{1,0:T(8,128)(2,1)S(1)}, u32[]{:S(2)}, u32[]{:S(2)}) collective-permute-start(bf16[256,1024]{1,0:T(8,128)(2,1)S(1)} %pad_maximum_fusion.refs_0_), channel_id=1, source_target_pairs={{0,1},{1,0},{2,3},{3,2},{4,5},{5,4},{6,7},{7,6},{8,9},{9,8},{10,11... | collective-permute-start | bytes 1572872 | tf_op jit(solution)/shard_map/ppermute | solution.py:93
  6.1 0.6 shard_map.136.refs_0_
  6.7 0.9 shard_map.137
  7.6 0.9 shard_map.138
  9.1 1.3 %copy-done.8 = f32[1,640,512]{2,1,0:T(8,128)S(1)} copy-done((f32[1,640,512]{2,1,0:T(8,128)S(1)}, f32[1,640,512]{2,1,0:T(8,128)}, u32[]{:S(2)}) %copy-start.8) | copy-done | bytes 1310744
  10.4 1.2 %shard_map.139 = (f32[640,512]{1,0:T(8,128)S(1)}, f32[640,512]{1,0:T(8,128)S(1)}, f32[640,512]{1,0:T(8,128)S(1)}) custom-call(s32[3]{0:T(128)S(1)} %pad_add_fusion.place_ref, f32[384,512]{1,0:T(8,128)S(1)} %get-tuple-element.39.refs_0_.refs_5_, f32[640,512]{1,0:T(8,128)S(1)} %bitcast.19, f32[640,512]{1,0:T(8,128)S(1)} %bitcast.20, f32[640,512]{1,0:T(8,128)S(1)} %bitcast.17, ...), custom_call_target="tpu_custom_call" | custom-call | flops 1 | bytes 1 | tf_op jit(solution)/shard_map/pallas_call | solution.py:110
  12.0 6.8 %collective-permute-done.refs_2_.refs_3_.refs_4_.refs_6_ = bf16[256,1024]{1,0:T(8,128)(2,1)S(1)} collective-permute-done((bf16[256,1024]{1,0:T(8,128)(2,1)S(1)}, bf16[256,1024]{1,0:T(8,128)(2,1)S(1)}, u32[]{:S(2)}, u32[]{:S(2)}) %collective-permute-start) | collective-permute-done | bytes 524320 | tf_op jit(solution)/shard_map/ppermute | solution.py:93
  18.7 0.8 shard_map.140.refs_0_
  19.6 3.1 %collective-permute-start.2 = (bf16[256,512]{1,0:T(8,128)(2,1)S(1)}, bf16[256,512]{1,0:T(8,128)(2,1)S(1)}, u32[]{:S(2)}, u32[]{:S(2)}) collective-permute-start(bf16[256,512]{1,0:T(8,128)(2,1)S(1)} %shard_map.140.refs_0_), channel_id=1, source_target_pairs={{0,2},{1,3},{2,0},{3,1},{4,6},{5,7},{6,4},{7,5},{8,10},{9,11},{10,... | collective-permute-start | bytes 786440 | tf_op jit(solution)/shard_map/ppermute | solution.py:93
  22.7 9.3 %collective-permute-done.1.refs_2_.refs_6_ = bf16[256,768]{1,0:T(8,128)(2,1)S(1)} collective-permute-done((bf16[256,768]{1,0:T(8,128)(2,1)S(1)}, bf16[256,768]{1,0:T(8,128)(2,1)S(1)}, u32[]{:S(2)}, u32[]{:S(2)}) %collective-permute-start.1) | collective-permute-done | bytes 393248 | tf_op jit(solution)/shard_map/ppermute | solution.py:93
  32.0 0.8 shard_map.141.refs_0_
  32.8 1.1 %shard_map.142 = (bf16[256,512]{1,0:T(8,128)(2,1)S(1)}, f32[256,512]{1,0:T(8,128)S(1)}) custom-call(s32[3]{0:T(128)S(1)} %pad_add_fusion.place_ref, bf16[384,512]{1,0:T(8,128)(2,1)S(1)} %shard_map.141.refs_0_, f32[640,512]{1,0:T(8,128)S(1)} %bitcast.11, f32[640,512]{1,0:T(8,128)S(1)} %bitcast.14, f32[640,512]{1,0:T(8,128)S(1)} %get-tuple-element.40.refs_0_.refs_3_, ...), custom_call_target="tpu_custom_call" | custom-call | flops 1 | bytes 1 | tf_op jit(solution)/shard_map/pallas_call | solution.py:110
  34.0 1.7 %collective-permute-start.4 = (bf16[128,512]{1,0:T(8,128)(2,1)S(1)}, bf16[128,512]{1,0:T(8,128)(2,1)S(1)}, u32[]{:S(2)}, u32[]{:S(2)}) collective-permute-start(bf16[128,512]{1,0:T(8,128)(2,1)S(1)} %get-tuple-element.78), channel_id=1, source_target_pairs={{0,8},{4,12},{8,0},{12,4},{1,9},{5,13},{9,1},{13,5},{2,10},{6,14},... | collective-permute-start | bytes 393224 | tf_op jit(solution)/shard_map/ppermute | solution.py:93
  35.7 1.5 %collective-permute-start.3 = (bf16[128,512]{1,0:T(8,128)(2,1)S(1)}, bf16[128,512]{1,0:T(8,128)(2,1)S(1)}, u32[]{:S(2)}, u32[]{:S(2)}) collective-permute-start(bf16[128,512]{1,0:T(8,128)(2,1)S(1)} %get-tuple-element.79), channel_id=1, source_target_pairs={{0,4},{4,0},{8,12},{12,8},{1,5},{5,1},{9,13},{13,9},{2,6},{6,2},{1... | collective-permute-start | bytes 393224 | tf_op jit(solution)/shard_map/ppermute | solution.py:93
  37.2 1.7 %collective-permute-start.11 = (bf16[384,512]{1,0:T(8,128)(2,1)S(1)}, bf16[384,512]{1,0:T(8,128)(2,1)S(1)}, u32[]{:S(2)}, u32[]{:S(2)}) collective-permute-start(bf16[384,512]{1,0:T(8,128)(2,1)S(1)} %shard_map.141.refs_0_), channel_id=1, source_target_pairs={{0,2},{1,3},{2,0},{3,1},{4,6},{5,7},{6,4},{7,5},{8,10},{9,11},{10,... | collective-permute-start | bytes 1179656 | tf_op jit(solution)/shard_map/ppermute | solution.py:93
  39.0 1.7 %collective-permute-done.3.refs_2_ = bf16[128,512]{1,0:T(8,128)(2,1)S(1)} collective-permute-done((bf16[128,512]{1,0:T(8,128)(2,1)S(1)}, bf16[128,512]{1,0:T(8,128)(2,1)S(1)}, u32[]{:S(2)}, u32[]{:S(2)}) %collective-permute-start.3) | collective-permute-done | bytes 131104 | tf_op jit(solution)/shard_map/ppermute | solution.py:93
  40.7 0.6 shard_map.143.refs_0_.refs_1_
  41.3 1.6 %collective-permute-start.6 = (bf16[128,512]{1,0:T(8,128)(2,1)S(1)}, bf16[128,512]{1,0:T(8,128)(2,1)S(1)}, u32[]{:S(2)}, u32[]{:S(2)}) collective-permute-start(bf16[128,512]{1,0:T(8,128)(2,1)S(1)} %get-tuple-element.76), channel_id=1, source_target_pairs={{0,4},{4,0},{8,12},{12,8},{1,5},{5,1},{9,13},{13,9},{2,6},{6,2},{1... | collective-permute-start | bytes 393224 | tf_op jit(solution)/shard_map/ppermute | solution.py:93
  43.4 3.0 %collective-permute-done.6.refs_3_ = bf16[128,512]{1,0:T(8,128)(2,1)S(1)} collective-permute-done((bf16[128,512]{1,0:T(8,128)(2,1)S(1)}, bf16[128,512]{1,0:T(8,128)(2,1)S(1)}, u32[]{:S(2)}, u32[]{:S(2)}) %collective-permute-start.6) | collective-permute-done | bytes 131104 | tf_op jit(solution)/shard_map/ppermute | solution.py:93
  46.4 1.5 %collective-permute-done.5.refs_2_ = bf16[128,512]{1,0:T(8,128)(2,1)S(1)} collective-permute-done((bf16[128,512]{1,0:T(8,128)(2,1)S(1)}, bf16[128,512]{1,0:T(8,128)(2,1)S(1)}, u32[]{:S(2)}, u32[]{:S(2)}) %collective-permute-start.5) | collective-permute-done | bytes 131104 | tf_op jit(solution)/shard_map/ppermute | solution.py:93
  47.9 1.3 %collective-permute-done.8.refs_5_ = bf16[128,512]{1,0:T(8,128)(2,1)S(1)} collective-permute-done((bf16[128,512]{1,0:T(8,128)(2,1)S(1)}, bf16[128,512]{1,0:T(8,128)(2,1)S(1)}, u32[]{:S(2)}, u32[]{:S(2)}) %collective-permute-start.8) | collective-permute-done | bytes 131104 | tf_op jit(solution)/shard_map/ppermute | solution.py:93
  49.2 1.1 %shard_map.144 = (bf16[256,512]{1,0:T(8,128)(2,1)S(1)}, bf16[256,256]{1,0:T(8,128)(2,1)S(1)}, f32[256,512]{1,0:T(8,128)S(1)}, f32[256,512]{1,0:T(8,128)S(1)}) custom-call(s32[3]{0:T(128)S(1)} %pad_add_fusion.place_ref, bf16[256,512]{1,0:T(8,128)(2,1)S(1)} %shard_map.143.refs_0_.refs_1_, bf16[256,512]{1,0:T(8,128)(2,1)S(1)} %shard_map.143.refs_0_.refs_1_, ...), custom_call_target="tpu_custom_call" | custom-call | flops 1 | bytes 1 | tf_op jit(solution)/shard_map/pallas_call | solution.py:110
  50.4 5.6 %collective-permute-done.11.refs_7_ = bf16[384,512]{1,0:T(8,128)(2,1)S(1)} collective-permute-done((bf16[384,512]{1,0:T(8,128)(2,1)S(1)}, bf16[384,512]{1,0:T(8,128)(2,1)S(1)}, u32[]{:S(2)}, u32[]{:S(2)}) %collective-permute-start.11) | collective-permute-done | bytes 393248 | tf_op jit(solution)/shard_map/ppermute | solution.py:93
  56.0 1.3 %shard_map.145 = (bf16[384,512]{1,0:T(8,128)(2,1)S(1)}, f32[384,512]{1,0:T(8,128)S(1)}) custom-call(s32[3]{0:T(128)S(1)} %pad_add_fusion.place_ref, bf16[256,512]{1,0:T(8,128)(2,1)S(1)} %get-tuple-element.46.refs_0_.refs_2_, f32[640,512]{1,0:T(8,128)S(1)} %bitcast.12, f32[640,512]{1,0:T(8,128)S(1)} %bitcast.15, ...), custom_call_target="tpu_custom_call" | custom-call | flops 1 | bytes 1 | tf_op jit(solution)/shard_map/pallas_call | solution.py:110
  57.3 0.6 collective-permute-start.13
  57.9 0.7 collective-permute-start.12
  58.6 2.4 %collective-permute-start.16 = (bf16[256,256]{1,0:T(8,128)(2,1)S(1)}, bf16[256,256]{1,0:T(8,128)(2,1)S(1)}, u32[]{:S(2)}, u32[]{:S(2)}) collective-permute-start(bf16[256,256]{1,0:T(8,128)(2,1)S(1)} %get-tuple-element.48.refs_2_), channel_id=1, source_target_pairs={{0,3},{1,2},{2,1},{3,0},{4,7},{5,6},{6,5},{7,4},{8,11},{9,10},{10,... | collective-permute-start | bytes 393224 | tf_op jit(solution)/shard_map/ppermute | solution.py:93
  61.0 2.0 %collective-permute-start.14 = (bf16[256,256]{1,0:T(8,128)(2,1)S(1)}, bf16[256,256]{1,0:T(8,128)(2,1)S(1)}, u32[]{:S(2)}, u32[]{:S(2)}) collective-permute-start(bf16[256,256]{1,0:T(8,128)(2,1)S(1)} %get-tuple-element.48.refs_2_), channel_id=1, source_target_pairs={{0,1},{1,0},{2,3},{3,2},{4,5},{5,4},{6,7},{7,6},{8,9},{9,8},{10,11... | collective-permute-start | bytes 393224 | tf_op jit(solution)/shard_map/ppermute | solution.py:93
  63.6 0.6 shard_map.146.refs_0_.refs_2_
  64.3 0.8 collective-permute-start.19
  65.1 1.5 %collective-permute-start.18 = (bf16[192,512]{1,0:T(8,128)(2,1)S(1)}, bf16[192,512]{1,0:T(8,128)(2,1)S(1)}, u32[]{:S(2)}, u32[]{:S(2)}) collective-permute-start(bf16[192,512]{1,0:T(8,128)(2,1)S(1)} %get-tuple-element.73), channel_id=1, source_target_pairs={{0,8},{4,12},{8,0},{12,4},{1,9},{5,13},{9,1},{13,5},{2,10},{6,14},... | collective-permute-start | bytes 589832 | tf_op jit(solution)/shard_map/ppermute | solution.py:93
  66.6 4.4 %collective-permute-done.15.refs_4_ = bf16[256,256]{1,0:T(8,128)(2,1)S(1)} collective-permute-done((bf16[256,256]{1,0:T(8,128)(2,1)S(1)}, bf16[256,256]{1,0:T(8,128)(2,1)S(1)}, u32[]{:S(2)}, u32[]{:S(2)}) %collective-permute-start.15) | collective-permute-done | bytes 131104 | tf_op jit(solution)/shard_map/ppermute | solution.py:93
  71.0 0.9 shard_map.147
  72.6 1.0 collective-permute-done.17.refs_1_.refs_4_
  74.1 1.5 %shard_map.148 = (bf16[384,512]{1,0:T(8,128)(2,1)S(1)}, bf16[384,256]{1,0:T(8,128)(2,1)S(1)}, f32[384,512]{1,0:T(8,128)S(1)}, f32[384,512]{1,0:T(8,128)S(1)}) custom-call(s32[3]{0:T(128)S(1)} %pad_add_fusion.place_ref, f32[256,256]{1,0:T(8,128)S(1)} %get-tuple-element.49.refs_0_.refs_3_, bf16[3,192,256]{2,1,0:T(8,128)(2,1)S(1)} %collective-permute-done.17.refs_1_.refs_4_, ...), custom_call_target="tpu_custom_call" | custom-call | flops 1 | bytes 1 | tf_op jit(solution)/shard_map/pallas_call | solution.py:110
  75.9 1.8 %collective-permute-start.25 = (bf16[384,256]{1,0:T(8,128)(2,1)S(1)}, bf16[384,256]{1,0:T(8,128)(2,1)S(1)}, u32[]{:S(2)}, u32[]{:S(2)}) collective-permute-start(bf16[384,256]{1,0:T(8,128)(2,1)S(1)} %get-tuple-element.59.refs_2_), channel_id=1, source_target_pairs={{0,1},{1,0},{2,3},{3,2},{4,5},{5,4},{6,7},{7,6},{8,9},{9,8},{10,11... | collective-permute-start | bytes 589832 | tf_op jit(solution)/shard_map/ppermute | solution.py:93
  77.6 0.9 shard_map.149.refs_0_.refs_7_
  78.5 1.7 %shard_map.150 = (f32[640,512]{1,0:T(8,128)}, f32[8,128]{1,0:T(8,128)S(1)}) custom-call(s32[3]{0:T(128)S(1)} %pad_add_fusion.place_ref, f32[256,512]{1,0:T(8,128)S(1)} %shard_map.149.refs_0_.refs_7_, f32[640,512]{1,0:T(8,128)S(1)} %bitcast.18, f32[256,512]{1,0:T(8,128)S(1)} %get-tuple-element.53.refs_2_, f32[384,512]{1,0:T(8,128)S(1)} %get-tuple-element.54.refs_3_), custom_call_target="tpu_custom_call" | custom-call | flops 1 | bytes 1 | tf_op jit(solution)/shard_map/pallas_call | solution.py:110
  80.3 2.4 %shard_map.151 = (f32[640,512]{1,0:T(8,128)}, f32[640,512]{1,0:T(8,128)}, f32[8,128]{1,0:T(8,128)S(1)}) custom-call(s32[3]{0:T(128)S(1)} %pad_add_fusion.place_ref, f32[8,128]{1,0:T(8,128)S(1)} %get-tuple-element.55.refs_0_, f32[640,512]{1,0:T(8,128)S(1)} %copy-done.3, f32[640,512]{1,0:T(8,128)S(1)} %copy-done.4, f32[256,512]{1,0:T(8,128)S(1)} %get-tuple-element.56.refs_3_, ...), custom_call_target="tpu_custom_call" | custom-call | flops 1 | bytes 1 | tf_op jit(solution)/shard_map/pallas_call | solution.py:110
  82.7 5.0 %collective-permute-done.24.refs_1_.refs_4_ = bf16[384,256]{1,0:T(8,128)(2,1)S(1)} collective-permute-done((bf16[384,256]{1,0:T(8,128)(2,1)S(1)}, bf16[384,256]{1,0:T(8,128)(2,1)S(1)}, u32[]{:S(2)}, u32[]{:S(2)}) %collective-permute-start.24) | collective-permute-done | bytes 196640 | tf_op jit(solution)/shard_map/ppermute | solution.py:93
  87.6 0.6 shard_map.152.refs_0_
  88.3 2.4 %shard_map.153 = (f32[640,512]{1,0:T(8,128)}, f32[640,512]{1,0:T(8,128)}, f32[8,128]{1,0:T(8,128)S(1)}) custom-call(s32[3]{0:T(128)S(1)} %pad_add_fusion.place_ref, bf16[384,256]{1,0:T(8,128)(2,1)S(1)} %shard_map.152.refs_0_, f32[640,512]{1,0:T(8,128)S(1)} %bitcast.13, f32[640,512]{1,0:T(8,128)S(1)} %bitcast.16, f32[256,512]{1,0:T(8,128)S(1)} %get-tuple-element.60.refs_3_, ...), custom_call_target="tpu_custom_call" | custom-call | flops 1 | bytes 1 | tf_op jit(solution)/shard_map/pallas_call | solution.py:110
  91.2 3.9 %collective-permute-done.26.refs_5_ = bf16[384,256]{1,0:T(8,128)(2,1)S(1)} collective-permute-done((bf16[384,256]{1,0:T(8,128)(2,1)S(1)}, bf16[384,256]{1,0:T(8,128)(2,1)S(1)}, u32[]{:S(2)}, u32[]{:S(2)}) %collective-permute-start.26) | collective-permute-done | bytes 196640 | tf_op jit(solution)/shard_map/ppermute | solution.py:93
  95.1 1.0 shard_map.154
  96.2 1.4 %collective-permute-done.29.refs_6_ = bf16[384,256]{1,0:T(8,128)(2,1)S(1)} collective-permute-done((bf16[384,256]{1,0:T(8,128)(2,1)S(1)}, bf16[384,256]{1,0:T(8,128)(2,1)S(1)}, u32[]{:S(2)}, u32[]{:S(2)}) %collective-permute-start.29) | collective-permute-done | bytes 196640 | tf_op jit(solution)/shard_map/ppermute | solution.py:93
  97.6 1.7 %shard_map.155 = bf16[256,512]{1,0:T(8,128)(2,1)} custom-call(s32[3]{0:T(128)S(1)} %pad_add_fusion.place_ref, f32[256,256]{1,0:T(8,128)S(1)} %get-tuple-element.68.refs_0_.refs_3_, bf16[256,2560]{1,0:T(8,128)(2,1)S(1)} %copy-done, bf16[384,512]{1,0:T(8,128)(2,1)S(1)} %get-tuple-element.51.refs_0_.refs_2_, f32[256,256]{1,0:T(8,128)S(1)} %get-tuple-element.68.refs_0_.refs_3_, ...), custom_call_target="tpu_custom_call" | custom-call | flops 1 | bytes 1 | tf_op jit(solution)/shard_map/pallas_call | solution.py:110
  (57 shorter events, 4.4 us)
Async XLA Ops:
  0.6 5.4 %copy-start = (bf16[256,2560]{1,0:T(8,128)(2,1)S(1)}, bf16[256,2560]{1,0:T(8,128)(2,1)}, u32[]{:S(2)}) copy-start(bf16[256,2560]{1,0:T(8,128)(2,1)} %refs_1_.15) | copy-start | bytes 3932164
  2.9 3.8 %copy-start.6 = (bf16[256,512]{1,0:T(8,128)(2,1)S(1)}, bf16[256,512]{1,0:T(8,128)(2,1)}, u32[]{:S(2)}) copy-start(bf16[256,512]{1,0:T(8,128)(2,1)} %refs_2_.4) | copy-start | bytes 786436
  2.9 15.8 %collective-permute-start = (bf16[256,1024]{1,0:T(8,128)(2,1)S(1)}, bf16[256,1024]{1,0:T(8,128)(2,1)S(1)}, u32[]{:S(2)}, u32[]{:S(2)}) collective-permute-start(bf16[256,1024]{1,0:T(8,128)(2,1)S(1)} %pad_maximum_fusion.refs_0_), channel_id=1, source_target_pairs={{0,1},{1,0},{2,3},{3,2},{4,5},{5,4},{6,7},{7,6},{8,9},{9,8},{10,11... | collective-permute-start | bytes 1572872 | tf_op jit(solution)/shard_map/ppermute | solution.py:93
  6.1 2.5 %copy-start.7 = (f32[1,1,640,512]{3,2,1,0:T(8,128)S(1)}, f32[1,1,640,512]{3,2,1,0:T(8,128)}, u32[]{:S(2)}) copy-start(f32[1,1,640,512]{3,2,1,0:T(8,128)} %param.11) | copy-start | bytes 3932164
  6.7 1.9 %copy-start.4 = (f32[640,512]{1,0:T(8,128)S(1)}, f32[640,512]{1,0:T(8,128)}, u32[]{:S(2)}) copy-start(f32[640,512]{1,0:T(8,128)} %refs_2_.5) | copy-start | bytes 3932164
  6.7 1.9 %copy-start.5 = (f32[1,640,512]{2,1,0:T(8,128)S(1)}, f32[1,640,512]{2,1,0:T(8,128)}, u32[]{:S(2)}) copy-start(f32[1,640,512]{2,1,0:T(8,128)} %param.15) | copy-start | bytes 3932164
  7.6 1.5 %copy-start.3 = (f32[640,512]{1,0:T(8,128)S(1)}, f32[640,512]{1,0:T(8,128)}, u32[]{:S(2)}) copy-start(f32[640,512]{1,0:T(8,128)} %refs_1_.13) | copy-start | bytes 3932164
  9.1 1.3 %copy-start.8 = (f32[1,640,512]{2,1,0:T(8,128)S(1)}, f32[1,640,512]{2,1,0:T(8,128)}, u32[]{:S(2)}) copy-start(f32[1,640,512]{2,1,0:T(8,128)} %param.14) | copy-start | bytes 3932164
  11.6 37.6 %collective-permute-start.10 = (f32[640,512]{1,0:T(8,128)S(1)}, f32[640,512]{1,0:T(8,128)S(1)}, u32[]{:S(2)}, u32[]{:S(2)}) collective-permute-start(f32[640,512]{1,0:T(8,128)S(1)} %get-tuple-element.44.refs_7_.refs_8_), channel_id=1, source_target_pairs={{0,16},{16,0},{1,17},{17,1},{2,18},{18,2},{3,19},{19,3},{4,20},{20... | collective-permute-start | bytes 3932168 | tf_op jit(solution)/shard_map/ppermute | solution.py:93
  11.7 20.2 %collective-permute-start.1 = (bf16[256,768]{1,0:T(8,128)(2,1)S(1)}, bf16[256,768]{1,0:T(8,128)(2,1)S(1)}, u32[]{:S(2)}, u32[]{:S(2)}) collective-permute-start(bf16[256,768]{1,0:T(8,128)(2,1)S(1)} %shard_map.136.refs_0_), channel_id=1, source_target_pairs={{0,1},{1,0},{2,3},{3,2},{4,5},{5,4},{6,7},{7,6},{8,9},{9,8},{10,11... | collective-permute-start | bytes 1179656 | tf_op jit(solution)/shard_map/ppermute | solution.py:93
  18.7 14.1 %copy-start.2 = (f32[1,1,640,512]{3,2,1,0:T(8,128)S(1)}, f32[1,1,640,512]{3,2,1,0:T(8,128)}, u32[]{:S(2)}) copy-start(f32[1,1,640,512]{3,2,1,0:T(8,128)} %param.13) | copy-start | bytes 3932164
  19.5 13.3 %copy-start.1 = (f32[1,1,640,512]{3,2,1,0:T(8,128)S(1)}, f32[1,1,640,512]{3,2,1,0:T(8,128)}, u32[]{:S(2)}) copy-start(f32[1,1,640,512]{3,2,1,0:T(8,128)} %param.12) | copy-start | bytes 3932164
  19.6 13.2 %collective-permute-start.2 = (bf16[256,512]{1,0:T(8,128)(2,1)S(1)}, bf16[256,512]{1,0:T(8,128)(2,1)S(1)}, u32[]{:S(2)}, u32[]{:S(2)}) collective-permute-start(bf16[256,512]{1,0:T(8,128)(2,1)S(1)} %shard_map.140.refs_0_), channel_id=1, source_target_pairs={{0,2},{1,3},{2,0},{3,1},{4,6},{5,7},{6,4},{7,5},{8,10},{9,11},{10,... | collective-permute-start | bytes 786440 | tf_op jit(solution)/shard_map/ppermute | solution.py:93
  34.0 5.0 %collective-permute-start.4 = (bf16[128,512]{1,0:T(8,128)(2,1)S(1)}, bf16[128,512]{1,0:T(8,128)(2,1)S(1)}, u32[]{:S(2)}, u32[]{:S(2)}) collective-permute-start(bf16[128,512]{1,0:T(8,128)(2,1)S(1)} %get-tuple-element.78), channel_id=1, source_target_pairs={{0,8},{4,12},{8,0},{12,4},{1,9},{5,13},{9,1},{13,5},{2,10},{6,14},... | collective-permute-start | bytes 393224 | tf_op jit(solution)/shard_map/ppermute | solution.py:93
  35.7 5.0 %collective-permute-start.3 = (bf16[128,512]{1,0:T(8,128)(2,1)S(1)}, bf16[128,512]{1,0:T(8,128)(2,1)S(1)}, u32[]{:S(2)}, u32[]{:S(2)}) collective-permute-start(bf16[128,512]{1,0:T(8,128)(2,1)S(1)} %get-tuple-element.79), channel_id=1, source_target_pairs={{0,4},{4,0},{8,12},{12,8},{1,5},{5,1},{9,13},{13,9},{2,6},{6,2},{1... | collective-permute-start | bytes 393224 | tf_op jit(solution)/shard_map/ppermute | solution.py:93
  37.2 18.7 %collective-permute-start.11 = (bf16[384,512]{1,0:T(8,128)(2,1)S(1)}, bf16[384,512]{1,0:T(8,128)(2,1)S(1)}, u32[]{:S(2)}, u32[]{:S(2)}) collective-permute-start(bf16[384,512]{1,0:T(8,128)(2,1)S(1)} %shard_map.141.refs_0_), channel_id=1, source_target_pairs={{0,2},{1,3},{2,0},{3,1},{4,6},{5,7},{6,4},{7,5},{8,10},{9,11},{10,... | collective-permute-start | bytes 1179656 | tf_op jit(solution)/shard_map/ppermute | solution.py:93
  41.3 5.0 %collective-permute-start.6 = (bf16[128,512]{1,0:T(8,128)(2,1)S(1)}, bf16[128,512]{1,0:T(8,128)(2,1)S(1)}, u32[]{:S(2)}, u32[]{:S(2)}) collective-permute-start(bf16[128,512]{1,0:T(8,128)(2,1)S(1)} %get-tuple-element.76), channel_id=1, source_target_pairs={{0,4},{4,0},{8,12},{12,8},{1,5},{5,1},{9,13},{13,9},{2,6},{6,2},{1... | collective-permute-start | bytes 393224 | tf_op jit(solution)/shard_map/ppermute | solution.py:93
  42.9 5.0 %collective-permute-start.5 = (bf16[128,512]{1,0:T(8,128)(2,1)S(1)}, bf16[128,512]{1,0:T(8,128)(2,1)S(1)}, u32[]{:S(2)}, u32[]{:S(2)}) collective-permute-start(bf16[128,512]{1,0:T(8,128)(2,1)S(1)} %get-tuple-element.77), channel_id=1, source_target_pairs={{0,8},{4,12},{8,0},{12,4},{1,9},{5,13},{9,1},{13,5},{2,10},{6,14},... | collective-permute-start | bytes 393224 | tf_op jit(solution)/shard_map/ppermute | solution.py:93
  43.4 5.8 %collective-permute-start.7 = (bf16[256,512]{1,0:T(8,128)(2,1)S(1)}, bf16[256,512]{1,0:T(8,128)(2,1)S(1)}, u32[]{:S(2)}, u32[]{:S(2)}) collective-permute-start(bf16[256,512]{1,0:T(8,128)(2,1)S(1)} %shard_map.143.refs_0_.refs_1_), channel_id=1, source_target_pairs={{0,16},{16,0},{1,17},{17,1},{2,18},{18,2},{3,19},{19,3},{4,20},{20... | collective-permute-start | bytes 786440 | tf_op jit(solution)/shard_map/ppermute | solution.py:93
  46.4 1.5 %collective-permute-start.9 = (bf16[128,512]{1,0:T(8,128)(2,1)S(1)}, bf16[128,512]{1,0:T(8,128)(2,1)S(1)}, u32[]{:S(2)}, u32[]{:S(2)}) collective-permute-start(bf16[128,512]{1,0:T(8,128)(2,1)S(1)} %collective-permute-done.6.refs_3_), channel_id=1, source_target_pairs={{0,16},{16,0},{1,17},{17,1},{2,18},{18,2},{3,19},{19,3},{4,20},{20... | collective-permute-start | bytes 393224 | tf_op jit(solution)/shard_map/ppermute | solution.py:93
  47.9 1.3 %collective-permute-start.8 = (bf16[128,512]{1,0:T(8,128)(2,1)S(1)}, bf16[128,512]{1,0:T(8,128)(2,1)S(1)}, u32[]{:S(2)}, u32[]{:S(2)}) collective-permute-start(bf16[128,512]{1,0:T(8,128)(2,1)S(1)} %collective-permute-done.5.refs_2_), channel_id=1, source_target_pairs={{0,16},{16,0},{1,17},{17,1},{2,18},{18,2},{3,19},{19,3},{4,20},{20... | collective-permute-start | bytes 393224 | tf_op jit(solution)/shard_map/ppermute | solution.py:93
  57.3 5.7 %collective-permute-start.13 = (bf16[192,512]{1,0:T(8,128)(2,1)S(1)}, bf16[192,512]{1,0:T(8,128)(2,1)S(1)}, u32[]{:S(2)}, u32[]{:S(2)}) collective-permute-start(bf16[192,512]{1,0:T(8,128)(2,1)S(1)} %get-tuple-element.74), channel_id=1, source_target_pairs={{0,8},{4,12},{8,0},{12,4},{1,9},{5,13},{9,1},{13,5},{2,10},{6,14},... | collective-permute-start | bytes 589832 | tf_op jit(solution)/shard_map/ppermute | solution.py:93
  57.9 5.7 %collective-permute-start.12 = (bf16[192,512]{1,0:T(8,128)(2,1)S(1)}, bf16[192,512]{1,0:T(8,128)(2,1)S(1)}, u32[]{:S(2)}, u32[]{:S(2)}) collective-permute-start(bf16[192,512]{1,0:T(8,128)(2,1)S(1)} %get-tuple-element.75), channel_id=1, source_target_pairs={{0,4},{4,0},{8,12},{12,8},{1,5},{5,1},{9,13},{13,9},{2,6},{6,2},{1... | collective-permute-start | bytes 589832 | tf_op jit(solution)/shard_map/ppermute | solution.py:93
  58.6 8.0 %collective-permute-start.16 = (bf16[256,256]{1,0:T(8,128)(2,1)S(1)}, bf16[256,256]{1,0:T(8,128)(2,1)S(1)}, u32[]{:S(2)}, u32[]{:S(2)}) collective-permute-start(bf16[256,256]{1,0:T(8,128)(2,1)S(1)} %get-tuple-element.48.refs_2_), channel_id=1, source_target_pairs={{0,3},{1,2},{2,1},{3,0},{4,7},{5,6},{6,5},{7,4},{8,11},{9,10},{10,... | collective-permute-start | bytes 393224 | tf_op jit(solution)/shard_map/ppermute | solution.py:93
  61.0 10.0 %collective-permute-start.15 = (bf16[256,256]{1,0:T(8,128)(2,1)S(1)}, bf16[256,256]{1,0:T(8,128)(2,1)S(1)}, u32[]{:S(2)}, u32[]{:S(2)}) collective-permute-start(bf16[256,256]{1,0:T(8,128)(2,1)S(1)} %get-tuple-element.48.refs_2_), channel_id=1, source_target_pairs={{0,2},{1,3},{2,0},{3,1},{4,6},{5,7},{6,4},{7,5},{8,10},{9,11},{10,... | collective-permute-start | bytes 393224 | tf_op jit(solution)/shard_map/ppermute | solution.py:93
  61.0 10.0 %collective-permute-start.14 = (bf16[256,256]{1,0:T(8,128)(2,1)S(1)}, bf16[256,256]{1,0:T(8,128)(2,1)S(1)}, u32[]{:S(2)}, u32[]{:S(2)}) collective-permute-start(bf16[256,256]{1,0:T(8,128)(2,1)S(1)} %get-tuple-element.48.refs_2_), channel_id=1, source_target_pairs={{0,1},{1,0},{2,3},{3,2},{4,5},{5,4},{6,7},{7,6},{8,9},{9,8},{10,11... | collective-permute-start | bytes 393224 | tf_op jit(solution)/shard_map/ppermute | solution.py:93
  64.3 7.7 %collective-permute-start.19 = (bf16[192,512]{1,0:T(8,128)(2,1)S(1)}, bf16[192,512]{1,0:T(8,128)(2,1)S(1)}, u32[]{:S(2)}, u32[]{:S(2)}) collective-permute-start(bf16[192,512]{1,0:T(8,128)(2,1)S(1)} %get-tuple-element.72), channel_id=1, source_target_pairs={{0,4},{4,0},{8,12},{12,8},{1,5},{5,1},{9,13},{13,9},{2,6},{6,2},{1... | collective-permute-start | bytes 589832 | tf_op jit(solution)/shard_map/ppermute | solution.py:93
  65.1 7.4 %collective-permute-start.18 = (bf16[192,512]{1,0:T(8,128)(2,1)S(1)}, bf16[192,512]{1,0:T(8,128)(2,1)S(1)}, u32[]{:S(2)}, u32[]{:S(2)}) collective-permute-start(bf16[192,512]{1,0:T(8,128)(2,1)S(1)} %get-tuple-element.73), channel_id=1, source_target_pairs={{0,8},{4,12},{8,0},{12,4},{1,9},{5,13},{9,1},{13,5},{2,10},{6,14},... | collective-permute-start | bytes 589832 | tf_op jit(solution)/shard_map/ppermute | solution.py:93
  66.6 7.5 %collective-permute-start.20 = (bf16[384,512]{1,0:T(8,128)(2,1)S(1)}, bf16[384,512]{1,0:T(8,128)(2,1)S(1)}, u32[]{:S(2)}, u32[]{:S(2)}) collective-permute-start(bf16[384,512]{1,0:T(8,128)(2,1)S(1)} %shard_map.146.refs_0_.refs_2_), channel_id=1, source_target_pairs={{0,16},{16,0},{1,17},{17,1},{2,18},{18,2},{3,19},{19,3},{4,20},{20... | collective-permute-start | bytes 1179656 | tf_op jit(solution)/shard_map/ppermute | solution.py:93
  71.9 1.6 %collective-permute-start.17 = (bf16[3,192,256]{2,1,0:T(8,128)(2,1)S(1)}, bf16[3,192,256]{2,1,0:T(8,128)(2,1)S(1)}, u32[]{:S(2)}, u32[]{:S(2)}) collective-permute-start(bf16[3,192,256]{2,1,0:T(8,128)(2,1)S(1)} %get-tuple-element.50), channel_id=1, source_target_pairs={{0,16},{16,0},{1,17},{17,1},{2,18},{18,2},{3,19},{19,3},{4,20},{20... | collective-permute-start | bytes 884744 | tf_op jit(solution)/shard_map/ppermute | solution.py:93
  72.0 1.8 %collective-permute-start.22 = (bf16[192,512]{1,0:T(8,128)(2,1)S(1)}, bf16[192,512]{1,0:T(8,128)(2,1)S(1)}, u32[]{:S(2)}, u32[]{:S(2)}) collective-permute-start(bf16[192,512]{1,0:T(8,128)(2,1)S(1)} %collective-permute-done.19.refs_4_), channel_id=1, source_target_pairs={{0,16},{16,0},{1,17},{17,1},{2,18},{18,2},{3,19},{19,3},{4,20},{20... | collective-permute-start | bytes 589832 | tf_op jit(solution)/shard_map/ppermute | solution.py:93
  72.5 1.6 %collective-permute-start.21 = (bf16[192,512]{1,0:T(8,128)(2,1)S(1)}, bf16[192,512]{1,0:T(8,128)(2,1)S(1)}, u32[]{:S(2)}, u32[]{:S(2)}) collective-permute-start(bf16[192,512]{1,0:T(8,128)(2,1)S(1)} %collective-permute-done.18.refs_3_), channel_id=1, source_target_pairs={{0,16},{16,0},{1,17},{17,1},{2,18},{18,2},{3,19},{19,3},{4,20},{20... | collective-permute-start | bytes 589832 | tf_op jit(solution)/shard_map/ppermute | solution.py:93
  75.6 12.1 %collective-permute-start.24 = (bf16[384,256]{1,0:T(8,128)(2,1)S(1)}, bf16[384,256]{1,0:T(8,128)(2,1)S(1)}, u32[]{:S(2)}, u32[]{:S(2)}) collective-permute-start(bf16[384,256]{1,0:T(8,128)(2,1)S(1)} %get-tuple-element.59.refs_2_), channel_id=1, source_target_pairs={{0,2},{1,3},{2,0},{3,1},{4,6},{5,7},{6,4},{7,5},{8,10},{9,11},{10,... | collective-permute-start | bytes 589832 | tf_op jit(solution)/shard_map/ppermute | solution.py:93
  75.7 2.0 %collective-permute-start.23 = (bf16[3,64,256]{2,1,0:T(8,128)(2,1)S(1)}, bf16[3,64,256]{2,1,0:T(8,128)(2,1)S(1)}, u32[]{:S(2)}, u32[]{:S(2)}) collective-permute-start(bf16[3,64,256]{2,1,0:T(8,128)(2,1)S(1)} %get-tuple-element.52), channel_id=1, source_target_pairs={{0,16},{16,0},{1,17},{17,1},{2,18},{18,2},{3,19},{19,3},{4,20},{20... | collective-permute-start | bytes 294920 | tf_op jit(solution)/shard_map/ppermute | solution.py:93
  75.9 14.8 %collective-permute-start.25 = (bf16[384,256]{1,0:T(8,128)(2,1)S(1)}, bf16[384,256]{1,0:T(8,128)(2,1)S(1)}, u32[]{:S(2)}, u32[]{:S(2)}) collective-permute-start(bf16[384,256]{1,0:T(8,128)(2,1)S(1)} %get-tuple-element.59.refs_2_), channel_id=1, source_target_pairs={{0,1},{1,0},{2,3},{3,2},{4,5},{5,4},{6,7},{7,6},{8,9},{9,8},{10,11... | collective-permute-start | bytes 589832 | tf_op jit(solution)/shard_map/ppermute | solution.py:93
  88.2 6.9 %collective-permute-start.26 = (bf16[384,256]{1,0:T(8,128)(2,1)S(1)}, bf16[384,256]{1,0:T(8,128)(2,1)S(1)}, u32[]{:S(2)}, u32[]{:S(2)}) collective-permute-start(bf16[384,256]{1,0:T(8,128)(2,1)S(1)} %shard_map.152.refs_0_), channel_id=1, source_target_pairs={{0,1},{1,0},{2,3},{3,2},{4,5},{5,4},{6,7},{7,6},{8,9},{9,8},{10,11... | collective-permute-start | bytes 589832 | tf_op jit(solution)/shard_map/ppermute | solution.py:93
  90.7 5.5 %collective-permute-start.28 = (bf16[384,256]{1,0:T(8,128)(2,1)S(1)}, bf16[384,256]{1,0:T(8,128)(2,1)S(1)}, u32[]{:S(2)}, u32[]{:S(2)}) collective-permute-start(bf16[384,256]{1,0:T(8,128)(2,1)S(1)} %collective-permute-done.24.refs_1_.refs_4_), channel_id=1, source_target_pairs={{0,16},{16,0},{1,17},{17,1},{2,18},{18,2},{3,19},{19,3},{4,20},{20... | collective-permute-start | bytes 589832 | tf_op jit(solution)/shard_map/ppermute | solution.py:93
  90.7 5.5 %collective-permute-start.27 = (bf16[384,256]{1,0:T(8,128)(2,1)S(1)}, bf16[384,256]{1,0:T(8,128)(2,1)S(1)}, u32[]{:S(2)}, u32[]{:S(2)}) collective-permute-start(bf16[384,256]{1,0:T(8,128)(2,1)S(1)} %collective-permute-done.25.refs_3_), channel_id=1, source_target_pairs={{0,16},{16,0},{1,17},{17,1},{2,18},{18,2},{3,19},{19,3},{4,20},{20... | collective-permute-start | bytes 589832 | tf_op jit(solution)/shard_map/ppermute | solution.py:93
  96.1 1.5 %collective-permute-start.29 = (bf16[384,256]{1,0:T(8,128)(2,1)S(1)}, bf16[384,256]{1,0:T(8,128)(2,1)S(1)}, u32[]{:S(2)}, u32[]{:S(2)}) collective-permute-start(bf16[384,256]{1,0:T(8,128)(2,1)S(1)} %get-tuple-element.69), channel_id=1, source_target_pairs={{0,16},{16,0},{1,17},{17,1},{2,18},{18,2},{3,19},{19,3},{4,20},{20... | collective-permute-start | bytes 589832 | tf_op jit(solution)/shard_map/ppermute | solution.py:93
